TPU v7x, 32 devices: a whole 2x2x4 slice. The times are simulated.
32 devices in a mesh: dp: 16 (over z, y, core), mp: 2 (over x).
Axes of the slice: x: 2, y: 2, z: 4, core: 2. Of those that a mesh axis runs over, the one named last changes fastest.
Arguments:
- tokens: bfloat16 [16384, 1024], P(('dp', 'mp')), may hold values from -6 to 6
- doc_lengths: int32 [16, 6], P('dp'), may hold values from 1 to 512, 1024 in all within a row
- cotangent: bfloat16 [16384, 1024], P(('dp', 'mp')), may hold values from -6 to 6
- query_weight: bfloat16 [1024, 1024], P(None, 'mp'), may hold values from -0.1875 to 0.1875
- query_bias: bfloat16 [1024], P('mp'), may hold values from -3 to 3
- key_weight: bfloat16 [1024, 1024], P(None, 'mp'), may hold values from -0.1875 to 0.1875
- value_weight: bfloat16 [1024, 1024], P(None, 'mp'), may hold values from -0.1875 to 0.1875
- value_bias: bfloat16 [1024], P('mp'), may hold values from -3 to 3
- out_weight: bfloat16 [1024, 1024], P('mp'), may hold values from -1 to 1
- out_bias: bfloat16 [1024], replicated, may hold values from -3 to 3
- first_gain: bfloat16 [1024], replicated, may hold values from 0.5 to 1.5
- first_shift: bfloat16 [1024], replicated, may hold values from -2 to 2
- up_weight: bfloat16 [1024, 4096], P(None, 'mp'), may hold values from -0.1875 to 0.1875
- up_bias: bfloat16 [4096], P('mp'), may hold values from -3 to 3
- down_weight: bfloat16 [4096, 1024], P('mp'), may hold values from -0.09375 to 0.09375
- down_bias: bfloat16 [1024], replicated, may hold values from -3 to 3
- second_gain: bfloat16 [1024], replicated, may hold values from 0.5 to 1.5
- second_shift: bfloat16 [1024], replicated, may hold values from -2 to 2
Outputs:
- output: bfloat16 [16384, 1024], P(('dp', 'mp'))
- input_grad: float32 [16384, 1024], P(('dp', 'mp'))
- grad_query_weight: float32 [1024, 1024], P(None, 'mp')
- grad_query_bias: float32 [1024], P('mp')
- grad_key_weight: float32 [1024, 1024], P(None, 'mp')
- grad_value_weight: float32 [1024, 1024], P(None, 'mp')
- grad_value_bias: float32 [1024], P('mp')
- grad_out_weight: float32 [1024, 1024], P('mp')
- grad_out_bias: float32 [1024], replicated
- grad_first_gain: float32 [1024], replicated
- grad_first_shift: float32 [1024], replicated
- grad_up_weight: float32 [1024, 4096], P(None, 'mp')
- grad_up_bias: float32 [4096], P('mp')
- grad_down_weight: float32 [4096, 1024], P('mp')
- grad_down_bias: float32 [1024], replicated
- grad_second_gain: float32 [1024], replicated
- grad_second_shift: float32 [1024], replicated
Inputs may be any that keep to these rules, and one draw needn't show every extreme that they name: `doc_lengths`: each row lists 6 - 1 document lengths and then the padding's length; a row sums to 1024, and its largest entry is 512.
All inputs are finite; a program needn't handle non-finite values.
Results may differ from a plain program's by a relative error of at most 0.023.
Values may be sent and summed in bfloat16 or wider, within the bound.
No kernel may reach another device: no remote copies, remote signals or barrier semaphores. Data moves between devices by JAX's collectives and lax.ppermute only.
A program may use at most 192 MiB of HBM per device.

v0:
```python
import jax
import jax.numpy as jnp
from jax import lax
from jax.sharding import PartitionSpec as P

HEAD = 64


epsilon = 1e-05
masked_score = -1000000000.0


def matmul(left, right):
    return jnp.dot(left, right, preferred_element_type=jnp.float32)


def matmul_tn(left, right):
    return lax.dot_general(
        left, right, (((0,), (0,)), ((), ())), preferred_element_type=jnp.float32
    )


def matmul_nt(left, right):
    return lax.dot_general(
        left, right, (((1,), (1,)), ((), ())), preferred_element_type=jnp.float32
    )


def layer_norm(inputs, gain, shift):
    center = inputs - jnp.mean(inputs, axis=-1, keepdims=True)
    spread = jnp.mean(center * center, axis=-1, keepdims=True)
    return center * lax.rsqrt(spread + epsilon) * gain + shift


def segment_ids(lengths, length):
    ends = jnp.cumsum(lengths, axis=-1)
    places = jnp.arange(length, dtype=jnp.int32)
    return jnp.sum((places[None, None, :] >= ends[:, :, None]).astype(jnp.int32), axis=1)


def score_block(q_block, s_block, key_rows, segment):
    raw = jnp.einsum(
        "qhd,khd->hqk", q_block, key_rows, preferred_element_type=jnp.float32
    ) * HEAD ** (-0.5)
    same = s_block[:, None] == segment[None, :]
    return jnp.where(same[None], raw, masked_score)


def body(
    tokens,
    doc_lengths,
    cotangent,
    query_weight,
    query_bias,
    key_weight,
    value_weight,
    value_bias,
    out_weight,
    out_bias,
    first_gain,
    first_shift,
    up_weight,
    up_bias,
    down_weight,
    down_bias,
    second_gain,
    second_shift,
):
    own_rows = tokens.shape[0]
    seq_count, doc_count = doc_lengths.shape
    all_rows = own_rows * lax.axis_size("mp")
    length = all_rows // seq_count
    head_count = query_weight.shape[1] // HEAD
    block_rows = min(512, length)
    block_count = length // block_rows
    score_scale = HEAD ** (-0.5)
    first_row = lax.axis_index("mp") * own_rows
    segment = segment_ids(doc_lengths, length)
    valid_all = (segment < doc_count - 1).reshape(all_rows)
    valid_rows = lax.dynamic_slice_in_dim(valid_all, first_row, own_rows, 0)
    shape_blocks = (seq_count, block_count, block_rows, head_count, HEAD)
    shape_seqs = (seq_count, length, head_count, HEAD)
    gain_first = first_gain.astype(jnp.float32)
    shift_first = first_shift.astype(jnp.float32)
    gathered = lax.all_gather(tokens, "mp", axis=0, tiled=True)
    queries = (matmul(gathered, query_weight) + query_bias).astype(jnp.bfloat16)
    key_rows = matmul(gathered, key_weight).astype(jnp.bfloat16)
    values = (matmul(gathered, value_weight) + value_bias).astype(jnp.bfloat16)

    def attend_sequence(members):
        q_seq, k_seq, v_seq, s_seq = members

        def attend_block(pieces):
            q_block, s_block = pieces
            scores = score_block(q_block, s_block, k_seq, s_seq)
            row_max = jnp.max(scores, axis=-1, keepdims=True)
            exponent = jnp.exp(scores - row_max)
            row_sum = jnp.sum(exponent, axis=-1, keepdims=True)
            attn_probs = (exponent / row_sum).astype(jnp.bfloat16)
            blended = jnp.einsum(
                "hqk,khd->qhd", attn_probs, v_seq, preferred_element_type=jnp.float32
            )
            return (blended.astype(jnp.bfloat16), (row_max + jnp.log(row_sum))[..., 0])

        return lax.map(attend_block, (q_seq, s_seq.reshape(block_count, block_rows)))

    context, log_mass = lax.map(
        attend_sequence,
        (
            queries.reshape(shape_blocks),
            key_rows.reshape(shape_seqs),
            values.reshape(shape_seqs),
            segment,
        ),
    )
    context = context.reshape(all_rows, head_count * HEAD)
    attn_part = lax.psum_scatter(matmul(context, out_weight), "mp", scatter_dimension=0, tiled=True)
    middle = attn_part + out_bias + tokens.astype(jnp.float32)
    hidden, norm_first = jax.vjp(layer_norm, middle, gain_first, shift_first)
    hidden_rows = lax.all_gather(hidden.astype(jnp.bfloat16), "mp", axis=0, tiled=True)
    pre = matmul(hidden_rows, up_weight) + up_bias
    act_exact, gelu_back = jax.vjp(lambda inputs: jax.nn.gelu(inputs, approximate=False), pre)
    act = act_exact.astype(jnp.bfloat16)
    ffn_part = lax.psum_scatter(matmul(act, down_weight), "mp", scatter_dimension=0, tiled=True)
    final = ffn_part + down_bias + hidden
    result, norm_second = jax.vjp(
        layer_norm, final, second_gain.astype(jnp.float32), second_shift.astype(jnp.float32)
    )
    upstream = cotangent.astype(jnp.float32) * valid_rows[:, None].astype(jnp.float32)
    d_final, grad_second_gain, grad_second_shift = norm_second(upstream)
    grad_down_bias = jnp.sum(d_final, axis=0)
    final_rows = lax.all_gather(d_final.astype(jnp.bfloat16), "mp", axis=0, tiled=True)
    grad_down_weight = matmul_tn(act, final_rows)
    d_pre = gelu_back(matmul_nt(final_rows, down_weight))[0].astype(jnp.bfloat16)
    grad_up_weight = matmul_tn(hidden_rows, d_pre)
    grad_up_bias = jnp.sum(d_pre, axis=0, dtype=jnp.float32)
    d_hidden = (
        lax.psum_scatter(matmul_nt(d_pre, up_weight), "mp", scatter_dimension=0, tiled=True)
        + d_final
    )
    d_middle, grad_first_gain, grad_first_shift = norm_first(d_hidden)
    grad_out_bias = jnp.sum(d_middle, axis=0)
    middle_rows = lax.all_gather(d_middle.astype(jnp.bfloat16), "mp", axis=0, tiled=True)
    grad_out_weight = matmul_tn(context, middle_rows)
    d_context = matmul_nt(middle_rows, out_weight).astype(jnp.bfloat16)

    def back_sequence(members):
        q_seq, k_seq, v_seq, s_seq, l_seq, g_seq = members

        def back_block(carried, pieces):
            grad_keys, grad_values = carried
            q_block, s_block, l_block, g_block = pieces
            scores = score_block(q_block, s_block, k_seq, s_seq)
            attn_probs = jnp.exp(scores - l_block[..., None])
            d_probs = jnp.einsum("qhd,khd->hqk", g_block, v_seq, preferred_element_type=jnp.float32)
            row_inner = jnp.sum(attn_probs * d_probs, axis=-1, keepdims=True)
            d_scores = (attn_probs * (d_probs - row_inner)).astype(jnp.bfloat16)
            d_block = (
                jnp.einsum("hqk,khd->qhd", d_scores, k_seq, preferred_element_type=jnp.float32)
                * score_scale
            )
            grad_keys = (
                grad_keys
                + jnp.einsum("hqk,qhd->khd", d_scores, q_block, preferred_element_type=jnp.float32)
                * score_scale
            )
            grad_values = grad_values + jnp.einsum(
                "hqk,qhd->khd",
                attn_probs.astype(jnp.bfloat16),
                g_block,
                preferred_element_type=jnp.float32,
            )
            return ((grad_keys, grad_values), d_block.astype(jnp.bfloat16))

        zero_grads = jnp.zeros((length, head_count, HEAD), jnp.float32)
        (grad_keys, grad_values), d_blocks = lax.scan(
            back_block,
            (zero_grads, zero_grads),
            (q_seq, s_seq.reshape(block_count, block_rows), l_seq, g_seq),
        )
        return (d_blocks, grad_keys.astype(jnp.bfloat16), grad_values.astype(jnp.bfloat16))

    d_queries, d_keys, d_values = lax.map(
        back_sequence,
        (
            queries.reshape(shape_blocks),
            key_rows.reshape(shape_seqs),
            values.reshape(shape_seqs),
            segment,
            log_mass,
            d_context.reshape(shape_blocks),
        ),
    )
    d_queries = d_queries.reshape(all_rows, head_count * HEAD)
    d_keys = d_keys.reshape(all_rows, head_count * HEAD)
    d_values = d_values.reshape(all_rows, head_count * HEAD)
    grad_query_weight = matmul_tn(gathered, d_queries)
    grad_key_weight = matmul_tn(gathered, d_keys)
    grad_value_weight = matmul_tn(gathered, d_values)
    grad_query_bias = jnp.sum(d_queries, axis=0, dtype=jnp.float32)
    grad_value_bias = jnp.sum(d_values, axis=0, dtype=jnp.float32)
    total_grad = matmul_nt(d_queries, query_weight)
    total_grad = total_grad + matmul_nt(d_keys, key_weight)
    input_grad = (
        lax.psum_scatter(
            (total_grad + matmul_nt(d_values, value_weight)).astype(jnp.bfloat16),
            "mp",
            scatter_dimension=0,
            tiled=True,
        ).astype(jnp.float32)
        + d_middle
    )
    (
        grad_out_bias,
        grad_first_gain,
        grad_first_shift,
        grad_down_bias,
        grad_second_gain,
        grad_second_shift,
    ) = lax.psum(
        (
            grad_out_bias,
            grad_first_gain,
            grad_first_shift,
            grad_down_bias,
            grad_second_gain,
            grad_second_shift,
        ),
        ("dp", "mp"),
    )
    (
        grad_query_weight,
        grad_query_bias,
        grad_key_weight,
        grad_value_weight,
        grad_value_bias,
        grad_out_weight,
        grad_up_weight,
        grad_up_bias,
        grad_down_weight,
    ) = (
        lax.psum(grad_query_weight.astype(jnp.bfloat16), "dp").astype(jnp.float32),
        lax.psum(grad_query_bias.astype(jnp.bfloat16), "dp").astype(jnp.float32),
        lax.psum(grad_key_weight.astype(jnp.bfloat16), "dp").astype(jnp.float32),
        lax.psum(grad_value_weight.astype(jnp.bfloat16), "dp").astype(jnp.float32),
        lax.psum(grad_value_bias.astype(jnp.bfloat16), "dp").astype(jnp.float32),
        lax.psum(grad_out_weight.astype(jnp.bfloat16), "dp").astype(jnp.float32),
        lax.psum(grad_up_weight.astype(jnp.bfloat16), "dp").astype(jnp.float32),
        lax.psum(grad_up_bias.astype(jnp.bfloat16), "dp").astype(jnp.float32),
        lax.psum(grad_down_weight.astype(jnp.bfloat16), "dp").astype(jnp.float32),
    )
    return (
        result.astype(jnp.bfloat16),
        input_grad,
        grad_query_weight,
        grad_query_bias,
        grad_key_weight,
        grad_value_weight,
        grad_value_bias,
        grad_out_weight,
        grad_out_bias,
        grad_first_gain,
        grad_first_shift,
        grad_up_weight,
        grad_up_bias,
        grad_down_weight,
        grad_down_bias,
        grad_second_gain,
        grad_second_shift,
    )


def solution(mesh):
    in_specs = (
        P(("dp", "mp"), None),
        P("dp", None),
        P(("dp", "mp"), None),
        P(None, "mp"),
        P("mp"),
        P(None, "mp"),
        P(None, "mp"),
        P("mp"),
        P("mp", None),
        P(),
        P(),
        P(),
        P(None, "mp"),
        P("mp"),
        P("mp", None),
        P(),
        P(),
        P(),
    )
    out_specs = (
        P(("dp", "mp"), None),
        P(("dp", "mp"), None),
        P(None, "mp"),
        P("mp"),
        P(None, "mp"),
        P(None, "mp"),
        P("mp"),
        P("mp", None),
        P(),
        P(),
        P(),
        P(None, "mp"),
        P("mp"),
        P("mp", None),
        P(),
        P(),
        P(),
    )
    return jax.shard_map(body, mesh=mesh, in_specs=in_specs, out_specs=out_specs, check_vma=False)
```

profile of v0, /device:TPU:0, one launch (start us, length us, event | category | flops | bytes accessed | tf_op | source)
XLA Modules:
  0.0 849.8 jit_solution(10177189193593002505)
XLA Ops:
  10.3 35.1 %all-gather.5.cloned.1.call-done = bf16[1024,1024]{1,0:T(8,128)(2,1)} async-done(((bf16[512,1024]{1,0:T(8,128)(2,1)}), bf16[1024,1024]{1,0:T(8,128)(2,1)}) %all-gather.5.cloned.1.call-update) | async-done | bytes 2097168 | tf_op jit(solution)/shard_map/all_gather | solution.py:85
  45.4 3.1 add_convert_fusion.4
  48.5 2.1 reshape.313
  50.6 2.5 copy.52
  53.2 3.3 convolution_convert_fusion.7
  56.5 2.3 add_convert_fusion.3
  59.8 29.3 %while.47 = (s32[]{:T(128)}, bf16[2,512,8,64]{1,3,2,0:T(8,128)(2,1)}, f32[2,8,512]{2,1,0:T(8,128)S(1)}, s32[2,512]{1,0:T(2,128)S(1)}, s32[1024]{0:T(1024)S(1)}, ...) while((s32[]{:T(128)}, ...), condition=%wide.region_5.6_spmd, body=%wide.region_2.5_spmd.sunk | while | flops 1124855808 | bytes 64104620 | solution.py:105
  60.2 3.0 fusion.120
  63.2 4.2 fusion.121
  67.5 5.9 fusion.122
  74.8 3.0 fusion.120
  77.8 4.2 fusion.121
  82.1 5.9 fusion.122
  89.1 2.3 copy.53
  92.7 3.3 fusion.54
  96.2 54.3 %reduce-scatter.5.cloned.1.call-done = f32[512,1024]{1,0:T(8,128)} async-done(((f32[1024,1024]{1,0:T(8,128)}), f32[512,1024]{1,0:T(8,128)}) %reduce-scatter.5.cloned.1.call-update) | async-done | bytes 2097168 | tf_op jit(solution)/shard_map/reduce_scatter | solution.py:117
  150.5 2.3 fusion.53
  155.6 33.2 %all-gather.7.cloned.1.call-done = bf16[1024,1024]{1,0:T(8,128)(2,1)} async-done(((bf16[512,1024]{1,0:T(8,128)(2,1)}), bf16[1024,1024]{1,0:T(8,128)(2,1)}) %all-gather.7.cloned.1.call-update) | async-done | bytes 2097168 | tf_op jit(solution)/shard_map/all_gather | solution.py:120
  188.8 26.0 %multiply_convert_fusion.1 = (bf16[1024,2048]{1,0:T(8,128)(2,1)S(1)}, f32[1024,2048]{1,0:T(8,128)}, f32[1024,2048]{1,0:T(8,128)}) fusion(f32[2048]{0:T(1024)S(1)} %convert_element_type.190, bf16[1024,1024]{1,0:T(8,128)(2,1)} %all-gather.7.cloned.1.call-done, bf16[1024,2048]{1,0:T(8,128)(2,1)} %param.34), kind=kOutput, calls=%fused_computation.48 | convolution fusion | flops 4433379328 | bytes 27271168 | tf_op jit(solution)/shard_map/dot_general | solution.py:14
  214.8 1.9 copy-done.58
  216.8 6.0 fusion.55
  223.6 53.7 %reduce-scatter.7.cloned.1.call-done = f32[512,1024]{1,0:T(8,128)} async-done(((f32[1024,1024]{1,0:T(8,128)}), f32[512,1024]{1,0:T(8,128)}) %reduce-scatter.7.cloned.1.call-update) | async-done | bytes 2097168 | tf_op jit(solution)/shard_map/reduce_scatter | solution.py:124
  277.3 3.0 fusion.51
  282.2 2.0 fusion.50
  285.5 1.8 add_reduce_fusion.1
  287.4 33.2 %all-gather.9.cloned.1.call-done = bf16[1024,1024]{1,0:T(8,128)(2,1)} async-done(((bf16[512,1024]{1,0:T(8,128)(2,1)}), bf16[1024,1024]{1,0:T(8,128)(2,1)}) %all-gather.9.cloned.1.call-update) | async-done | bytes 2097168 | tf_op jit(solution)/shard_map/all_gather | solution.py:132
  320.6 14.0 %fusion.47 = (bf16[2048]{0:T(1024)(128)(2,1)}, bf16[1024,2048]{1,0:T(8,128)(2,1)S(1)}) fusion(f32[1024,2048]{1,0:T(8,128)} %get-tuple-element.390, f32[1024,2048]{1,0:T(8,128)} %get-tuple-element.402, f32[2048]{0:T(1024)S(1)} %convert_element_type.190, bf16[1024,1024]{1,0:T(8,128)(2,1)} %all-gather.9.cloned.1.call-done, bf16[2048,1024]{1,0:T(8,128)(2,1)} %param.36), kind=kOutput, calls=%fused_computation.112 | convolution fusion | flops 4328519680 | bytes 27275264 | tf_op jit(solution)/shard_map/dot_general | solution.py:24
  334.6 2.0 copy-done.56
  336.6 6.1 fusion.56
  342.7 54.4 %reduce-scatter.9.cloned.1.call-done = f32[512,1024]{1,0:T(8,128)} async-done(((f32[1024,1024]{1,0:T(8,128)}), f32[512,1024]{1,0:T(8,128)}) %reduce-scatter.9.cloned.1.call-update) | async-done | bytes 2097168 | tf_op jit(solution)/shard_map/reduce_scatter | solution.py:138
  397.1 4.5 multiply_reduce_fusion.2
  403.7 1.8 add_reduce_fusion
  405.6 33.2 %all-gather.11.cloned.1.call-done = bf16[1024,1024]{1,0:T(8,128)(2,1)} async-done(((bf16[512,1024]{1,0:T(8,128)(2,1)}), bf16[1024,1024]{1,0:T(8,128)(2,1)}) %all-gather.11.cloned.1.call-update) | async-done | bytes 2097168 | tf_op jit(solution)/shard_map/all_gather | solution.py:143
  438.8 3.8 convolution_convert_fusion.6
  442.6 4.0 reshape.312
  446.7 3.3 copy.56
  451.0 83.9 %while.48 = (s32[]{:T(128)}, f32[1024,8,64]{0,2,1:T(8,128)}, f32[1024,8,64]{0,2,1:T(8,128)}, bf16[2,512,8,64]{1,3,2,0:T(8,128)(2,1)}, bf16[2,512,8,64]{1,3,2,0:T...) while((s32[]{:T(128)}, f32[1024,8,64]{0,2,1:T(8,128)}, ...), condition=%wide.region_19.20_spmd.clone, body=%wide.region_17.19_spmd.clone.sunk | while | flops 2725769216 | bytes 221080080 | solution.py:176
  452.7 3.8 fusion.132
  456.5 11.6 %multiply_reduce_fusion.8 = (f32[8,512]{1,0:T(8,128)}, f32[8,512,1024]{2,1,0:T(8,128)}) fusion(f32[8,512,1024]{2,1,0:T(8,128)S(1)} %fusion.132, f32[8,512]{1,0:T(8,128)S(1)} %dynamic-slice_bitcast_fusion.2, bf16[1024,8,64]{0,2,1:T(8,128)(2,1)} %copy-done.5, bf16[2,512,8,64]{1,3,2,0:T(8,128)(2,1)} %copy-done.7, s32[]{:T(128)S(6)} %copy.83, ...), kind=kOutput, calls=%fused_computation.19.clone.1 | convolution fusion | flops 557838336 | bytes 35684356 | tf_op jit(solution)/shard_map/while/body/eval_jaxpr/while/body/eval_jaxpr/qhd,khd->hqk/dot_general | solution.py:42
  468.1 9.4 %multiply_convert_fusion.3 = bf16[8,512,1024]{2,1,0:T(8,128)(2,1)} fusion(f32[8,512,1024]{2,1,0:T(8,128)} %get-tuple-element.525, f32[8,512,1024]{2,1,0:T(8,128)S(1)} %fusion.132, f32[8,512]{1,0:T(8,128)} %get-tuple-element.526), kind=kLoop, calls=%fused_computation.18.clone.1 | loop fusion | flops 12582912 | bytes 41959424 | tf_op jit(solution)/shard_map/while/body/eval_jaxpr/while/body/eval_jaxpr/convert_element_type | solution.py:157
  477.6 8.8 %bitcast_add_fusion.5 = f32[1024,8,64]{0,2,1:T(8,128)} fusion(f32[1024,8,64]{0,2,1:T(8,128)} %get-tuple-element.569, f32[8,512,1024]{2,1,0:T(8,128)} %get-tuple-element.525, pred[]{:T(512)S(6)} %compare.3, bf16[2,512,8,64]{1,3,2,0:T(8,128)(2,1)S(1)} %copy-done.11, s32[]{:T(128)S(6)} %copy.83), kind=kOutput, calls=%fused_computation.23.clone.1 | convolution fusion | flops 542113792 | bytes 21495812 | tf_op jit(solution)/shard_map/while/body/eval_jaxpr/while/body/eval_jaxpr/hqk,qhd->khd/dot_general | solution.py:167
  486.8 2.7 fusion.133
  494.3 3.8 fusion.132
  498.0 11.6 %multiply_reduce_fusion.8 = (f32[8,512]{1,0:T(8,128)}, f32[8,512,1024]{2,1,0:T(8,128)}) fusion(f32[8,512,1024]{2,1,0:T(8,128)S(1)} %fusion.132, f32[8,512]{1,0:T(8,128)S(1)} %dynamic-slice_bitcast_fusion.2, bf16[1024,8,64]{0,2,1:T(8,128)(2,1)} %copy-done.5, bf16[2,512,8,64]{1,3,2,0:T(8,128)(2,1)} %copy-done.7, s32[]{:T(128)S(6)} %copy.83, ...), kind=kOutput, calls=%fused_computation.19.clone.1 | convolution fusion | flops 557838336 | bytes 35684356 | tf_op jit(solution)/shard_map/while/body/eval_jaxpr/while/body/eval_jaxpr/qhd,khd->hqk/dot_general | solution.py:42
  509.7 9.4 %multiply_convert_fusion.3 = bf16[8,512,1024]{2,1,0:T(8,128)(2,1)} fusion(f32[8,512,1024]{2,1,0:T(8,128)} %get-tuple-element.525, f32[8,512,1024]{2,1,0:T(8,128)S(1)} %fusion.132, f32[8,512]{1,0:T(8,128)} %get-tuple-element.526), kind=kLoop, calls=%fused_computation.18.clone.1 | loop fusion | flops 12582912 | bytes 41959424 | tf_op jit(solution)/shard_map/while/body/eval_jaxpr/while/body/eval_jaxpr/convert_element_type | solution.py:157
  519.1 9.4 %bitcast_add_fusion.5 = f32[1024,8,64]{0,2,1:T(8,128)} fusion(f32[1024,8,64]{0,2,1:T(8,128)} %get-tuple-element.569, f32[8,512,1024]{2,1,0:T(8,128)} %get-tuple-element.525, pred[]{:T(512)S(6)} %compare.3, bf16[2,512,8,64]{1,3,2,0:T(8,128)(2,1)S(1)} %copy-done.11, s32[]{:T(128)S(6)} %copy.83), kind=kOutput, calls=%fused_computation.23.clone.1 | convolution fusion | flops 542113792 | bytes 21495812 | tf_op jit(solution)/shard_map/while/body/eval_jaxpr/while/body/eval_jaxpr/hqk,qhd->khd/dot_general | solution.py:167
  528.9 2.7 fusion.133
  536.7 2.4 copy.57
  539.3 2.2 fusion.48
  544.2 2.7 add_convert_fusion.1
  547.0 9.5 %convolution_convert_fusion = bf16[2048,1024]{1,0:T(8,128)(2,1)} fusion(bf16[1024,2048]{1,0:T(8,128)(2,1)} %copy-done.58, bf16[1024,1024]{1,0:T(8,128)(2,1)} %all-gather.9.cloned.1.call-done), kind=kOutput, calls=%fused_computation.63 | convolution fusion | flops 4297064448 | bytes 10485760 | tf_op jit(solution)/shard_map/dot_general | solution.py:18
  556.5 6.5 convolution_convert_fusion.1
  563.0 2.3 convolution_convert_fusion.2
  565.3 2.2 fusion.41
  567.5 2.3 fusion.42
  569.8 2.3 fusion.43
  572.8 41.0 %all-reduce = (f32[1024]{0:T(1024)}, f32[1024]{0:T(1024)}, f32[1024]{0:T(1024)}, f32[1024]{0:T(1024)}, f32[1024]{0:T(1024)}, /*index=5*/f32[1024]{0:T(1024)}) all-reduce(f32[1024]{0:T(1024)S(1)} %copy-done.39, f32[1024]{0:T(1024)S(1)} %copy-done.37, f32[1024]{0:T(1024)S(1)} %copy-done.38, ...), channel_id=1, replica_groups=mesh['dp'=16,'mp'=2] {'dp','mp'}, use_global_device_ids=true, to_apply=%region_30.31 | all-reduce | flops 6144 | bytes 49152 | tf_op jit(solution)/shard_map/psum | solution.py:220
  614.2 35.3 %all-reduce.1 = (bf16[512]{0:T(512)(128)(2,1)S(1)}, bf16[512]{0:T(512)(128)(2,1)S(1)}, bf16[2048]{0:T(1024)(128)(2,1)S(1)}) all-reduce(bf16[512]{0:T(512)(128)(2,1)S(1)} %reduce_sum.235, bf16[512]{0:T(512)(128)(2,1)S(1)} %reduce_sum.237, bf16[2048]{0:T(1024)(128)(2,1)S(1)} %copy-done.41), channel_id=1, replica_groups=mesh['dp'=16,'mp'=2] {'dp'}, use_global_device_ids=true, to_apply=%region_23.24 | all-reduce | flops 3072 | bytes 12288 | tf_op jit(solution)/shard_map/psum | solution.py:243
  651.3 2.8 convert_add_fusion
  654.1 169.0 %all-reduce.5.cloned.1.call-done = (bf16[1024,512]{0,1:T(8,128)(2,1)}, bf16[1024,512]{0,1:T(8,128)(2,1)}, bf16[1024,512]{0,1:T(8,128)(2,1)}, bf16[512,1024]{1,0:...) async-done(((bf16[1024,512]{0,1:T(8,128)(2,1)}, bf16[1024,512]{0,1:T(8,128)(2,1)}, bf16[1024,512]{0,1:T(8,128)(2,1)}, bf16[512,1024]{1,0:T(8,128)(2,1)}, ...) | async-done | bytes 12582928 | tf_op jit(solution)/shard_map/psum | solution.py:242
  823.1 2.7 copy.58
  825.8 2.6 copy.59
  831.6 6.8 convert_element_type.220
  838.4 4.4 convert_element_type.223
  (222 shorter events, 39.2 us)
Async XLA Ops:
  7.2 85.5 %copy-start = (bf16[512,1024]{1,0:T(8,128)(2,1)S(1)}, bf16[512,1024]{1,0:T(8,128)(2,1)}, u32[]{:S(2)}) copy-start(bf16[512,1024]{1,0:T(8,128)(2,1)} %param.30) | copy-start | bytes 3145732
  7.2 38.2 %all-gather.5.cloned.1.call-start = ((), (), s32[]{:S(2)}) async-start(), calls=%async_computation.4 | async-start | bytes 3145728 | tf_op jit(solution)/shard_map/all_gather | solution.py:85
  7.9 142.6 %reduce-scatter.5.cloned.1.call-start = ((), (), s32[]{:S(2)}) async-start(), calls=%async_computation.5 | async-start | bytes 6291456 | tf_op jit(solution)/shard_map/reduce_scatter | solution.py:117
  53.1 3.3 copy-start.24
  53.1 3.3 copy-start.50
  63.2 4.3 copy-start.21
  77.8 4.3 copy-start.21
  92.7 3.4 copy-start.42
  92.7 3.4 copy-start.43
  92.7 3.4 copy-start.44
  96.1 92.7 %all-gather.7.cloned.1.call-start = ((), (), s32[]{:S(2)}) async-start(), calls=%async_computation.6 | async-start | bytes 3145728 | tf_op jit(solution)/shard_map/all_gather | solution.py:120
  152.8 1.3 copy-start.9
  152.8 2.8 copy-start.40
  155.5 121.8 %reduce-scatter.7.cloned.1.call-start = ((), (), s32[]{:S(2)}) async-start(), calls=%async_computation.7 | async-start | bytes 6291456 | tf_op jit(solution)/shard_map/reduce_scatter | solution.py:124
  188.8 27.9 %copy-start.48 = (bf16[2048,1024]{1,0:T(8,128)(2,1)S(1)}, bf16[2048,1024]{1,0:T(8,128)(2,1)}, u32[]{:S(2)}) copy-start(bf16[2048,1024]{1,0:T(8,128)(2,1)} %param.36) | copy-start | bytes 12582916
  214.8 2.0 copy-start.58
  222.8 97.8 %all-gather.9.cloned.1.call-start = ((), (), s32[]{:S(2)}) async-start(), calls=%async_computation.8 | async-start | bytes 3145728 | tf_op jit(solution)/shard_map/all_gather | solution.py:132
  277.3 3.4 copy-start.23
  284.2 1.3 copy-start.14
  287.3 109.8 %reduce-scatter.9.cloned.1.call-start = ((), (), s32[]{:S(2)}) async-start(), calls=%async_computation.9 | async-start | bytes 6291456 | tf_op jit(solution)/shard_map/reduce_scatter | solution.py:138
  320.6 16.0 %copy-start.49 = (bf16[1024,2048]{1,0:T(8,128)(2,1)S(1)}, bf16[1024,2048]{1,0:T(8,128)(2,1)}, u32[]{:S(2)}) copy-start(bf16[1024,2048]{1,0:T(8,128)(2,1)} %param.34) | copy-start | bytes 12582916
  334.6 2.0 copy-start.56
  342.7 96.1 %all-gather.11.cloned.1.call-start = ((), (), s32[]{:S(2)}) async-start(), calls=%async_computation.10 | async-start | bytes 3145728 | tf_op jit(solution)/shard_map/all_gather | solution.py:143
  397.1 4.6 copy-start.10
  402.3 1.3 copy-start.12
  402.4 40.3 %copy-start.32 = (f32[512]{0:T(512)}, f32[512]{0:T(512)S(1)}, u32[]{:S(2)}) copy-start(f32[512]{0:T(512)S(1)} %negate_multiply_fusion.1) | copy-start | bytes 6148
  405.5 245.8 %reduce-scatter.11.cloned.1.call-start = ((), (), s32[]{:S(2)}) async-start(), calls=%async_computation.11 | async-start | bytes 3145728 | tf_op jit(solution)/shard_map/reduce_scatter | solution.py:205
  468.1 9.4 %copy-start.11 = (bf16[2,512,8,64]{1,3,2,0:T(8,128)(2,1)S(1)}, bf16[2,512,8,64]{1,3,2,0:T(8,128)(2,1)}, u32[]{:S(2)}) copy-start(bf16[2,512,8,64]{1,3,2,0:T(8,128)(2,1)} %get-tuple-element.589) | copy-start | bytes 3145732 | tf_op jit(solution)/shard_map/while/body/eval_jaxpr/while
  477.5 8.8 %copy-start.2 = (bf16[8,512,1024]{2,1,0:T(8,128)(2,1)S(1)}, bf16[8,512,1024]{2,1,0:T(8,128)(2,1)}, u32[]{:S(2)}) copy-start(bf16[8,512,1024]{2,1,0:T(8,128)(2,1)} %multiply_convert_fusion.3) | copy-start | bytes 25165828 | tf_op jit(solution)/shard_map/while/body/eval_jaxpr/while
  477.5 8.8 %copy-start.6 = (bf16[1024,8,64]{0,2,1:T(8,128)(2,1)S(1)}, bf16[1024,8,64]{0,2,1:T(8,128)(2,1)}, u32[]{:S(2)}) copy-start(bf16[1024,8,64]{0,2,1:T(8,128)(2,1)} %copy-done.5) | copy-start | bytes 3145732 | tf_op jit(solution)/shard_map/while/body/eval_jaxpr/while
  477.5 9.2 %copy-start.15 = (bf16[2,512,8,64]{1,3,2,0:T(8,128)(2,1)S(1)}, bf16[2,512,8,64]{1,3,2,0:T(8,128)(2,1)}, u32[]{:S(2)}) copy-start(bf16[2,512,8,64]{1,3,2,0:T(8,128)(2,1)} %get-tuple-element.570) | copy-start | bytes 3145732 | tf_op jit(solution)/shard_map/while/body/eval_jaxpr/while
  486.8 2.7 copy-start.3
  486.8 2.7 copy-start.8
  489.4 1.8 copy-start.16
  489.5 3.1 copy-start.31
  491.3 1.3 copy-start.4
  509.7 9.4 %copy-start.11 = (bf16[2,512,8,64]{1,3,2,0:T(8,128)(2,1)S(1)}, bf16[2,512,8,64]{1,3,2,0:T(8,128)(2,1)}, u32[]{:S(2)}) copy-start(bf16[2,512,8,64]{1,3,2,0:T(8,128)(2,1)} %get-tuple-element.589) | copy-start | bytes 3145732 | tf_op jit(solution)/shard_map/while/body/eval_jaxpr/while
  519.1 9.4 %copy-start.2 = (bf16[8,512,1024]{2,1,0:T(8,128)(2,1)S(1)}, bf16[8,512,1024]{2,1,0:T(8,128)(2,1)}, u32[]{:S(2)}) copy-start(bf16[8,512,1024]{2,1,0:T(8,128)(2,1)} %multiply_convert_fusion.3) | copy-start | bytes 25165828 | tf_op jit(solution)/shard_map/while/body/eval_jaxpr/while
  519.1 9.4 %copy-start.6 = (bf16[1024,8,64]{0,2,1:T(8,128)(2,1)S(1)}, bf16[1024,8,64]{0,2,1:T(8,128)(2,1)}, u32[]{:S(2)}) copy-start(bf16[1024,8,64]{0,2,1:T(8,128)(2,1)} %copy-done.5) | copy-start | bytes 3145732 | tf_op jit(solution)/shard_map/while/body/eval_jaxpr/while
  519.1 9.8 %copy-start.15 = (bf16[2,512,8,64]{1,3,2,0:T(8,128)(2,1)S(1)}, bf16[2,512,8,64]{1,3,2,0:T(8,128)(2,1)}, u32[]{:S(2)}) copy-start(bf16[2,512,8,64]{1,3,2,0:T(8,128)(2,1)} %get-tuple-element.570) | copy-start | bytes 3145732 | tf_op jit(solution)/shard_map/while/body/eval_jaxpr/while
  528.9 2.7 copy-start.3
  528.9 2.7 copy-start.8
  531.6 1.8 copy-start.16
  531.6 3.1 copy-start.31
  533.4 1.3 copy-start.4
  536.7 4.8 copy-start.54
  539.3 3.5 copy-start.28
  541.5 1.3 copy-start.55
  542.9 1.3 copy-start.25
  546.9 276.2 %all-reduce.5.cloned.1.call-start = ((), (), s32[]{:S(2)}) async-start(), calls=%async_computation.12 | async-start | bytes 25165824 | tf_op jit(solution)/shard_map/psum | solution.py:242
  546.9 9.6 %copy-start.52 = (bf16[1024,1024]{1,0:T(8,128)(2,1)S(1)}, bf16[1024,1024]{1,0:T(8,128)(2,1)}, u32[]{:S(2)}) copy-start(bf16[1024,1024]{1,0:T(8,128)(2,1)} %all-gather.7.cloned.1.call-done) | copy-start | bytes 6291460
  547.0 9.6 %copy-start.57 = (bf16[1024,2048]{1,0:T(8,128)(2,1)S(1)}, bf16[1024,2048]{1,0:T(8,128)(2,1)}, u32[]{:S(2)}) copy-start(bf16[1024,2048]{1,0:T(8,128)(2,1)} %copy-done.56) | copy-start | bytes 12582916
  556.5 6.5 copy-start.19
  556.5 6.5 copy-start.53
  563.0 2.3 copy-start.29
  563.0 2.3 copy-start.51
  572.1 41.7 %copy-start.17 = (bf16[2,512,8,64]{1,3,2,0:T(8,128)(2,1)S(1)}, bf16[2,512,8,64]{1,3,2,0:T(8,128)(2,1)}, u32[]{:S(2)}) copy-start(bf16[2,512,8,64]{1,3,2,0:T(8,128)(2,1)} %get-tuple-element.172) | copy-start | bytes 3145732
  572.1 42.1 %copy-start.41 = (bf16[2048]{0:T(1024)(128)(2,1)S(1)}, bf16[2048]{0:T(1024)(128)(2,1)}, u32[]{:S(2)}) copy-start(bf16[2048]{0:T(1024)(128)(2,1)} %get-tuple-element.378) | copy-start | bytes 12292
  572.1 79.2 %copy-start.13 = (f32[512,1024]{1,0:T(8,128)S(1)}, f32[512,1024]{1,0:T(8,128)}, u32[]{:S(2)}) copy-start(f32[512,1024]{1,0:T(8,128)} %copy-done.12) | copy-start | bytes 6291460
  572.1 79.2 %copy-start.33 = (f32[512]{0:T(512)S(1)}, f32[512]{0:T(512)}, u32[]{:S(2)}) copy-start(f32[512]{0:T(512)} %copy-done.32) | copy-start | bytes 6148
  823.1 5.3 copy-start.27
  823.1 6.9 copy-start.26
  831.6 6.8 copy-start.20
  838.4 4.4 copy-start.1
  (18 other events, 16.6 us)
Sparse Core Ops, SparseCore 0:
  9.6 35.8 all-gather.4
  96.2 54.2 reduce-scatter.4
  155.6 33.1 all-gather.6
  222.9 54.3 reduce-scatter.6
  287.4 33.1 all-gather.8
  342.8 54.2 reduce-scatter.8
  405.6 33.1 all-gather.10
  547.0 31.8 reduce-scatter.10
  585.2 237.8 all-reduce.4
where the time goes:
time: 859 us; the launch traced here: 850 us
  waiting for transfers between devices  467 us (54%)
  matrix products  174 us (20%)
  blocking collectives  76.3 us (9%)
  other arithmetic  72.4 us (8%)
  local copies, waits for them, and re-layouts  43.9 us (5%)
  between operations  14.8 us (2%)
    psum x1, waiting for transfers between devices, body(): lax.psum(grad_query_weight.astype(jnp.bfloat16), 'dp').astype(jnp.float32)  169 us
    reduce_scatter x1, waiting for transfers between devices, body(): lax.psum_scatter(matmul_nt(d_pre, up_weight), 'mp', scatter_dimension=0,...  54.4 us
    reduce_scatter x1, waiting for transfers between devices, body(): lax.psum_scatter(matmul(context, out_weight), 'mp', scatter_dimension=0,...  54.3 us
    reduce_scatter x1, waiting for transfers between devices, body(): lax.psum_scatter(matmul(act, down_weight), 'mp', scatter_dimension=0, til...  53.7 us
    dot_general x6, matrix products, matmul(): return jnp.dot(left, right, preferred_element_type=jnp.float32)  44 us
    psum x1, blocking collectives, body(): lax.psum((grad_out_bias, grad_first_gain, grad_first_shift, grad_down_bia...  41 us
    psum x1, blocking collectives, body(): lax.psum(grad_query_bias.astype(jnp.bfloat16), 'dp').astype(jnp.float32)  35.3 us
    all_gather x1, waiting for transfers between devices, body(): gathered = lax.all_gather(tokens, 'mp', axis=0, tiled=True)  35.1 us
  transfers between devices with their start and end apart: 9, of which 8 were waited for; matrix products, arithmetic and copies ran while one was open for 4% of the time, Pallas kernels for 0%

commit v1 on v0

--- a/solution.py
+++ b/solution.py
@@ -1,13 +1,166 @@
+import functools
 import jax
 import jax.numpy as jnp
 from jax import lax
+from jax.experimental import pallas as pl
+from jax.experimental.pallas import tpu as pltpu
 from jax.sharding import PartitionSpec as P
 
 HEAD = 64
+LANES = 128
 
 
 epsilon = 1e-05
 masked_score = -1000000000.0
+
+
+def dot_nn(left, right):
+    return lax.dot_general(left, right, (((1,), (0,)), ((), ())), preferred_element_type=jnp.float32)
+
+
+def dot_nt(left, right):
+    return lax.dot_general(left, right, (((1,), (1,)), ((), ())), preferred_element_type=jnp.float32)
+
+
+def dot_tn(left, right):
+    return lax.dot_general(left, right, (((0,), (0,)), ((), ())), preferred_element_type=jnp.float32)
+
+
+def forward_kernel(pairs, q_ref, k_ref, v_ref, row_ref, col_ref, ctx_ref, lse_ref, bias_ref):
+    bias_ref[...] = jnp.where(col_ref[...] == row_ref[...], 0.0, masked_score)
+    rows = q_ref.shape[0]
+    lane = lax.broadcasted_iota(jnp.int32, (rows, LANES), 1)
+    stats = jnp.zeros((rows, LANES), jnp.float32)
+    for pair in range(pairs):
+        cols = slice(pair * LANES, (pair + 1) * LANES)
+        q_pair = q_ref[:, cols] * jnp.bfloat16(HEAD ** (-0.5))
+        k_pair = k_ref[:, cols]
+        v_pair = v_ref[:, cols]
+        halves = []
+        for half in range(2):
+            keep = (lane >= HEAD) == (half == 1)
+            q_half = jnp.where(keep, q_pair, jnp.bfloat16(0))
+            scores = dot_nt(q_half, k_pair) + bias_ref[...]
+            row_max = jnp.max(scores, axis=-1, keepdims=True)
+            exponent = jnp.exp(scores - row_max)
+            row_sum = jnp.sum(exponent, axis=-1, keepdims=True)
+            blended = dot_nn(exponent.astype(jnp.bfloat16), v_pair)
+            halves.append(blended * (1.0 / row_sum))
+            stats = jnp.where(lane == 2 * pair + half, row_max + jnp.log(row_sum), stats)
+        ctx_ref[:, cols] = jnp.where(lane >= HEAD, halves[1], halves[0]).astype(ctx_ref.dtype)
+    lse_ref[...] = jnp.transpose(stats)[: lse_ref.shape[0], :]
+
+
+def attention_forward(queries, key_rows, values, segment, block=256):
+    length, width = queries.shape
+    pairs = width // LANES
+    heads = width // HEAD
+    whole = lambda shape: pl.BlockSpec(shape, lambda i: (0, 0))
+    return pl.pallas_call(
+        functools.partial(forward_kernel, pairs),
+        grid=(length // block,),
+        in_specs=[
+            pl.BlockSpec((block, width), lambda i: (i, 0)),
+            whole((length, width)),
+            whole((length, width)),
+            whole((1, length)),
+            pl.BlockSpec((block, 1), lambda i: (i, 0)),
+        ],
+        out_specs=[
+            pl.BlockSpec((block, width), lambda i: (i, 0)),
+            pl.BlockSpec((heads, block), lambda i: (0, i)),
+        ],
+        out_shape=[
+            jax.ShapeDtypeStruct((length, width), jnp.bfloat16),
+            jax.ShapeDtypeStruct((heads, length), jnp.float32),
+        ],
+        scratch_shapes=[pltpu.VMEM((block, length), jnp.float32)],
+        compiler_params=pltpu.CompilerParams(vmem_limit_bytes=48 * 1024 * 1024),
+        name="attention_forward",
+    )(queries, key_rows, values, segment.reshape(1, length), segment.reshape(length, 1))
+
+
+def backward_kernel(
+    pairs, q_ref, k_ref, v_ref, g_ref, c_ref, lse_ref, row_ref, col_ref,
+    dq_ref, dk_ref, dv_ref, bias_ref, dk_sum, dv_sum,
+):
+    step = pl.program_id(0)
+    bias_ref[...] = jnp.where(col_ref[...] == row_ref[...], 0.0, masked_score)
+    rows = q_ref.shape[0]
+    lane = lax.broadcasted_iota(jnp.int32, (rows, LANES), 1)
+    key_lane = lax.broadcasted_iota(jnp.int32, (k_ref.shape[0], LANES), 1)
+    inner = jnp.zeros((rows, LANES), jnp.float32)
+    for pair in range(pairs):
+        cols = slice(pair * LANES, (pair + 1) * LANES)
+        both = g_ref[:, cols].astype(jnp.float32) * c_ref[:, cols].astype(jnp.float32)
+        low = jnp.sum(jnp.where(lane < HEAD, both, 0.0), axis=-1, keepdims=True)
+        high = jnp.sum(jnp.where(lane < HEAD, 0.0, both), axis=-1, keepdims=True)
+        inner = jnp.where(lane == 2 * pair, low, jnp.where(lane == 2 * pair + 1, high, inner))
+    inner = jnp.transpose(inner)
+
+    @pl.when(step == 0)
+    def _():
+        dk_sum[...] = jnp.zeros_like(dk_sum)
+        dv_sum[...] = jnp.zeros_like(dv_sum)
+
+    for pair in range(pairs):
+        cols = slice(pair * LANES, (pair + 1) * LANES)
+        q_pair = q_ref[:, cols] * jnp.bfloat16(HEAD ** (-0.5))
+        k_pair = k_ref[:, cols]
+        v_pair = v_ref[:, cols]
+        g_pair = g_ref[:, cols]
+        dq = None
+        for half in range(2):
+            head = 2 * pair + half
+            keep = (lane >= HEAD) == (half == 1)
+            q_half = jnp.where(keep, q_pair, jnp.bfloat16(0))
+            g_half = jnp.where(keep, g_pair, jnp.bfloat16(0))
+            k_half = jnp.where((key_lane >= HEAD) == (half == 1), k_pair, jnp.bfloat16(0))
+            probs = jnp.exp(dot_nt(k_pair, q_half) + bias_ref[...] - lse_ref[head : head + 1, :])
+            d_probs = dot_nt(v_pair, g_half)
+            d_scores = (probs * (d_probs - inner[head : head + 1, :])).astype(jnp.bfloat16)
+            dv_sum[:, cols] += dot_nn(probs.astype(jnp.bfloat16), g_half)
+            dk_sum[:, cols] += dot_nn(d_scores, q_half)
+            part = dot_tn(d_scores, k_half)
+            dq = part if dq is None else dq + part
+        dq_ref[:, cols] = (dq * HEAD ** (-0.5)).astype(dq_ref.dtype)
+
+    @pl.when(step == pl.num_programs(0) - 1)
+    def _():
+        dk_ref[...] = dk_sum[...].astype(dk_ref.dtype)
+        dv_ref[...] = dv_sum[...].astype(dv_ref.dtype)
+
+
+def attention_backward(queries, key_rows, values, d_context, context, lse, segment, block=256):
+    length, width = queries.shape
+    pairs = width // LANES
+    heads = width // HEAD
+    whole = lambda shape: pl.BlockSpec(shape, lambda i: (0, 0))
+    part = pl.BlockSpec((block, width), lambda i: (i, 0))
+    return pl.pallas_call(
+        functools.partial(backward_kernel, pairs),
+        grid=(length // block,),
+        in_specs=[
+            part,
+            whole((length, width)),
+            whole((length, width)),
+            part,
+            part,
+            pl.BlockSpec((heads, block), lambda i: (0, i)),
+            pl.BlockSpec((1, block), lambda i: (0, i)),
+            whole((length, 1)),
+        ],
+        out_specs=[part, whole((length, width)), whole((length, width))],
+        out_shape=[jax.ShapeDtypeStruct((length, width), jnp.bfloat16)] * 3,
+        scratch_shapes=[
+            pltpu.VMEM((length, block), jnp.float32),
+            pltpu.VMEM((length, width), jnp.float32),
+            pltpu.VMEM((length, width), jnp.float32),
+        ],
+        compiler_params=pltpu.CompilerParams(vmem_limit_bytes=48 * 1024 * 1024),
+        name="attention_backward",
+    )(queries, key_rows, values, d_context, context, lse,
+      segment.reshape(1, length), segment.reshape(length, 1))
 
 
 def matmul(left, right):
@@ -46,7 +199,7 @@
     return jnp.where(same[None], raw, masked_score)
 
 
-def body(
+def body_general(
     tokens,
     doc_lengths,
     cotangent,
@@ -270,6 +423,237 @@
     )
 
 
+def swap(rows):
+    return lax.ppermute(rows, "mp", [(0, 1), (1, 0)])
+
+
+def normal_parts(pre):
+    size = jnp.abs(pre) * (0.5**0.5)
+    t = 1.0 / (1.0 + 0.3275911 * size)
+    bell = jnp.exp(-size * size)
+    series = t * (
+        0.254829592
+        + t * (-0.284496736 + t * (1.421413741 + t * (-1.453152027 + t * 1.061405429)))
+    )
+    tail = 0.5 * series * bell
+    return jnp.where(pre < 0, tail, 1.0 - tail), pre * bell * 0.3989422804014327
+
+
+def gelu_parts(pre):
+    cumulative, slope = normal_parts(pre)
+    return (pre * cumulative).astype(jnp.bfloat16), (cumulative + slope).astype(jnp.bfloat16)
+
+
+def norm_stats(inputs):
+    center = inputs - jnp.mean(inputs, axis=-1, keepdims=True)
+    spread = jnp.mean(center * center, axis=-1, keepdims=True)
+    inverse = lax.rsqrt(spread + epsilon)
+    return center * inverse, inverse
+
+
+def norm_back(upstream, normal, inverse, gain):
+    scaled = upstream * gain
+    mean = jnp.mean(scaled, axis=-1, keepdims=True)
+    along = jnp.mean(scaled * normal, axis=-1, keepdims=True)
+    back = (scaled - mean - normal * along) * inverse
+    return back, jnp.sum(upstream * normal, axis=0), jnp.sum(upstream, axis=0)
+
+
+def body_pair(
+    tokens,
+    doc_lengths,
+    cotangent,
+    query_weight,
+    query_bias,
+    key_weight,
+    value_weight,
+    value_bias,
+    out_weight,
+    out_bias,
+    first_gain,
+    first_shift,
+    up_weight,
+    up_bias,
+    down_weight,
+    down_bias,
+    second_gain,
+    second_shift,
+):
+    own_rows = tokens.shape[0]
+    length = 2 * own_rows
+    doc_count = doc_lengths.shape[1]
+    side = lax.axis_index("mp")
+    first = side == 0
+    f32 = jnp.float32
+    bf16 = jnp.bfloat16
+
+    def in_order(own, other):
+        return jnp.concatenate([jnp.where(first, own, other), jnp.where(first, other, own)])
+
+    def split(whole):
+        own = lax.dynamic_slice_in_dim(whole, side * own_rows, own_rows, 0)
+        other = lax.dynamic_slice_in_dim(whole, (1 - side) * own_rows, own_rows, 0)
+        return own, other
+
+    segment = segment_ids(doc_lengths, length)[0]
+    valid_rows = lax.dynamic_slice_in_dim(segment < doc_count - 1, side * own_rows, own_rows, 0)
+    gain_first = first_gain.astype(f32)
+    gain_second = second_gain.astype(f32)
+
+    gathered = in_order(tokens, swap(tokens))
+    out_other = swap(out_weight)
+    queries = (matmul(gathered, query_weight) + query_bias).astype(bf16)
+    key_rows = matmul(gathered, key_weight).astype(bf16)
+    values = (matmul(gathered, value_weight) + value_bias).astype(bf16)
+    context, log_mass = attention_forward(queries, key_rows, values, segment)
+    context_own, context_away = split(context)
+    context_here = swap(context_away)
+
+    middle = (
+        matmul(context_own, out_weight)
+        + matmul(context_here, out_other)
+        + out_bias
+        + tokens.astype(f32)
+    )
+    normal_first, inverse_first = norm_stats(middle)
+    hidden = normal_first * gain_first + first_shift
+    hidden_own = hidden.astype(bf16)
+    hidden_other = swap(hidden_own)
+
+    act_own, slope_own = gelu_parts(matmul(hidden_own, up_weight) + up_bias)
+    act_other, slope_other = gelu_parts(matmul(hidden_other, up_weight) + up_bias)
+    back = swap(matmul(act_other, down_weight).astype(bf16))
+    final = matmul(act_own, down_weight) + back.astype(f32) + down_bias + hidden
+    normal_second, inverse_second = norm_stats(final)
+    output = (normal_second * gain_second + second_shift).astype(bf16)
+    upstream = cotangent.astype(f32) * valid_rows[:, None].astype(f32)
+    d_final, grad_second_gain, grad_second_shift = norm_back(
+        upstream, normal_second, inverse_second, gain_second
+    )
+    grad_down_bias = jnp.sum(d_final, axis=0)
+    final_own = d_final.astype(bf16)
+    final_other = swap(final_own)
+    d_pre_own = (matmul_nt(final_own, down_weight) * slope_own).astype(bf16)
+    d_pre_other = (matmul_nt(final_other, down_weight) * slope_other).astype(bf16)
+    back = swap(matmul_nt(d_pre_other, up_weight).astype(bf16))
+    d_hidden = matmul_nt(d_pre_own, up_weight) + back.astype(f32) + d_final
+    grad_down_weight = matmul_tn(act_own, final_own) + matmul_tn(act_other, final_other)
+    grad_up_weight = matmul_tn(hidden_own, d_pre_own) + matmul_tn(hidden_other, d_pre_other)
+    grad_up_bias = jnp.sum(d_pre_own, axis=0, dtype=f32) + jnp.sum(d_pre_other, axis=0, dtype=f32)
+
+    d_middle, grad_first_gain, grad_first_shift = norm_back(
+        d_hidden, normal_first, inverse_first, gain_first
+    )
+    grad_out_bias = jnp.sum(d_middle, axis=0)
+    middle_own = d_middle.astype(bf16)
+    d_context_away = swap(matmul_nt(middle_own, out_other).astype(bf16))
+    d_context = in_order(matmul_nt(middle_own, out_weight).astype(bf16), d_context_away)
+    grad_out_weight = matmul_tn(context_own, middle_own) + swap(
+        matmul_tn(context_here, middle_own).astype(bf16)
+    ).astype(f32)
+
+    d_queries, d_keys, d_values = attention_backward(
+        queries, key_rows, values, d_context, context, log_mass, segment
+    )
+    dq_own, dq_other = split(d_queries)
+    dk_own, dk_other = split(d_keys)
+    dv_own, dv_other = split(d_values)
+    back = swap(
+        (
+            matmul_nt(dq_other, query_weight)
+            + matmul_nt(dk_other, key_weight)
+            + matmul_nt(dv_other, value_weight)
+        ).astype(bf16)
+    )
+    input_grad = (
+        matmul_nt(dq_own, query_weight)
+        + matmul_nt(dk_own, key_weight)
+        + matmul_nt(dv_own, value_weight)
+        + back.astype(f32)
+        + d_middle
+    )
+    grad_query_weight = matmul_tn(gathered, d_queries)
+    grad_key_weight = matmul_tn(gathered, d_keys)
+    grad_value_weight = matmul_tn(gathered, d_values)
+    grad_query_bias = jnp.sum(d_queries, axis=0, dtype=f32)
+    grad_value_bias = jnp.sum(d_values, axis=0, dtype=f32)
+
+    shared = jnp.stack(
+        [
+            grad_out_bias,
+            grad_first_gain,
+            grad_first_shift,
+            grad_down_bias,
+            grad_second_gain,
+            grad_second_shift,
+        ]
+    )
+    shared = (shared + swap(shared)).astype(bf16)
+    low = lambda items: tuple(item.astype(bf16) for item in items)
+    grad_down_weight, grad_up_weight = lax.psum(low((grad_down_weight, grad_up_weight)), "dp")
+    (
+        grad_down_weight,
+        grad_up_weight,
+        grad_query_weight,
+        grad_key_weight,
+        grad_value_weight,
+        grad_out_weight,
+    ) = lax.optimization_barrier(
+        (
+            grad_down_weight,
+            grad_up_weight,
+            grad_query_weight,
+            grad_key_weight,
+            grad_value_weight,
+            grad_out_weight,
+        )
+    )
+    (
+        grad_query_weight,
+        grad_key_weight,
+        grad_value_weight,
+        grad_out_weight,
+        grad_query_bias,
+        grad_value_bias,
+        grad_up_bias,
+        shared,
+    ) = lax.psum(
+        low(
+            (
+                grad_query_weight,
+                grad_key_weight,
+                grad_value_weight,
+                grad_out_weight,
+                grad_query_bias,
+                grad_value_bias,
+                grad_up_bias,
+                shared,
+            )
+        ),
+        "dp",
+    )
+    shared = shared.astype(f32)
+    return (
+        output,
+        input_grad,
+        grad_query_weight.astype(f32),
+        grad_query_bias.astype(f32),
+        grad_key_weight.astype(f32),
+        grad_value_weight.astype(f32),
+        grad_value_bias.astype(f32),
+        grad_out_weight.astype(f32),
+        shared[0],
+        shared[1],
+        shared[2],
+        grad_up_weight.astype(f32),
+        grad_up_bias.astype(f32),
+        grad_down_weight.astype(f32),
+        shared[3],
+        shared[4],
+        shared[5],
+    )
+
+
 def solution(mesh):
     in_specs = (
         P(("dp", "mp"), None),
@@ -310,4 +694,5 @@
         P(),
         P(),
     )
+    body = body_pair if mesh.shape["mp"] == 2 else body_general
     return jax.shard_map(body, mesh=mesh, in_specs=in_specs, out_specs=out_specs, check_vma=False)

time: 859 us -> 489 us (0.57)
  waiting for transfers between devices: 467 us -> 214 us
  matrix products: 174 us -> 96.6 us
  Pallas kernels: 0 us -> 45.3 us
  local copies, waits for them, and re-layouts: 43.9 us -> 4.78 us
  other arithmetic: 72.4 us -> 34.6 us
  blocking collectives: 76.3 us -> 61.4 us
  starting transfers between devices: 0.77 us -> 13.2 us
    reduce_scatter x4 -> x0, waiting for transfers between devices: 162 us -> none  [the longest x1 54.4 us: body(): lax.psum_scatter(matmul_nt(d_pre, up_weight), 'mp', scatter_dimension=0,...]
    all_gather x4 -> x0, waiting for transfers between devices: 135 us -> none  [the longest x1 35.1 us: body(): gathered = lax.all_gather(tokens, 'mp', axis=0, tiled=True)]
    ppermute x0 -> x11, waiting for transfers between devices: none -> 90.7 us  [swap(): return lax.ppermute(rows, 'mp', [(0, 1), (1, 0)])]
    dot_general x14 -> x0, matrix products: 75.7 us -> none  [the longest x4 29.3 us: score_block(): jnp.einsum('qhd,khd->hqk', q_block, key_rows, preferred_element_type=jnp....]
    psum x1 -> x2, waiting for transfers between devices: 169 us -> 123 us  [the longest x1 95.7 us: body_pair(): lax.psum(low((grad_down_weight, grad_up_weight)), 'dp')]
    pallas_call x0 -> x2, Pallas kernels: none -> 45.3 us  [the longest x1 27.6 us: attention_backward(): pl.pallas_call(functools.partial(backward_kernel, pairs), grid=(length //...]
    reduce_sum x14 -> x7, other arithmetic: 29.1 us -> 7.3 us  [the longest x1 1.97 us: body_pair(): grad_out_bias = jnp.sum(d_middle, axis=0)]
    dot_general x6 -> x9, matrix products: 44 us -> 24 us  [matmul(): return jnp.dot(left, right, preferred_element_type=jnp.float32)]
  transfers between devices with their start and end apart: 9 -> 13, of which waited for: 8 -> 9; matrix products, arithmetic and copies ran while one was open for 4% -> 20% of each run, Pallas kernels for 0% -> 9%
where the time goes in v1:
time: 489 us; the launch traced here: 485 us
  waiting for transfers between devices  214 us (44%)
  matrix products  96.6 us (20%)
  blocking collectives  61.4 us (13%)
  Pallas kernels  45.3 us (9%)
  other arithmetic  34.6 us (7%)
  between operations  15 us (3%)
  starting transfers between devices  13.2 us (3%)
    psum x1, waiting for transfers between devices, body_pair(): lax.psum(low((grad_down_weight, grad_up_weight)), 'dp')  95.7 us
    ppermute x11, waiting for transfers between devices, swap(): return lax.ppermute(rows, 'mp', [(0, 1), (1, 0)])  90.7 us
    psum x1, blocking collectives, body_pair(): lax.psum(low((grad_query_weight, grad_key_weight, grad_value_weight, grad...  61.4 us
    dot_general x12, matrix products, matmul_nt(): lax.dot_general(left, right, (((1,), (1,)), ((), ())), preferred_element_...  43 us
    dot_general x9, matrix products, matmul_tn(): lax.dot_general(left, right, (((0,), (0,)), ((), ())), preferred_element_...  29.6 us
    psum x1, waiting for transfers between devices, body_pair(): lax.psum(low((grad_query_weight, grad_key_weight, grad_value_weight, grad...  27.8 us
    pallas_call x1, Pallas kernels, attention_backward(): pl.pallas_call(functools.partial(backward_kernel, pairs), grid=(length //...  27.6 us
    dot_general x9, matrix products, matmul(): return jnp.dot(left, right, preferred_element_type=jnp.float32)  24 us
  transfers between devices with their start and end apart: 13, of which 9 were waited for; matrix products, arithmetic and copies ran while one was open for 20% of the time, Pallas kernels for 9%

profile of v1, /device:TPU:0, one launch (start us, length us, event | category | flops | bytes accessed | tf_op | source)
XLA Modules:
  0.0 485.1 jit_solution(15776247596508213274)
XLA Ops:
  7.3 3.0 collective-permute-start
  10.3 0.8 reduce_window_sum.14
  12.9 21.7 %collective-permute-done = bf16[512,1024]{1,0:T(8,128)(2,1)} collective-permute-done((bf16[512,1024]{1,0:T(8,128)(2,1)}, bf16[512,1024]{1,0:T(8,128)(2,1)}, u32[]{:S(2)}, u32[]{:S(2)}) %collective-permute-start) | collective-permute-done | bytes 1048608 | tf_op jit(solution)/shard_map/ppermute | solution.py:427
  34.6 1.7 broadcast_select_fusion.1
  36.3 1.2 add_convert_fusion.6.v_ref
  37.6 1.2 convolution_convert_fusion.k_ref
  39.2 1.2 add_convert_fusion.7.q_ref
  40.5 17.8 %attention_forward.1 = (bf16[1024,512]{1,0:T(8,128)(2,1)S(1)}, f32[8,1024]{1,0:T(8,128)S(1)}) custom-call(bf16[1024,512]{1,0:T(8,128)(2,1)S(1)} %add_convert_fusion.7.q_ref, bf16[1024,512]{1,0:T(8,128)(2,1)S(1)} %convolution_convert_fusion.k_ref, bf16[1024,512]{1,0:T(8,128)(2,1)S(1)} %add_convert_fusion.6.v_ref, s32[1,1024]{1,0:T(1,128)S(1)} %bitcast.61, ...), custom_call_target="tpu_custom_call" | custom-call | tf_op jit(solution)/shard_map/attention_forward/pallas_call | solution.py:59
  58.3 2.1 collective-permute-start.1
  60.5 2.0 fusion.18
  62.6 8.2 %collective-permute-done.1 = bf16[512,512]{1,0:T(8,128)(2,1)} collective-permute-done((bf16[512,512]{1,0:T(8,128)(2,1)S(1)}, bf16[512,512]{1,0:T(8,128)(2,1)}, u32[]{:S(2)}, u32[]{:S(2)}) %collective-permute-start.1) | collective-permute-done | bytes 524320 | tf_op jit(solution)/shard_map/ppermute | solution.py:427
  70.8 2.3 fusion.38
  73.9 1.5 collective-permute-start.3
  75.5 21.0 %collective-permute-done.3 = bf16[512,1024]{1,0:T(8,128)(2,1)S(1)} collective-permute-done((bf16[512,1024]{1,0:T(8,128)(2,1)S(1)}, bf16[512,1024]{1,0:T(8,128)(2,1)S(1)}, u32[]{:S(2)}, u32[]{:S(2)}) %collective-permute-start.3) | collective-permute-done | bytes 1048608 | tf_op jit(solution)/shard_map/ppermute | solution.py:427
  96.6 2.4 fusion.39
  99.0 2.0 copy-done.38
  101.0 5.1 %convolution_convert_fusion.3 = bf16[512,1024]{1,0:T(8,128)(2,1)S(1)} fusion(bf16[2048,1024]{1,0:T(8,128)(2,1)S(1)} %copy-done.35, f32[512,2048]{1,0:T(8,128)S(1)} %fusion.39, f32[2048]{0:T(1024)S(1)} %convert_element_type.199), kind=kOutput, calls=%fused_computation.46 | convolution fusion | flops 2173173760 | bytes 9445376 | tf_op jit(solution)/shard_map/dot_general | solution.py:167
  106.9 5.8 %multiply_convert_fusion.3 = (bf16[512,2048]{1,0:T(8,128)(2,1)S(1)}, f32[512,2048]{1,0:T(8,128)S(1)}) fusion(f32[2048]{0:T(1024)S(1)} %convert_element_type.199, bf16[512,1024]{1,0:T(8,128)(2,1)S(1)} %fusion.5, bf16[1024,2048]{1,0:T(8,128)(2,1)S(1)} %copy-done.36), kind=kOutput, calls=%fused_computation.15 | convolution fusion | flops 2172649472 | bytes 11542528 | tf_op jit(solution)/shard_map/dot_general | solution.py:167
  112.7 15.1 %collective-permute-done.4 = bf16[512,1024]{1,0:T(8,128)(2,1)S(1)} collective-permute-done((bf16[512,1024]{1,0:T(8,128)(2,1)S(1)}, bf16[512,1024]{1,0:T(8,128)(2,1)S(1)}, u32[]{:S(2)}, u32[]{:S(2)}) %collective-permute-start.4) | collective-permute-done | bytes 1048608 | tf_op jit(solution)/shard_map/ppermute | solution.py:427
  127.8 2.8 fusion.36
  130.9 1.1 multiply_reduce_fusion
  132.1 1.9 fusion.34
  133.9 1.3 copy-done.13
  135.8 6.3 %convert_reduce_fusion.1 = (f32[2048]{0:T(1024)S(1)}, bf16[512,2048]{1,0:T(8,128)(2,1)S(1)}) fusion(f32[512,2048]{1,0:T(8,128)S(1)} %get-tuple-element.78, f32[2048]{0:T(1024)S(1)} %convert_element_type.199, bf16[512,1024]{1,0:T(8,128)(2,1)S(1)} %convert_element_type.210, bf16[2048,1024]{1,0:T(8,128)(2,1)S(1)} %copy-done.35), kind=kOutput, calls=%fused_computation.9 | convolution fusion | flops 2179987456 | bytes 11550720 | tf_op jit(solution)/shard_map/dot_general | solution.py:177
  142.1 2.4 fusion.40
  144.5 2.4 fusion.41
  146.9 9.3 %collective-permute-done.5 = bf16[512,1024]{1,0:T(8,128)(2,1)S(1)} collective-permute-done((bf16[512,1024]{1,0:T(8,128)(2,1)S(1)}, bf16[512,1024]{1,0:T(8,128)(2,1)S(1)}, u32[]{:S(2)}, u32[]{:S(2)}) %collective-permute-start.5) | collective-permute-done | bytes 1048608 | tf_op jit(solution)/shard_map/ppermute | solution.py:427
  156.2 7.7 %convert_reduce_fusion = (f32[2048]{0:T(1024)S(1)}, bf16[512,2048]{1,0:T(8,128)(2,1)S(1)}) fusion(f32[512,2048]{1,0:T(8,128)} %copy-done.38, f32[2048]{0:T(1024)S(1)} %convert_element_type.199, bf16[512,1024]{1,0:T(8,128)(2,1)S(1)} %collective-permute-done.5, bf16[2048,1024]{1,0:T(8,128)(2,1)S(1)} %copy-done.35), kind=kOutput, calls=%fused_computation.8 | convolution fusion | flops 2179987456 | bytes 11550720 | tf_op jit(solution)/shard_map/dot_general | solution.py:177
  163.9 3.4 convolution_convert_fusion.2
  167.6 9.8 %add_convert_fusion.1 = bf16[2048,1024]{1,0:T(8,128)(2,1)} fusion(f32[2048,1024]{1,0:T(8,128)S(1)} %fusion.40, bf16[512,1024]{1,0:T(8,128)(2,1)S(1)} %collective-permute-done.5, f32[512,2048]{1,0:T(8,128)} %copy-done.38, f32[2048]{0:T(1024)S(1)} %convert_element_type.199), kind=kOutput, calls=%fused_computation.1 | convolution fusion | flops 2176843776 | bytes 17833984 | tf_op jit(solution)/shard_map/dot_general | solution.py:171
  177.4 4.7 add_convert_fusion
  182.4 5.1 %collective-permute-done.6 = bf16[512,1024]{1,0:T(8,128)(2,1)} collective-permute-done((bf16[512,1024]{1,0:T(8,128)(2,1)}, bf16[512,1024]{1,0:T(8,128)(2,1)}, u32[]{:S(2)}, u32[]{:S(2)}) %collective-permute-start.6) | collective-permute-done | bytes 1048608 | tf_op jit(solution)/shard_map/ppermute | solution.py:427
  187.4 7.5 %multiply_reduce_fusion.1 = (f32[1024]{0:T(1024)S(1)}, f32[512]{0:T(512)S(1)}, f32[512]{0:T(512)S(1)}, f32[1024]{0:T(1024)S(1)}, f32[512,1024]{1,0:T(8,128)S(1)}) fusion(f32[512,1024]{1,0:T(8,128)} %copy-done.10, f32[512]{0:T(512)S(1)} %add_rsqrt_fusion.1, f32[512]{0:T(512)S(1)} %broadcast_multiply_fusion.5, f32[1024]{0:T(1024)S(1)} %convert_element_type.196, ...), kind=kOutput, calls=%fused_computation.18 | convolution fusion | flops 2153772032 | bytes 13651968 | tf_op jit(solution)/shard_map/dot_general | solution.py:177
  195.0 2.0 fusion.35
  197.0 1.2 collective-permute-start.10
  198.2 1.9 convert_element_type.219
  200.1 2.0 convolution_convert_fusion.4
  202.1 0.9 collective-permute-start.7
  203.0 1.8 convolution_convert_fusion.1
  204.9 1.2 collective-permute-start.9
  206.8 10.2 %collective-permute-done.7 = bf16[512,512]{1,0:T(8,128)(2,1)S(1)} collective-permute-done((bf16[512,512]{1,0:T(8,128)(2,1)S(1)}, bf16[512,512]{1,0:T(8,128)(2,1)S(1)}, u32[]{:S(2)}, u32[]{:S(2)}) %collective-permute-start.7) | collective-permute-done | bytes 524320 | tf_op jit(solution)/shard_map/ppermute | solution.py:427
  217.1 1.0 pad_maximum_fusion.1.g_ref
  218.2 27.6 %attention_backward.1 = (bf16[1024,512]{1,0:T(8,128)(2,1)S(1)}, bf16[1024,512]{1,0:T(8,128)(2,1)S(1)}, bf16[1024,512]{1,0:T(8,128)(2,1)S(1)}) custom-call(bf16[1024,512]{1,0:T(8,128)(2,1)S(1)} %copy-done.7, bf16[1024,512]{1,0:T(8,128)(2,1)S(1)} %copy-done.5, bf16[1024,512]{1,0:T(8,128)(2,1)} %copy-done.3, bf16[1024,512]{1,0:T(8,128)(2,1)} %pad_maximum_fusion.1.g_ref, ...), custom_call_target="tpu_custom_call" | custom-call | tf_op jit(solution)/shard_map/attention_backward/pallas_call | solution.py:140
  245.8 2.3 fusion.32
  248.1 2.1 fusion.7
  250.1 2.2 fusion.33
  252.4 2.3 fusion.31
  254.7 1.7 convert_add_fusion
  256.4 95.7 %all-reduce.8.cloned.1.call-done = (bf16[2048,1024]{1,0:T(8,128)(2,1)}, bf16[1024,2048]{1,0:T(8,128)(2,1)}) async-done(((bf16[2048,1024]{1,0:T(8,128)(2,1)}, bf16[1024,2048]{1,0:T(8,128)(2,1)}), (bf16[2048,1024]{1,0:T(8,128)(2,1)}, bf16[1024,2048]{1,0:T(8,128)(2,1)})) %all-reduce.8.cloned.1.call-update) | async-done | bytes 8388624 | tf_op jit(solution)/shard_map/psum | solution.py:593
  352.1 2.3 fusion.9
  354.4 3.0 add_convert_fusion.4
  357.4 1.5 collective-permute-start.8
  358.9 1.4 reduce_sum.189
  360.5 61.4 %all-reduce = (bf16[512]{0:T(512)(128)(2,1)S(1)}, bf16[512]{0:T(512)(128)(2,1)S(1)}, bf16[6,1024]{1,0:T(8,128)(2,1)S(1)}, bf16[2048]{0:T(1024)(128)(2,1)S(1)}) all-reduce(bf16[512]{0:T(512)(128)(2,1)S(1)} %reduce_sum.189, bf16[512]{0:T(512)(128)(2,1)S(1)} %reduce_sum.190, ...), channel_id=1, replica_groups=mesh['dp'=16,'mp'=2] {'dp'}, use_global_device_ids=true, to_apply=%region_14.15 | all-reduce | flops 9216 | bytes 36864 | tf_op jit(solution)/shard_map/psum | solution.py:620
  424.3 1.8 fusion.12
  426.1 2.1 fusion.14
  428.3 4.1 add_add_fusion
  432.4 4.5 convert_element_type.240
  436.8 4.4 convert_element_type.245
  441.3 27.8 %all-reduce.6.cloned.1.call-done = (bf16[1024,512]{1,0:T(8,128)(2,1)}, bf16[1024,512]{1,0:T(8,128)(2,1)}, bf16[1024,512]{1,0:T(8,128)(2,1)}, bf16[512,1024]{1,0:T(8,128)(2,1)}) async-done(((bf16[1024,512]{1,0:T(8,128)(2,1)}, bf16[1024,512]{1,0:T(8,128)(2,1)}, bf16[1024,512]{1,0:T(8,128)(2,1)}, bf16[512,1024]{1,0:T(8,128)(2,1)}), (bf16[1024,512]{1,0:T(8,128)(2,1)}, bf16[1024,512]{1,0:T(8,128)(2,1)}, ...) | async-done | bytes 4194320 | tf_op jit(solution)/shard_map/psum | solution.py:620
  469.0 3.0 convert_element_type.229
  472.0 2.8 convert_element_type.232
  474.9 1.6 convert_element_type.234
  476.5 1.6 convert_element_type.237
  (123 shorter events, 9.0 us)
Async XLA Ops:
  7.2 30.4 %copy-start = (bf16[1024,512]{1,0:T(8,128)(2,1)S(1)}, bf16[1024,512]{1,0:T(8,128)(2,1)}, u32[]{:S(2)}) copy-start(bf16[1024,512]{1,0:T(8,128)(2,1)} %param.23) | copy-start | bytes 3145732
  7.2 29.1 %copy-start.20 = (bf16[1024,512]{1,0:T(8,128)(2,1)S(1)}, bf16[1024,512]{1,0:T(8,128)(2,1)}, u32[]{:S(2)}) copy-start(bf16[1024,512]{1,0:T(8,128)(2,1)} %param.24) | copy-start | bytes 3145732
  7.2 344.9 %all-reduce.8.cloned.1.call-start = ((), (), s32[]{:S(2)}) async-start(), calls=%async_computation.1 | async-start | bytes 16777216 | tf_op jit(solution)/shard_map/psum | solution.py:593
  7.3 27.3 %collective-permute-start = (bf16[512,1024]{1,0:T(8,128)(2,1)}, bf16[512,1024]{1,0:T(8,128)(2,1)}, u32[]{:S(2)}, u32[]{:S(2)}) collective-permute-start(bf16[512,1024]{1,0:T(8,128)(2,1)} %param.18), channel_id=1, source_target_pairs={{0,1},{1,0},{2,3},{3,2},{4,5},{5,4},{6,7},{7,6},{8,9},{9,8},{10,11... | collective-permute-start | bytes 3145736 | tf_op jit(solution)/shard_map/ppermute | solution.py:427
  10.3 52.3 %collective-permute-start.2 = (bf16[512,1024]{1,0:T(8,128)(2,1)}, bf16[512,1024]{1,0:T(8,128)(2,1)}, u32[]{:S(2)}, u32[]{:S(2)}) collective-permute-start(bf16[512,1024]{1,0:T(8,128)(2,1)} %param.26), channel_id=1, source_target_pairs={{0,1},{1,0},{2,3},{3,2},{4,5},{5,4},{6,7},{7,6},{8,9},{9,8},{10,11... | collective-permute-start | bytes 3145736 | tf_op jit(solution)/shard_map/ppermute | solution.py:427
  36.3 2.6 copy-start.21
  36.3 2.6 copy-start.23
  37.6 2.9 copy-start.3
  37.6 1.6 copy-start.19
  39.2 1.3 copy-start.4
  40.4 17.8 %copy-start.6 = (bf16[1024,512]{1,0:T(8,128)(2,1)}, bf16[1024,512]{1,0:T(8,128)(2,1)S(1)}, u32[]{:S(2)}) copy-start(bf16[1024,512]{1,0:T(8,128)(2,1)S(1)} %add_convert_fusion.7.q_ref) | copy-start | bytes 3145732
  40.4 20.0 %copy-start.29 = (bf16[1024]{0:T(1024)(128)(2,1)S(1)}, bf16[1024]{0:T(1024)(128)(2,1)}, u32[]{:S(2)}) copy-start(bf16[1024]{0:T(1024)(128)(2,1)} %param.28) | copy-start | bytes 6148
  40.4 20.0 %copy-start.30 = (bf16[1024]{0:T(1024)(128)(2,1)S(1)}, bf16[1024]{0:T(1024)(128)(2,1)}, u32[]{:S(2)}) copy-start(bf16[1024]{0:T(1024)(128)(2,1)} %param.29) | copy-start | bytes 6148
  40.5 20.0 %copy-start.31 = (bf16[1024]{0:T(1024)(128)(2,1)S(1)}, bf16[1024]{0:T(1024)(128)(2,1)}, u32[]{:S(2)}) copy-start(bf16[1024]{0:T(1024)(128)(2,1)} %param.27) | copy-start | bytes 6148
  58.3 14.8 %copy-start.1 = (bf16[1024,512]{1,0:T(8,128)(2,1)}, bf16[1024,512]{1,0:T(8,128)(2,1)S(1)}, u32[]{:S(2)}) copy-start(bf16[1024,512]{1,0:T(8,128)(2,1)S(1)} %get-tuple-element.28.c_ref) | copy-start | bytes 3145732
  58.3 12.5 %collective-permute-start.1 = (bf16[512,512]{1,0:T(8,128)(2,1)S(1)}, bf16[512,512]{1,0:T(8,128)(2,1)}, u32[]{:S(2)}, u32[]{:S(2)}) collective-permute-start(bf16[512,512]{1,0:T(8,128)(2,1)S(1)} %constant_dynamic-slice_fusion), channel_id=1, source_target_pairs={{0,1},{1,0},{2,3},{3,2},{4,5},{5,4},{6,7},{7,6},{8,9},{9,8},{10,11... | collective-permute-start | bytes 1572872 | tf_op jit(solution)/shard_map/ppermute | solution.py:427
  60.5 10.3 %copy-start.18 = (bf16[512,1024]{1,0:T(8,128)(2,1)S(1)}, bf16[512,1024]{1,0:T(8,128)(2,1)}, u32[]{:S(2)}) copy-start(bf16[512,1024]{1,0:T(8,128)(2,1)} %param.18) | copy-start | bytes 3145732
  73.1 54.7 %copy-start.10 = (f32[512,1024]{1,0:T(8,128)}, f32[512,1024]{1,0:T(8,128)S(1)}, u32[]{:S(2)}) copy-start(f32[512,1024]{1,0:T(8,128)S(1)} %get-tuple-element.76) | copy-start | bytes 6291460
  73.1 2.3 copy-start.32
  73.1 2.3 copy-start.33
  73.1 2.3 copy-start.34
  73.1 2.3 copy-start.28
  73.1 23.4 %copy-start.36 = (bf16[1024,2048]{1,0:T(8,128)(2,1)S(1)}, bf16[1024,2048]{1,0:T(8,128)(2,1)}, u32[]{:S(2)}) copy-start(bf16[1024,2048]{1,0:T(8,128)(2,1)} %param.30) | copy-start | bytes 12582916
  73.9 22.6 %collective-permute-start.3 = (bf16[512,1024]{1,0:T(8,128)(2,1)S(1)}, bf16[512,1024]{1,0:T(8,128)(2,1)S(1)}, u32[]{:S(2)}, u32[]{:S(2)}) collective-permute-start(bf16[512,1024]{1,0:T(8,128)(2,1)S(1)} %fusion.5), channel_id=1, source_target_pairs={{0,1},{1,0},{2,3},{3,2},{4,5},{5,4},{6,7},{7,6},{8,9},{9,8},{10,11... | collective-permute-start | bytes 3145736 | tf_op jit(solution)/shard_map/ppermute | solution.py:427
  75.5 25.4 %copy-start.35 = (bf16[2048,1024]{1,0:T(8,128)(2,1)S(1)}, bf16[2048,1024]{1,0:T(8,128)(2,1)}, u32[]{:S(2)}) copy-start(bf16[2048,1024]{1,0:T(8,128)(2,1)} %param.32) | copy-start | bytes 12582916
  99.0 2.0 copy-start.38
  106.1 21.7 %collective-permute-start.4 = (bf16[512,1024]{1,0:T(8,128)(2,1)S(1)}, bf16[512,1024]{1,0:T(8,128)(2,1)S(1)}, u32[]{:S(2)}, u32[]{:S(2)}) collective-permute-start(bf16[512,1024]{1,0:T(8,128)(2,1)S(1)} %convolution_convert_fusion.3), channel_id=1, source_target_pairs={{0,1},{1,0},{2,3},{3,2},{4,5},{5,4},{6,7},{7,6},{8,9},{9,8},{10,11... | collective-permute-start | bytes 3145736 | tf_op jit(solution)/shard_map/ppermute | solution.py:427
  127.8 3.1 copy-start.17
  133.9 1.3 copy-start.13
  135.4 20.8 %collective-permute-start.5 = (bf16[512,1024]{1,0:T(8,128)(2,1)S(1)}, bf16[512,1024]{1,0:T(8,128)(2,1)S(1)}, u32[]{:S(2)}, u32[]{:S(2)}) collective-permute-start(bf16[512,1024]{1,0:T(8,128)(2,1)S(1)} %convert_element_type.210), channel_id=1, source_target_pairs={{0,1},{1,0},{2,3},{3,2},{4,5},{5,4},{6,7},{7,6},{8,9},{9,8},{10,11... | collective-permute-start | bytes 3145736 | tf_op jit(solution)/shard_map/ppermute | solution.py:427
  142.1 2.4 copy-start.37
  167.3 20.1 %collective-permute-start.6 = (bf16[512,1024]{1,0:T(8,128)(2,1)}, bf16[512,1024]{1,0:T(8,128)(2,1)}, u32[]{:S(2)}, u32[]{:S(2)}) collective-permute-start(bf16[512,1024]{1,0:T(8,128)(2,1)} %convolution_convert_fusion.2), channel_id=1, source_target_pairs={{0,1},{1,0},{2,3},{3,2},{4,5},{5,4},{6,7},{7,6},{8,9},{9,8},{10,11... | collective-permute-start | bytes 3145736 | tf_op jit(solution)/shard_map/ppermute | solution.py:427
  182.1 287.0 %all-reduce.6.cloned.1.call-start = ((), (), s32[]{:S(2)}) async-start(), calls=%async_computation | async-start | bytes 8388608 | tf_op jit(solution)/shard_map/psum | solution.py:620
  182.4 12.6 %copy-start.11 = (f32[512,1024]{1,0:T(8,128)S(1)}, f32[512,1024]{1,0:T(8,128)}, u32[]{:S(2)}) copy-start(f32[512,1024]{1,0:T(8,128)} %copy-done.10) | copy-start | bytes 6291460
  197.0 161.9 %collective-permute-start.10 = (f32[6,1024]{1,0:T(8,128)S(1)}, f32[6,1024]{1,0:T(8,128)S(1)}, u32[]{:S(2)}, u32[]{:S(2)}) collective-permute-start(f32[6,1024]{1,0:T(8,128)S(1)} %stack.27), channel_id=1, source_target_pairs={{0,1},{1,0},{2,3},{3,2},{4,5},{5,4},{6,7},{7,6},{8,9},{9,8},{10,11... | collective-permute-start | bytes 73736 | tf_op jit(solution)/shard_map/ppermute | solution.py:427
  198.2 7.9 %copy-start.27 = (bf16[512,1024]{1,0:T(8,128)(2,1)S(1)}, bf16[512,1024]{1,0:T(8,128)(2,1)}, u32[]{:S(2)}) copy-start(bf16[512,1024]{1,0:T(8,128)(2,1)} %param.26) | copy-start | bytes 3145732
  202.1 14.9 %collective-permute-start.7 = (bf16[512,512]{1,0:T(8,128)(2,1)S(1)}, bf16[512,512]{1,0:T(8,128)(2,1)S(1)}, u32[]{:S(2)}, u32[]{:S(2)}) collective-permute-start(bf16[512,512]{1,0:T(8,128)(2,1)S(1)} %convolution_convert_fusion.4), channel_id=1, source_target_pairs={{0,1},{1,0},{2,3},{3,2},{4,5},{5,4},{6,7},{7,6},{8,9},{9,8},{10,11... | collective-permute-start | bytes 1572872 | tf_op jit(solution)/shard_map/ppermute | solution.py:427
  204.8 13.3 %copy-start.5 = (bf16[1024,512]{1,0:T(8,128)(2,1)S(1)}, bf16[1024,512]{1,0:T(8,128)(2,1)}, u32[]{:S(2)}) copy-start(bf16[1024,512]{1,0:T(8,128)(2,1)} %copy-done.4) | copy-start | bytes 3145732
  204.8 13.3 %copy-start.7 = (bf16[1024,512]{1,0:T(8,128)(2,1)S(1)}, bf16[1024,512]{1,0:T(8,128)(2,1)}, u32[]{:S(2)}) copy-start(bf16[1024,512]{1,0:T(8,128)(2,1)} %copy-done.6) | copy-start | bytes 3145732
  204.9 49.8 %collective-permute-start.9 = (bf16[512,1024]{1,0:T(8,128)(2,1)S(1)}, bf16[512,1024]{1,0:T(8,128)(2,1)S(1)}, u32[]{:S(2)}, u32[]{:S(2)}) collective-permute-start(bf16[512,1024]{1,0:T(8,128)(2,1)S(1)} %convolution_convert_fusion.1), channel_id=1, source_target_pairs={{0,1},{1,0},{2,3},{3,2},{4,5},{5,4},{6,7},{7,6},{8,9},{9,8},{10,11... | collective-permute-start | bytes 3145736 | tf_op jit(solution)/shard_map/ppermute | solution.py:427
  217.1 28.7 %copy-start.22 = (bf16[512,1024]{1,0:T(8,128)(2,1)S(1)}, bf16[512,1024]{1,0:T(8,128)(2,1)}, u32[]{:S(2)}) copy-start(bf16[512,1024]{1,0:T(8,128)(2,1)} %copy-done.21) | copy-start | bytes 3145732
  217.1 28.7 %copy-start.24 = (bf16[512,1024]{1,0:T(8,128)(2,1)S(1)}, bf16[512,1024]{1,0:T(8,128)(2,1)}, u32[]{:S(2)}) copy-start(bf16[512,1024]{1,0:T(8,128)(2,1)} %copy-done.23) | copy-start | bytes 3145732
  245.7 2.3 copy-start.9
  245.8 4.4 copy-start.8
  252.4 2.3 copy-start.2
  352.1 2.3 copy-start.14
  357.4 70.9 %collective-permute-start.8 = (bf16[512,1024]{1,0:T(8,128)(2,1)}, bf16[512,1024]{1,0:T(8,128)(2,1)}, u32[]{:S(2)}, u32[]{:S(2)}) collective-permute-start(bf16[512,1024]{1,0:T(8,128)(2,1)} %add_convert_fusion.4), channel_id=1, source_target_pairs={{0,1},{1,0},{2,3},{3,2},{4,5},{5,4},{6,7},{7,6},{8,9},{9,8},{10,11... | collective-permute-start | bytes 3145736 | tf_op jit(solution)/shard_map/ppermute | solution.py:427
  422.0 6.3 %copy-start.12 = (f32[512,1024]{1,0:T(8,128)S(1)}, f32[512,1024]{1,0:T(8,128)}, u32[]{:S(2)}) copy-start(f32[512,1024]{1,0:T(8,128)} %get-tuple-element.60) | copy-start | bytes 6291460
  428.3 4.1 copy-start.16
  432.4 4.5 copy-start.15
  469.0 5.8 %copy-start.26 = (bf16[1024,512]{1,0:T(8,128)(2,1)S(1)}, bf16[1024,512]{1,0:T(8,128)(2,1)}, u32[]{:S(2)}) copy-start(bf16[1024,512]{1,0:T(8,128)(2,1)} %get-tuple-element.53) | copy-start | bytes 3145732
  469.0 7.4 %copy-start.25 = (bf16[512,1024]{1,0:T(8,128)(2,1)S(1)}, bf16[512,1024]{1,0:T(8,128)(2,1)}, u32[]{:S(2)}) copy-start(bf16[512,1024]{1,0:T(8,128)(2,1)} %get-tuple-element.54) | copy-start | bytes 3145732
Sparse Core Ops, SparseCore 0:
  182.2 169.8 all-reduce.7
  356.7 112.2 all-reduce.5

commit v2 on v0

--- a/solution.py
+++ b/solution.py
@@ -1,13 +1,176 @@
+import functools
 import jax
 import jax.numpy as jnp
 from jax import lax
+from jax.experimental import pallas as pl
+from jax.experimental.pallas import tpu as pltpu
 from jax.sharding import PartitionSpec as P
 
 HEAD = 64
+LANES = 128
 
 
 epsilon = 1e-05
 masked_score = -1000000000.0
+
+
+def work(flops):
+    return pl.CostEstimate(flops=flops, bytes_accessed=0, transcendentals=0)
+
+
+def dot_nn(left, right):
+    return lax.dot_general(left, right, (((1,), (0,)), ((), ())), preferred_element_type=jnp.float32)
+
+
+def dot_nt(left, right):
+    return lax.dot_general(left, right, (((1,), (1,)), ((), ())), preferred_element_type=jnp.float32)
+
+
+def dot_tn(left, right):
+    return lax.dot_general(left, right, (((0,), (0,)), ((), ())), preferred_element_type=jnp.float32)
+
+
+def forward_kernel(pairs, q_ref, k_ref, v_ref, row_ref, col_ref, ctx_ref, lse_ref, bias_ref):
+    bias_ref[...] = jnp.where(col_ref[...] == row_ref[...], 0.0, masked_score)
+    rows = q_ref.shape[0]
+    lane = lax.broadcasted_iota(jnp.int32, (rows, LANES), 1)
+    stats = jnp.zeros((rows, LANES), jnp.float32)
+    for pair in range(pairs):
+        cols = slice(pair * LANES, (pair + 1) * LANES)
+        q_pair = q_ref[:, cols] * jnp.bfloat16(HEAD ** (-0.5))
+        k_pair = k_ref[:, cols]
+        v_pair = v_ref[:, cols]
+        halves = []
+        for half in range(2):
+            keep = (lane >= HEAD) == (half == 1)
+            q_half = jnp.where(keep, q_pair, jnp.bfloat16(0))
+            scores = dot_nt(q_half, k_pair) + bias_ref[...]
+            row_max = jnp.max(scores, axis=-1, keepdims=True)
+            exponent = jnp.exp(scores - row_max)
+            row_sum = jnp.sum(exponent, axis=-1, keepdims=True)
+            blended = dot_nn(exponent.astype(jnp.bfloat16), v_pair)
+            halves.append(blended * (1.0 / row_sum))
+            stats = jnp.where(lane == 2 * pair + half, row_max + jnp.log(row_sum), stats)
+        ctx_ref[:, cols] = jnp.where(lane >= HEAD, halves[1], halves[0]).astype(ctx_ref.dtype)
+    lse_ref[...] = jnp.transpose(stats)[: lse_ref.shape[0], :]
+
+
+def attention_forward(queries, key_rows, values, row_segment, segment, block=256):
+    rows, width = queries.shape
+    length = key_rows.shape[0]
+    pairs = width // LANES
+    heads = width // HEAD
+    whole = lambda shape: pl.BlockSpec(shape, lambda i: (0, 0))
+    return pl.pallas_call(
+        functools.partial(forward_kernel, pairs),
+        grid=(rows // block,),
+        in_specs=[
+            pl.BlockSpec((block, width), lambda i: (i, 0)),
+            whole((length, width)),
+            whole((length, width)),
+            whole((1, length)),
+            pl.BlockSpec((block, 1), lambda i: (i, 0)),
+        ],
+        out_specs=[
+            pl.BlockSpec((block, width), lambda i: (i, 0)),
+            pl.BlockSpec((heads, block), lambda i: (0, i)),
+        ],
+        out_shape=[
+            jax.ShapeDtypeStruct((rows, width), jnp.bfloat16),
+            jax.ShapeDtypeStruct((heads, rows), jnp.float32),
+        ],
+        scratch_shapes=[pltpu.VMEM((block, length), jnp.float32)],
+        compiler_params=pltpu.CompilerParams(vmem_limit_bytes=48 * 1024 * 1024),
+        name="attention_forward",
+        cost_estimate=work(2 * 8 * rows * length * width),
+    )(queries, key_rows, values, segment.reshape(1, length), row_segment.reshape(rows, 1))
+
+
+def backward_kernel(
+    pairs, start, q_ref, k_ref, v_ref, g_ref, c_ref, lse_ref, row_ref, col_ref,
+    out_q_ref, out_k_ref, out_v_ref, bias_ref, dk_sum, dv_sum,
+):
+    step = pl.program_id(0)
+    bias_ref[...] = jnp.where(col_ref[...] == row_ref[...], 0.0, masked_score)
+    rows = q_ref.shape[0]
+    lane = lax.broadcasted_iota(jnp.int32, (rows, LANES), 1)
+    key_lane = lax.broadcasted_iota(jnp.int32, (k_ref.shape[0], LANES), 1)
+    inner = jnp.zeros((rows, LANES), jnp.float32)
+    for pair in range(pairs):
+        cols = slice(pair * LANES, (pair + 1) * LANES)
+        both = g_ref[:, cols].astype(jnp.float32) * c_ref[:, cols].astype(jnp.float32)
+        low = jnp.sum(jnp.where(lane < HEAD, both, 0.0), axis=-1, keepdims=True)
+        high = jnp.sum(jnp.where(lane < HEAD, 0.0, both), axis=-1, keepdims=True)
+        inner = jnp.where(lane == 2 * pair, low, jnp.where(lane == 2 * pair + 1, high, inner))
+    inner = jnp.transpose(inner)
+
+    @pl.when(step == 0)
+    def _():
+        dk_sum[...] = jnp.zeros_like(dk_sum)
+        dv_sum[...] = jnp.zeros_like(dv_sum)
+
+    for pair in range(pairs):
+        cols = slice(pair * LANES, (pair + 1) * LANES)
+        q_pair = q_ref[:, cols] * jnp.bfloat16(HEAD ** (-0.5))
+        k_pair = k_ref[:, cols]
+        v_pair = v_ref[:, cols]
+        g_pair = g_ref[:, cols]
+        dq = None
+        for half in range(2):
+            head = 2 * pair + half
+            keep = (lane >= HEAD) == (half == 1)
+            q_half = jnp.where(keep, q_pair, jnp.bfloat16(0))
+            g_half = jnp.where(keep, g_pair, jnp.bfloat16(0))
+            k_half = jnp.where((key_lane >= HEAD) == (half == 1), k_pair, jnp.bfloat16(0))
+            mass = lse_ref[start + head : start + head + 1, :]
+            probs = jnp.exp(dot_nt(k_pair, q_half) + bias_ref[...] - mass)
+            d_probs = dot_nt(v_pair, g_half)
+            d_scores = (probs * (d_probs - inner[head : head + 1, :])).astype(jnp.bfloat16)
+            dv_sum[:, cols] += dot_nn(probs.astype(jnp.bfloat16), g_half)
+            dk_sum[:, cols] += dot_nn(d_scores, q_half)
+            part = dot_tn(d_scores, k_half)
+            dq = part if dq is None else dq + part
+        out_q_ref[:, cols] = (dq * HEAD ** (-0.5)).astype(out_q_ref.dtype)
+
+    @pl.when(step == pl.num_programs(0) - 1)
+    def _():
+        out_k_ref[...] = dk_sum[...].astype(out_k_ref.dtype)
+        out_v_ref[...] = dv_sum[...].astype(out_v_ref.dtype)
+
+
+def attention_backward(
+    queries, key_rows, values, d_context, context, lse, segment, at, of, block=256
+):
+    rows, width = queries.shape
+    length = key_rows.shape[0]
+    width = width // of
+    pairs = width // LANES
+    heads = lse.shape[0]
+    part = pl.BlockSpec((block, width), lambda i: (i, at))
+    keys = pl.BlockSpec((length, width), lambda i: (0, at))
+    whole = pl.BlockSpec((length, width), lambda i: (0, 0))
+    return pl.pallas_call(
+        functools.partial(backward_kernel, pairs, at * (heads // of)),
+        grid=(rows // block,),
+        in_specs=[
+            part, keys, keys, part, part,
+            pl.BlockSpec((heads, block), lambda i: (0, i)),
+            pl.BlockSpec((1, block), lambda i: (0, i)),
+            pl.BlockSpec((length, 1), lambda i: (0, 0)),
+        ],
+        out_specs=[pl.BlockSpec((block, width), lambda i: (i, 0)), whole, whole],
+        out_shape=[jax.ShapeDtypeStruct((rows, width), jnp.bfloat16)]
+        + [jax.ShapeDtypeStruct((length, width), jnp.bfloat16)] * 2,
+        scratch_shapes=[
+            pltpu.VMEM((length, block), jnp.float32),
+            pltpu.VMEM((length, width), jnp.float32),
+            pltpu.VMEM((length, width), jnp.float32),
+        ],
+        compiler_params=pltpu.CompilerParams(vmem_limit_bytes=48 * 1024 * 1024),
+        name="attention_backward",
+        cost_estimate=work(2 * 4 * rows * length * width),
+    )(queries, key_rows, values, d_context, context, lse,
+      segment.reshape(1, rows), segment.reshape(length, 1))
 
 
 def matmul(left, right):
@@ -46,7 +209,7 @@
     return jnp.where(same[None], raw, masked_score)
 
 
-def body(
+def body_general(
     tokens,
     doc_lengths,
     cotangent,
@@ -270,6 +433,680 @@
     )
 
 
+def swap(rows):
+    return lax.ppermute(rows, "mp", [(0, 1), (1, 0)])
+
+
+def normal_parts(pre):
+    size = jnp.abs(pre) * (0.5**0.5)
+    t = 1.0 / (1.0 + 0.3275911 * size)
+    bell = jnp.exp(-size * size)
+    series = t * (
+        0.254829592
+        + t * (-0.284496736 + t * (1.421413741 + t * (-1.453152027 + t * 1.061405429)))
+    )
+    tail = 0.5 * series * bell
+    return jnp.where(pre < 0, tail, 1.0 - tail), pre * bell * 0.3989422804014327
+
+
+def gelu_parts(pre):
+    cumulative, slope = normal_parts(pre)
+    return (pre * cumulative).astype(jnp.bfloat16), (cumulative + slope).astype(jnp.bfloat16)
+
+
+def mean_of(rows):
+    return jnp.mean(rows, axis=-1, keepdims=True)
+
+
+def column_sums(rows):
+    return jnp.sum(rows, axis=0, keepdims=True)
+
+
+def pack_kernel(place_ref, up_ref, down_ref, out_ref):
+    rows = up_ref.shape[0]
+    half = down_ref.shape[2]
+    out_ref[:rows, :] = up_ref[...]
+    out_ref[rows:, :half] = down_ref[0]
+    out_ref[rows:, half:] = down_ref[1]
+
+
+def pack_weights(place, count, up_weight, down_weight):
+    depth, units = up_weight.shape
+    rows = depth // count
+    return pl.pallas_call(
+        pack_kernel,
+        grid_spec=pltpu.PrefetchScalarGridSpec(
+            num_scalar_prefetch=1,
+            grid=(1,),
+            in_specs=[
+                pl.BlockSpec((rows, units), lambda i, at: (at[0], 0)),
+                pl.BlockSpec((2, rows, depth), lambda i, at: (0, at[0], 0)),
+            ],
+            out_specs=pl.BlockSpec((2 * rows, units), lambda i, at: (0, 0)),
+        ),
+        out_shape=jax.ShapeDtypeStruct((2 * rows, units), up_weight.dtype),
+        name="pack_weights",
+        cost_estimate=work(rows * units * 4096),
+    )(place, up_weight, down_weight.reshape(2, units // 2, depth))
+
+
+BIG = 56 * 1024 * 1024
+
+
+def middle_kernel(own_ref, here_ref, w_own_ref, w_other_ref, bias_ref, tokens_ref, gain_ref,
+                  shift_ref, hidden_ref, low_ref, normal_ref, inverse_ref):
+    middle = (
+        dot_nn(own_ref[...], w_own_ref[...])
+        + dot_nn(here_ref[...], w_other_ref[...])
+        + bias_ref[...]
+        + tokens_ref[...].astype(jnp.float32)
+    )
+    center = middle - mean_of(middle)
+    inverse = lax.rsqrt(mean_of(center * center) + epsilon)
+    normal = center * inverse
+    hidden = normal * gain_ref[...] + shift_ref[...]
+    hidden_ref[...] = hidden
+    low_ref[...] = hidden.astype(jnp.bfloat16)
+    normal_ref[...] = normal
+    inverse_ref[...] = inverse
+
+
+def middle_norm(context_own, context_here, out_weight, out_other, bias, tokens, gain, shift,
+                block=256):
+    rows, depth = tokens.shape
+    heads = context_own.shape[1]
+    part = lambda width: pl.BlockSpec((block, width), lambda i: (i, 0))
+    whole = lambda shape: pl.BlockSpec(shape, lambda i: (0, 0))
+    return pl.pallas_call(
+        middle_kernel,
+        grid=(rows // block,),
+        in_specs=[part(heads), part(heads), whole((heads, depth)), whole((heads, depth)),
+                  whole((1, depth)), part(depth), whole((1, depth)), whole((1, depth))],
+        out_specs=[part(depth), part(depth), part(depth), part(1)],
+        out_shape=[
+            jax.ShapeDtypeStruct((rows, depth), jnp.float32),
+            jax.ShapeDtypeStruct((rows, depth), jnp.bfloat16),
+            jax.ShapeDtypeStruct((rows, depth), jnp.float32),
+            jax.ShapeDtypeStruct((rows, 1), jnp.float32),
+        ],
+        compiler_params=pltpu.CompilerParams(vmem_limit_bytes=BIG),
+        name="middle_norm",
+        cost_estimate=work(8 * rows * depth * heads),
+    )(context_own, context_here, out_weight, out_other, bias, tokens, gain, shift)
+
+
+UNITS = 512
+PIECE = 512
+STRIP = 64
+
+
+def gelu_block(h_ref, up, bias_ref, act_ref, slope_ref, pre_scr):
+    pre_scr[...] = dot_nn(h_ref[...], up)
+    bias = bias_ref[...]
+    for at in range(0, pre_scr.shape[0], STRIP):
+        rows = slice(at, at + STRIP)
+        act, slope = gelu_parts(pre_scr[rows, :] + bias)
+        act_ref[rows, :] = act
+        slope_ref[rows, :] = slope
+
+
+def forward_own_kernel(h_ref, up_ref, bias_ref, down_ref, act_ref, slope_ref, base_ref, pre_scr):
+    step = pl.program_id(0)
+
+    @pl.when(step == 0)
+    def _():
+        base_ref[...] = jnp.zeros_like(base_ref)
+
+    gelu_block(h_ref, up_ref[...], bias_ref, act_ref, slope_ref, pre_scr)
+    base_ref[...] += dot_nn(act_ref[...], down_ref[...])
+
+
+def forward_own(hidden, up_weight, up_bias, down_weight):
+    rows, depth = hidden.shape
+    units = up_weight.shape[1]
+    return pl.pallas_call(
+        forward_own_kernel,
+        grid=(units // UNITS,),
+        in_specs=[
+            pl.BlockSpec((rows, depth), lambda j: (0, 0)),
+            pl.BlockSpec((depth, UNITS), lambda j: (0, j)),
+            pl.BlockSpec((1, UNITS), lambda j: (0, j)),
+            pl.BlockSpec((UNITS, depth), lambda j: (j, 0)),
+        ],
+        out_specs=[
+            pl.BlockSpec((rows, UNITS), lambda j: (0, j)),
+            pl.BlockSpec((rows, UNITS), lambda j: (0, j)),
+            pl.BlockSpec((rows, depth), lambda j: (0, 0)),
+        ],
+        out_shape=[
+            jax.ShapeDtypeStruct((rows, units), jnp.bfloat16),
+            jax.ShapeDtypeStruct((rows, units), jnp.bfloat16),
+            jax.ShapeDtypeStruct((rows, depth), jnp.float32),
+        ],
+        scratch_shapes=[pltpu.VMEM((rows, UNITS), jnp.float32)],
+        compiler_params=pltpu.CompilerParams(vmem_limit_bytes=BIG),
+        name="forward_own",
+        cost_estimate=work(6 * rows * depth * units),
+    )(hidden, up_weight, up_bias, down_weight)
+
+
+def packed_specs(packs, at):
+    count, _, features, _ = packs.shape
+    groups = UNITS // features
+    split = count // groups
+    depth = count * features
+    up = pl.BlockSpec((count, 1, features, UNITS), lambda j: (0, 0, 0, at(j)))
+    down = pl.BlockSpec(
+        (groups, 1, features, depth), lambda j: (at(j) % split, 1, 0, at(j) // split)
+    )
+    return up, down
+
+
+def flat(ref):
+    count, _, features, width = ref.shape
+    return ref[...].reshape(count * features, width)
+
+
+def forward_other_kernel(h_ref, up_ref, bias_ref, down_ref, base_ref, hidden_ref, down_bias_ref,
+                         outer_ref, valid_ref, gain_ref, shift_ref,
+                         slope_ref, out_ref, d_ref, low_ref, sums_ref, total, act_scr, pre_scr):
+    step = pl.program_id(0)
+
+    @pl.when(step == 0)
+    def _():
+        total[...] = base_ref[...]
+
+    gelu_block(h_ref, flat(up_ref), bias_ref, act_scr, slope_ref, pre_scr)
+    total[...] += dot_nn(act_scr[...], flat(down_ref))
+
+    @pl.when(step == pl.num_programs(0) - 1)
+    def _():
+        gain = gain_ref[...]
+        for_gain = for_shift = for_bias = 0.0
+        for at in range(0, h_ref.shape[0], PIECE):
+            rows = slice(at, at + PIECE)
+            final = total[rows, :] + down_bias_ref[...] + hidden_ref[rows, :]
+            center = final - mean_of(final)
+            inverse = lax.rsqrt(mean_of(center * center) + epsilon)
+            normal = center * inverse
+            out_ref[rows, :] = (normal * gain + shift_ref[...]).astype(jnp.bfloat16)
+            upstream = outer_ref[rows, :].astype(jnp.float32) * valid_ref[rows, :]
+            scaled = upstream * gain
+            back = (scaled - mean_of(scaled) - normal * mean_of(scaled * normal)) * inverse
+            d_ref[rows, :] = back
+            low_ref[rows, :] = back.astype(jnp.bfloat16)
+            for_gain += column_sums(upstream * normal)
+            for_shift += column_sums(upstream)
+            for_bias += column_sums(back)
+        sums_ref[...] = jnp.zeros_like(sums_ref)
+        sums_ref[0:1, :] = for_gain
+        sums_ref[1:2, :] = for_shift
+        sums_ref[2:3, :] = for_bias
+
+
+def forward_other(hidden_low, packs, bias, base, hidden, down_bias, outer, valid, gain, shift):
+    rows, depth = hidden_low.shape
+    units = packs.shape[3]
+    up, down = packed_specs(packs, lambda j: j)
+    whole = lambda shape: pl.BlockSpec(shape, lambda j: (0, 0))
+    return pl.pallas_call(
+        forward_other_kernel,
+        grid=(units // UNITS,),
+        in_specs=[
+            whole((rows, depth)), up, pl.BlockSpec((1, UNITS), lambda j: (0, j)), down,
+            whole((rows, depth)), whole((rows, depth)), whole((1, depth)), whole((rows, depth)),
+            whole((rows, 1)), whole((1, depth)), whole((1, depth)),
+        ],
+        out_specs=[
+            pl.BlockSpec((rows, UNITS), lambda j: (0, j)),
+            whole((rows, depth)), whole((rows, depth)), whole((rows, depth)), whole((8, depth)),
+        ],
+        out_shape=[
+            jax.ShapeDtypeStruct((rows, units), jnp.bfloat16),
+            jax.ShapeDtypeStruct((rows, depth), jnp.bfloat16),
+            jax.ShapeDtypeStruct((rows, depth), jnp.float32),
+            jax.ShapeDtypeStruct((rows, depth), jnp.bfloat16),
+            jax.ShapeDtypeStruct((8, depth), jnp.float32),
+        ],
+        scratch_shapes=[
+            pltpu.VMEM((rows, depth), jnp.float32), pltpu.VMEM((rows, UNITS), jnp.bfloat16),
+            pltpu.VMEM((rows, UNITS), jnp.float32),
+        ],
+        compiler_params=pltpu.CompilerParams(vmem_limit_bytes=BIG),
+        name="forward_other",
+        cost_estimate=work(8 * rows * depth * units),
+    )(hidden_low, packs, bias, packs, base, hidden, down_bias, outer, valid, gain, shift)
+
+
+def backward_rows_kernel(half, f_ref, slope_own_ref, slope_other_ref, up_ref, down_ref,
+                         up_pack_ref, down_pack_ref, d_ref, normal_ref, inverse_ref, gain_ref,
+                         d_pre_ref, middle_ref, low_ref, sums_ref, total):
+    step = pl.program_id(0)
+
+    def block(up, down, slope_ref, keep):
+        for at in range(0, f_ref.shape[0], PIECE):
+            rows = slice(at, at + PIECE)
+            d_pre = (dot_nt(f_ref[rows, :], down) * slope_ref[rows, :]).astype(jnp.bfloat16)
+            if keep:
+                d_pre_ref[rows, :] = d_pre
+            total[rows, :] += dot_nt(d_pre, up)
+
+    @pl.when(step == 0)
+    def _():
+        total[...] = d_ref[...]
+
+    @pl.when(step < half)
+    def _():
+        block(up_ref[...], down_ref[...], slope_own_ref, True)
+
+    @pl.when(step >= half)
+    def _():
+        block(flat(up_pack_ref), flat(down_pack_ref), slope_other_ref, False)
+
+    @pl.when(step == pl.num_programs(0) - 1)
+    def _():
+        gain = gain_ref[...]
+        for_gain = for_shift = for_bias = 0.0
+        for at in range(0, f_ref.shape[0], PIECE):
+            rows = slice(at, at + PIECE)
+            upstream = total[rows, :]
+            normal = normal_ref[rows, :]
+            scaled = upstream * gain
+            back = (
+                scaled - mean_of(scaled) - normal * mean_of(scaled * normal)
+            ) * inverse_ref[rows, :]
+            middle_ref[rows, :] = back
+            low_ref[rows, :] = back.astype(jnp.bfloat16)
+            for_gain += column_sums(upstream * normal)
+            for_shift += column_sums(upstream)
+            for_bias += column_sums(back)
+        sums_ref[...] = jnp.zeros_like(sums_ref)
+        sums_ref[0:1, :] = for_gain
+        sums_ref[1:2, :] = for_shift
+        sums_ref[2:3, :] = for_bias
+
+
+def backward_rows(final_low, slope_own, slope_other, up_weight, down_weight, packs, d_final,
+                  normal, inverse, gain):
+    rows, depth = final_low.shape
+    units = up_weight.shape[1]
+    half = units // UNITS
+    own = lambda j: jnp.minimum(j, half - 1)
+    other = lambda j: jnp.maximum(j - half, 0)
+    up, down = packed_specs(packs, other)
+    whole = lambda shape: pl.BlockSpec(shape, lambda j: (0, 0))
+    return pl.pallas_call(
+        functools.partial(backward_rows_kernel, half),
+        grid=(2 * half,),
+        in_specs=[
+            whole((rows, depth)),
+            pl.BlockSpec((rows, UNITS), lambda j: (0, own(j))),
+            pl.BlockSpec((rows, UNITS), lambda j: (0, other(j))),
+            pl.BlockSpec((depth, UNITS), lambda j: (0, own(j))),
+            pl.BlockSpec((UNITS, depth), lambda j: (own(j), 0)),
+            up, down,
+            whole((rows, depth)), whole((rows, depth)), whole((rows, 1)), whole((1, depth)),
+        ],
+        out_specs=[
+            pl.BlockSpec((rows, UNITS), lambda j: (0, own(j))),
+            whole((rows, depth)), whole((rows, depth)), whole((8, depth)),
+        ],
+        out_shape=[
+            jax.ShapeDtypeStruct((rows, units), jnp.bfloat16),
+            jax.ShapeDtypeStruct((rows, depth), jnp.float32),
+            jax.ShapeDtypeStruct((rows, depth), jnp.bfloat16),
+            jax.ShapeDtypeStruct((8, depth), jnp.float32),
+        ],
+        scratch_shapes=[pltpu.VMEM((rows, depth), jnp.float32)],
+        compiler_params=pltpu.CompilerParams(vmem_limit_bytes=BIG),
+        name="backward_rows",
+        cost_estimate=work(10 * rows * depth * units),
+    )(final_low, slope_own, slope_other, up_weight, down_weight, packs, packs, d_final, normal,
+      inverse, gain)
+
+
+def down_grad_kernel(h_ref, up_ref, bias_ref, act_ref, f_own_ref, f_other_ref,
+                     slope_ref, grad_ref, act_scr, pre_scr):
+    gelu_block(h_ref, up_ref[...], bias_ref, act_scr, slope_ref, pre_scr)
+    grad_ref[...] = (
+        dot_tn(act_ref[...], f_own_ref[...]) + dot_tn(act_scr[...], f_other_ref[...])
+    ).astype(jnp.bfloat16)
+
+
+def down_grad(hidden_other, up_weight, up_bias, act_own, final_own, final_other):
+    rows, depth = hidden_other.shape
+    units = up_weight.shape[1]
+    whole = lambda shape: pl.BlockSpec(shape, lambda j: (0, 0))
+    return pl.pallas_call(
+        down_grad_kernel,
+        grid=(units // UNITS,),
+        in_specs=[
+            whole((rows, depth)),
+            pl.BlockSpec((depth, UNITS), lambda j: (0, j)),
+            pl.BlockSpec((1, UNITS), lambda j: (0, j)),
+            pl.BlockSpec((rows, UNITS), lambda j: (0, j)),
+            whole((rows, depth)), whole((rows, depth)),
+        ],
+        out_specs=[
+            pl.BlockSpec((rows, UNITS), lambda j: (0, j)),
+            pl.BlockSpec((UNITS, depth), lambda j: (j, 0)),
+        ],
+        out_shape=[
+            jax.ShapeDtypeStruct((rows, units), jnp.bfloat16),
+            jax.ShapeDtypeStruct((units, depth), jnp.bfloat16),
+        ],
+        scratch_shapes=[pltpu.VMEM((rows, UNITS), jnp.bfloat16), pltpu.VMEM((rows, UNITS), jnp.float32)],
+        compiler_params=pltpu.CompilerParams(vmem_limit_bytes=BIG),
+        name="down_grad",
+        cost_estimate=work(8 * rows * depth * units),
+    )(hidden_other, up_weight, up_bias, act_own, final_own, final_other)
+
+
+def up_grad_kernel(f_ref, down_ref, slope_ref, d_pre_ref, h_own_ref, h_other_ref,
+                   grad_ref, sums_ref, d_scr):
+    for at in range(0, f_ref.shape[0], PIECE):
+        rows = slice(at, at + PIECE)
+        d_scr[rows, :] = (
+            dot_nt(f_ref[rows, :], down_ref[...]) * slope_ref[rows, :]
+        ).astype(jnp.bfloat16)
+    grad_ref[...] = (
+        dot_tn(h_own_ref[...], d_pre_ref[...]) + dot_tn(h_other_ref[...], d_scr[...])
+    ).astype(jnp.bfloat16)
+    sums_ref[...] = column_sums(d_pre_ref[...].astype(jnp.float32)) + column_sums(
+        d_scr[...].astype(jnp.float32)
+    )
+
+
+def up_grad(final_other, down_weight, slope_other, d_pre_own, hidden_own, hidden_other):
+    rows, depth = hidden_own.shape
+    units = down_weight.shape[0]
+    whole = lambda shape: pl.BlockSpec(shape, lambda j: (0, 0))
+    part = pl.BlockSpec((rows, UNITS), lambda j: (0, j))
+    return pl.pallas_call(
+        up_grad_kernel,
+        grid=(units // UNITS,),
+        in_specs=[
+            whole((rows, depth)),
+            pl.BlockSpec((UNITS, depth), lambda j: (j, 0)),
+            part, part,
+            whole((rows, depth)), whole((rows, depth)),
+        ],
+        out_specs=[
+            pl.BlockSpec((depth, UNITS), lambda j: (0, j)),
+            pl.BlockSpec((1, UNITS), lambda j: (0, j)),
+        ],
+        out_shape=[
+            jax.ShapeDtypeStruct((depth, units), jnp.bfloat16),
+            jax.ShapeDtypeStruct((1, units), jnp.float32),
+        ],
+        scratch_shapes=[pltpu.VMEM((rows, UNITS), jnp.bfloat16)],
+        compiler_params=pltpu.CompilerParams(vmem_limit_bytes=BIG),
+        name="up_grad",
+        cost_estimate=work(6 * rows * depth * units),
+    )(final_other, down_weight, slope_other, d_pre_own, hidden_own, hidden_other)
+
+
+def after(value, *earlier):
+    return lax.optimization_barrier((value,) + earlier)[0]
+
+
+def join_halves(kept, arrived):
+    return (kept.astype(jnp.float32) + arrived.astype(jnp.float32)).astype(jnp.bfloat16)
+
+
+class Chain:
+    def __init__(self, item, swapped=False):
+        self.count = lax.axis_size("dp")
+        bits = list(range(self.count.bit_length() - 1))
+        if swapped:
+            bits[1:3] = bits[1:3][::-1]
+        self.steps = [("fold", bit) for bit in bits] + [("spread", bit) for bit in reversed(bits)]
+        self.held = item.astype(jnp.bfloat16)
+        self.flying = None
+
+    def end(self, *earlier):
+        if self.flying is not None:
+            kind, bit, kept, arrived = self.flying
+            self.flying = None
+            if earlier:
+                arrived = after(arrived, *earlier)
+            if kind == "fold":
+                self.held = join_halves(kept, arrived)
+            else:
+                low = (lax.axis_index("dp") >> bit) & 1 == 0
+                self.held = jnp.concatenate(
+                    [jnp.where(low, kept, arrived), jnp.where(low, arrived, kept)]
+                )
+
+    def push(self, *earlier):
+        self.end(*earlier)
+        if self.steps:
+            kind, bit = self.steps.pop(0)
+            perm = [(at, at ^ (1 << bit)) for at in range(self.count)]
+            kept = sent = self.held
+            if kind == "fold":
+                rows = self.held.shape[0] // 2
+                place = (lax.axis_index("dp") >> bit) & 1
+                kept = lax.dynamic_slice_in_dim(self.held, place * rows, rows, 0)
+                sent = lax.dynamic_slice_in_dim(self.held, (1 - place) * rows, rows, 0)
+            self.flying = kind, bit, kept, lax.ppermute(sent, "dp", perm)
+        return self
+
+    def gate(self, value):
+        return after(value, self.held)
+
+    def done(self):
+        return not self.steps and self.flying is None
+
+
+def sum_small(values):
+    count = lax.axis_size("dp")
+    for bit in range(count.bit_length() - 1):
+        perm = [(at, at ^ (1 << bit)) for at in range(count)]
+        values = values + lax.ppermute(values, "dp", perm)
+    return values
+
+
+def body_pair(
+    tokens,
+    doc_lengths,
+    cotangent,
+    query_weight,
+    query_bias,
+    key_weight,
+    value_weight,
+    value_bias,
+    out_weight,
+    out_bias,
+    first_gain,
+    first_shift,
+    up_weight,
+    up_bias,
+    down_weight,
+    down_bias,
+    second_gain,
+    second_shift,
+):
+    own_rows = tokens.shape[0]
+    length = 2 * own_rows
+    doc_count = doc_lengths.shape[1]
+    side = lax.axis_index("mp")
+    first = side == 0
+    f32 = jnp.float32
+    bf16 = jnp.bfloat16
+
+    def parts(rows, count=2):
+        size = rows.shape[0] // count
+        return [rows[at * size : (at + 1) * size] for at in range(count)]
+
+    row = lambda vector: vector.astype(f32).reshape(1, -1)
+    whole_segment = segment_ids(doc_lengths, length)[0]
+    segment_own = lax.dynamic_slice_in_dim(whole_segment, side * own_rows, own_rows, 0)
+    segment_other = lax.dynamic_slice_in_dim(whole_segment, (1 - side) * own_rows, own_rows, 0)
+    segment = jnp.concatenate([segment_own, segment_other])
+    valid = (segment_own < doc_count - 1).astype(f32)[:, None]
+
+    place = lax.axis_index("dp")
+    count = lax.axis_size("dp")
+    pack = swap(pack_weights(place.reshape(1), count, up_weight, down_weight))
+    packs = lax.all_gather(pack, "dp", axis=0)
+    packs = packs.reshape(count, 2, pack.shape[0] // 2, pack.shape[1])
+    bias_other = swap(up_bias)
+
+    tokens_other = swap(after(tokens, pack))
+    out_other = swap(after(out_weight, tokens_other))
+    project = lambda rows: (
+        (matmul(rows, query_weight) + query_bias).astype(bf16),
+        matmul(rows, key_weight).astype(bf16),
+        (matmul(rows, value_weight) + value_bias).astype(bf16),
+    )
+    query_own, key_own, value_own = project(tokens)
+    query_other, key_other, value_other = project(tokens_other)
+    key_rows = jnp.concatenate([key_own, key_other])
+    values = jnp.concatenate([value_own, value_other])
+    context_away, mass_other = attention_forward(
+        query_other, key_rows, values, segment_other, segment
+    )
+    context_here = swap(context_away)
+    context_own, mass_own = attention_forward(
+        query_own, key_rows, values, after(segment_own, context_away, out_other), segment
+    )
+
+    hidden, hidden_own, normal_first, inverse_first = middle_norm(
+        context_own, context_here, out_weight, out_other, row(out_bias), tokens,
+        row(first_gain), row(first_shift),
+    )
+    hidden_other = swap(hidden_own)
+
+    act_own, slope_own, base = forward_own(hidden_own, up_weight, row(up_bias), down_weight)
+    slope_local, output, d_final, final_own, second_sums = forward_other(
+        hidden_own, packs, row(bias_other), base, hidden, row(down_bias), cotangent, valid,
+        row(second_gain), row(second_shift),
+    )
+    final_other = swap(final_own)
+    d_pre_own, d_middle, middle_own, first_sums = backward_rows(
+        final_own, slope_own, slope_local, up_weight, down_weight, packs, d_final,
+        normal_first, inverse_first, row(first_gain),
+    )
+    d_context_away = matmul_nt(middle_own, out_other).astype(bf16)
+    d_context_other = swap(d_context_away)
+    d_context_own = matmul_nt(middle_own, out_weight).astype(bf16)
+
+    hidden_other = after(hidden_other, d_context_away, d_context_own)
+    final_other = after(final_other, d_context_away, d_context_own)
+    slope_other, grad_down_weight = down_grad(
+        hidden_other, up_weight, row(up_bias), act_own, final_own, final_other
+    )
+    down_sum = lax.psum(grad_down_weight, "dp")
+    queries = jnp.concatenate([query_own, query_other])
+    context = jnp.concatenate([context_own, context_away])
+    mass = jnp.concatenate([mass_own, mass_other], axis=1)
+    d_context_other = after(d_context_other, grad_down_weight)
+    d_context = jnp.concatenate([d_context_own, d_context_other])
+    gathered = jnp.concatenate([tokens, tokens_other])
+    weights = (query_weight, key_weight, value_weight)
+    width = query_weight.shape[1]
+    once = jnp.minimum(doc_lengths[0, 0], 1)
+
+    def entering(rows):
+        return functools.reduce(jnp.add, [matmul_nt(d, w) for d, w in zip(rows, weights)])
+
+    def run(part, start):
+        return lax.while_loop(
+            lambda carry: carry[0] < once,
+            lambda carry: (carry[0] + 1, part(carry[1])),
+            (0, start),
+        )[1]
+
+    left = []
+
+    def backward_part(carry):
+        d_context, final_other, d_middle = carry[0], carry[3], carry[5]
+        grad_up_weight, grad_up_bias = up_grad(
+            final_other, down_weight, slope_other, d_pre_own, hidden_own, hidden_other
+        )
+        up_sum = Chain(grad_up_weight).push()
+        partial_away = matmul_tn(after(context_here, grad_up_weight), middle_own).astype(bf16)
+        partial_here = swap(partial_away)
+        up_sum.push(partial_away)
+        rows, up_sum.held = lax.optimization_barrier((d_context, up_sum.held))
+        d_rows = attention_backward(
+            queries, key_rows, values, rows, context, mass, segment, 0, 1
+        )
+        up_sum.push(*d_rows)
+        grads = [matmul_tn(gathered, d).astype(bf16) for d in d_rows]
+        grad_out_weight = matmul_tn(after(context_own, d_rows[0]), middle_own)
+        grads.append((grad_out_weight + partial_here.astype(f32)).astype(bf16))
+        away = [parts(d)[1] for d in d_rows]
+        away[0] = after(away[0], *grads)
+        away = entering(away).astype(bf16)
+        back = swap(away)
+        own = [parts(d)[0] for d in d_rows]
+        own[0] = after(own[0], away)
+        own = entering(own) + d_middle
+        biases = [jnp.sum(d_rows[at], axis=0, dtype=f32) for at in (0, 2)]
+        up_sum.end(own)
+        left[:] = [up_sum.steps]
+        return (*grads, up_sum.held, own + back.astype(f32), *biases, grad_up_bias)
+
+    *grads, held, input_grad, query_bias_sum, value_bias_sum, grad_up_bias = run(
+        backward_part,
+        (
+            d_context, jnp.zeros_like(key_rows), jnp.zeros_like(values), final_other,
+            jnp.zeros((2 * up_weight.shape[0] // count, up_bias.size), bf16), d_middle,
+            jnp.zeros((width,), f32), jnp.zeros((width,), f32),
+            jnp.zeros((1, up_bias.size), f32),
+        ),
+    )
+    down_sum, *grads = lax.optimization_barrier((down_sum, *grads))
+    *qkv, out_sum = lax.psum(tuple(grads), "dp")
+
+    short = jnp.concatenate(
+        [
+            first_sums[:3].reshape(-1), second_sums[:3].reshape(-1), grad_up_bias.reshape(-1),
+            query_bias_sum, value_bias_sum,
+        ]
+    )
+    sizes = [tokens.shape[1]] * 6 + [up_bias.size, width, width]
+
+    def last_part(carry):
+        held, _, short = carry
+        up_sum = Chain(held)
+        up_sum.steps = list(left[0])
+        both = 6 * tokens.shape[1]
+        shared = short[:both] + swap(short[:both])
+        short = sum_small(jnp.concatenate([shared, short[both:]]))
+        while not up_sum.done():
+            up_sum.push()
+        return held, up_sum.held, short
+
+    held = after(held, grads[0])
+    _, up_total, small = run(last_part, (held, jnp.zeros(up_weight.shape, bf16), short))
+    pieces, at = [], 0
+    for size in sizes:
+        pieces.append(small[at : at + size])
+        at += size
+    return (
+        output,
+        input_grad,
+        qkv[0].astype(f32),
+        pieces[7],
+        qkv[1].astype(f32),
+        qkv[2].astype(f32),
+        pieces[8],
+        out_sum.astype(f32),
+        pieces[2],
+        pieces[0],
+        pieces[1],
+        up_total.astype(f32),
+        pieces[6],
+        after(down_sum, up_total).astype(f32),
+        pieces[5],
+        pieces[3],
+        pieces[4],
+    )
+
+
 def solution(mesh):
     in_specs = (
         P(("dp", "mp"), None),
@@ -310,4 +1147,7 @@
         P(),
         P(),
     )
+    dp, mp = mesh.shape["dp"], mesh.shape["mp"]
+    paired = mp == 2 and dp > 1 and dp & (dp - 1) == 0
+    body = body_pair if paired else body_general
     return jax.shard_map(body, mesh=mesh, in_specs=in_specs, out_specs=out_specs, check_vma=False)

time: 859 us -> 464 us (0.54)
  waiting for transfers between devices: 467 us -> 176 us
  matrix products: 174 us -> 33.3 us
  Pallas kernels: 0 us -> 127 us
  blocking collectives: 76.3 us -> 0 us
  other arithmetic: 72.4 us -> 47.9 us
  starting transfers between devices: 0.77 us -> 24.4 us
    ppermute x0 -> x23, waiting for transfers between devices: none -> 167 us  [the longest x8 127 us: push(): self.flying = (kind, bit, kept, lax.ppermute(sent, 'dp', perm))]
    reduce_scatter x4 -> x0, waiting for transfers between devices: 162 us -> none  [the longest x1 54.4 us: body(): lax.psum_scatter(matmul_nt(d_pre, up_weight), 'mp', scatter_dimension=0,...]
    psum x1 -> x2, waiting for transfers between devices: 169 us -> 9.02 us  [the longest x1 9.02 us: body_pair(): *qkv, out_sum = lax.psum(tuple(grads), 'dp')]
    all_gather x4 -> x1, waiting for transfers between devices: 135 us -> 0.02 us  [body_pair(): packs = lax.all_gather(pack, 'dp', axis=0)]
    pallas_call x0 -> x10, Pallas kernels: none -> 127 us  [the longest x1 27.2 us: attention_backward(): pl.pallas_call(functools.partial(backward_kernel, pairs, at * (heads // o...]
    psum x2 -> x0, blocking collectives: 76.3 us -> none  [the longest x1 41 us: body(): lax.psum((grad_out_bias, grad_first_gain, grad_first_shift, grad_down_bia...]
    dot_general x14 -> x0, matrix products: 75.7 us -> none  [the longest x4 29.3 us: score_block(): jnp.einsum('qhd,khd->hqk', q_block, key_rows, preferred_element_type=jnp....]
    dot_general x6, matrix products: 44 us -> 13.3 us  [matmul(): return jnp.dot(left, right, preferred_element_type=jnp.float32)]
  transfers between devices with their start and end apart: 9 -> 26, of which waited for: 8 -> 17; matrix products, arithmetic and copies ran while one was open for 4% -> 22% of each run, Pallas kernels for 0% -> 27%
where the time goes in v2:
time: 464 us; the launch traced here: 459 us
  waiting for transfers between devices  176 us (38%)
  Pallas kernels  127 us (27%)
  other arithmetic  47.9 us (10%)
  local copies, waits for them, and re-layouts  35.5 us (8%)
  matrix products  33.3 us (7%)
  starting transfers between devices  24.4 us (5%)
  between operations  14.5 us (3%)
    ppermute x8, waiting for transfers between devices, push(): self.flying = (kind, bit, kept, lax.ppermute(sent, 'dp', perm))  127 us
    ppermute x11, waiting for transfers between devices, swap(): return lax.ppermute(rows, 'mp', [(0, 1), (1, 0)])  29.5 us
    pallas_call x1, Pallas kernels, attention_backward(): pl.pallas_call(functools.partial(backward_kernel, pairs, at * (heads // o...  27.2 us
    pallas_call x1, Pallas kernels, backward_rows(): pl.pallas_call(functools.partial(backward_rows_kernel, half), grid=(2 * h...  19 us
    pallas_call x2, Pallas kernels, attention_forward(): pl.pallas_call(functools.partial(forward_kernel, pairs), grid=(rows // bl...  18.8 us
    pallas_call x1, Pallas kernels, forward_other(): pl.pallas_call(forward_other_kernel, grid=(units // UNITS,), in_specs=[wh...  17 us
    ppermute x11, starting transfers between devices, swap(): return lax.ppermute(rows, 'mp', [(0, 1), (1, 0)])  14.5 us
    pallas_call x1, Pallas kernels, down_grad(): pl.pallas_call(down_grad_kernel, grid=(units // UNITS,), in_specs=[whole(...  14.3 us
  transfers between devices with their start and end apart: 26, of which 17 were waited for; matrix products, arithmetic and copies ran while one was open for 22% of the time, Pallas kernels for 27%

profile of v2, /device:TPU:0, one launch (start us, length us, event | category | flops | bytes accessed | tf_op | source)
XLA Modules:
  0.0 459.0 jit_solution(1910684235288470931)
XLA Ops:
  7.3 1.9 pack_weights.1
  9.2 2.9 collective-permute-start.15
  12.2 12.1 %collective-permute-done.15 = bf16[128,2048]{1,0:T(8,128)(2,1)S(1)} collective-permute-done((bf16[128,2048]{1,0:T(8,128)(2,1)}, bf16[128,2048]{1,0:T(8,128)(2,1)S(1)}, u32[]{:S(2)}, u32[]{:S(2)}) %collective-permute-start.15) | collective-permute-done | bytes 524320 | tf_op jit(solution)/shard_map/ppermute | solution.py:437
  25.2 1.8 collective-permute-start.19
  27.8 1.9 convolution_convert_fusion.7
  29.7 2.0 fusion.11.q_ref
  31.8 2.8 fusion.12
  40.4 11.0 %collective-permute-done.16 = bf16[512,1024]{1,0:T(8,128)(2,1)} collective-permute-done((bf16[512,1024]{1,0:T(8,128)(2,1)}, bf16[512,1024]{1,0:T(8,128)(2,1)}, u32[]{:S(2)}, u32[]{:S(2)}) %collective-permute-start.16) | collective-permute-done | bytes 1048608 | tf_op jit(solution)/shard_map/ppermute | solution.py:437
  52.1 1.9 convolution_convert_fusion.6
  54.1 2.0 fusion.13
  56.3 2.7 fusion.14.q_ref
  59.0 8.7 %attention_forward.2 = (bf16[512,512]{1,0:T(8,128)(2,1)S(1)}, f32[8,512]{1,0:T(8,128)S(1)}) custom-call(bf16[512,512]{1,0:T(8,128)(2,1)S(1)} %fusion.14.q_ref, bf16[1024,512]{1,0:T(8,128)(2,1)S(1)} %get-tuple-element.744.k_ref, bf16[1024,512]{1,0:T(8,128)(2,1)S(1)} %get-tuple-element.745.v_ref, s32[1,1024]{1,0:T(1,128)S(1)} %bitcast.109, ...), custom_call_target="tpu_custom_call" | custom-call | flops 4294967296 | tf_op jit(solution)/shard_map/attention_forward/pallas_call | solution.py:64
  69.2 3.0 pad_maximum_fusion.5
  73.3 4.5 collective-permute-done.17.w_other_ref
  78.9 10.1 %attention_forward.3 = (bf16[512,512]{1,0:T(8,128)(2,1)S(1)}, f32[8,512]{1,0:T(8,128)S(1)}) custom-call(bf16[512,512]{1,0:T(8,128)(2,1)S(1)} %fusion.11.q_ref, bf16[1024,512]{1,0:T(8,128)(2,1)} %copy-done.21, bf16[1024,512]{1,0:T(8,128)(2,1)} %copy-done.22, s32[1,1024]{1,0:T(1,128)S(1)} %bitcast.110, s32[512,1]{1,0:T(8,128)S(1)} %copy.52.col_ref), custom_call_target="tpu_custom_call" | custom-call | flops 4294967296 | tf_op jit(solution)/shard_map/attention_forward/pallas_call | solution.py:64
  89.1 5.8 %middle_norm.1 = (f32[512,1024]{1,0:T(8,128)}, bf16[512,1024]{1,0:T(8,128)(2,1)}, f32[512,1024]{1,0:T(8,128)}, f32[512,1]{1,0:T(8,128)}) custom-call(bf16[512,512]{1,0:T(8,128)(2,1)S(1)} %get-tuple-element.749.own_ref, bf16[512,512]{1,0:T(8,128)(2,1)S(1)} %collective-permute-done.18.here_ref, bf16[512,1024]{1,0:T(8,128)(2,1)} %w_own_ref.1, ...), custom_call_target="tpu_custom_call" | custom-call | flops 2147483648 | tf_op jit(solution)/shard_map/middle_norm/pallas_call | solution.py:520
  96.7 11.6 %forward_own.1 = (bf16[512,2048]{1,0:T(8,128)(2,1)}, bf16[512,2048]{1,0:T(8,128)(2,1)}, f32[512,1024]{1,0:T(8,128)}) custom-call(bf16[512,1024]{1,0:T(8,128)(2,1)} %get-tuple-element.738.h_ref, bf16[1024,2048]{1,0:T(8,128)(2,1)} %up_ref.7, f32[1,2048]{1,0:T(1,128)} %bitcast.117, bf16[2048,1024]{1,0:T(8,128)(2,1)S(1)} %copy-done.14), custom_call_target="tpu_custom_call" | custom-call | flops 6442450944 | tf_op jit(solution)/shard_map/forward_own/pallas_call | solution.py:567
  108.3 17.0 %forward_other.1 = (bf16[512,2048]{1,0:T(8,128)(2,1)}, bf16[512,1024]{1,0:T(8,128)(2,1)}, f32[512,1024]{1,0:T(8,128)}, bf16[512,1024]{1,0:T(8,128)(2,1)}, f32[8,1024]{1,0:T(8,128)}) custom-call(bf16[512,1024]{1,0:T(8,128)(2,1)} %get-tuple-element.738.h_ref, bf16[16,2,64,2048]{3,2,1,0:T(8,128)(2,1)} %bitcast.128, f32[1,2048]{1,0:T(1,128)} %bitcast.119, ...), custom_call_target="tpu_custom_call" | custom-call | flops 8589934592 | tf_op jit(solution)/shard_map/forward_other/pallas_call | solution.py:652
  126.8 19.0 %backward_rows.1 = (bf16[512,2048]{1,0:T(8,128)(2,1)}, f32[512,1024]{1,0:T(8,128)}, bf16[512,1024]{1,0:T(8,128)(2,1)}, f32[8,1024]{1,0:T(8,128)}) custom-call(bf16[512,1024]{1,0:T(8,128)(2,1)} %get-tuple-element.252.f_ref.f_own_ref, bf16[512,2048]{1,0:T(8,128)(2,1)} %get-tuple-element.253.slope_own_ref, ...), custom_call_target="tpu_custom_call" | custom-call | flops 10737418240 | tf_op jit(solution)/shard_map/backward_rows/pallas_call | solution.py:738
  145.8 2.9 convolution_convert_fusion.4
  149.3 1.5 convolution_convert_fusion.5
  152.1 14.3 %down_grad.1 = (bf16[512,2048]{1,0:T(8,128)(2,1)}, bf16[2048,1024]{1,0:T(8,128)(2,1)}) custom-call(bf16[512,1024]{1,0:T(8,128)(2,1)} %collective-permute-done.21.h_ref, bf16[1024,2048]{1,0:T(8,128)(2,1)} %up_ref.7, f32[1,2048]{1,0:T(1,128)} %bitcast.118, bf16[512,2048]{1,0:T(8,128)(2,1)} %get-tuple-element.260.act_ref, ...), custom_call_target="tpu_custom_call" | custom-call | flops 8589934592 | tf_op jit(solution)/shard_map/down_grad/pallas_call | solution.py:780
  174.9 116.7 %while.38 = (s32[]{:T(128)}, bf16[1024,512]{0,1:T(8,128)(2,1)}, bf16[1024,512]{0,1:T(8,128)(2,1)}, bf16[1024,512]{0,1:T(8,128)(2,1)}, bf16[512,1024]{1,0:T(8,128...) while((s32[]{:T(128)}, bf16[1024,512]{0,1:T(8,128)(2,1)}, ...), condition=%wide.region_5.6_spmd, body=%wide.region_2.0_spmd.sunk | while | flops 18270912512 | bytes 153629936 | solution.py:1015
  175.1 11.4 %up_grad.1 = (bf16[1024,2048]{1,0:T(8,128)(2,1)}, f32[1,2048]{1,0:T(1,128)}) custom-call(bf16[512,1024]{1,0:T(8,128)(2,1)S(1)} %get-tuple-element.766.f_ref, bf16[2048,1024]{1,0:T(8,128)(2,1)} %get-tuple-element.811.down_ref, bf16[512,2048]{1,0:T(8,128)(2,1)} %get-tuple-element.812.slope_ref, bf16[512,2048]{1,0:T(8,128)(2,1)} %get-tuple-element.813.d_pre_ref, ...), custom_call_target="tpu_custom_call" | custom-call | flops 6442450944 | tf_op jit(solution)/shard_map/while/body/up_grad/pallas_call | solution.py:825
  186.5 3.3 constant_dynamic-slice_fusion.8
  189.9 1.8 convolution_convert_fusion.9
  194.4 4.5 add_convert_fusion.12
  198.9 1.5 copy.60.g_ref
  200.4 27.2 %attention_backward.1 = (bf16[1024,512]{1,0:T(8,128)(2,1)S(1)}, bf16[1024,512]{1,0:T(8,128)(2,1)S(1)}, bf16[1024,512]{1,0:T(8,128)(2,1)S(1)}) custom-call(bf16[1024,512]{1,0:T(8,128)(2,1)} %get-tuple-element.819.q_ref, bf16[1024,512]{1,0:T(8,128)(2,1)} %get-tuple-element.820.k_ref, bf16[1024,512]{1,0:T(8,128)(2,1)} %get-tuple-element.821.v_ref, ...), custom_call_target="tpu_custom_call" | custom-call | flops 4294967296 | tf_op jit(solution)/shard_map/while/body/attention_backward/pallas_call | solution.py:152
  227.7 1.5 copy-done
  229.3 2.2 fusion.105
  231.6 1.6 collective-permute-start.2
  234.7 2.2 fusion.106
  236.9 2.2 fusion.107
  239.2 2.0 add_convert_fusion.13
  242.0 1.6 collective-permute-start.4
  245.9 18.7 %collective-permute-done.2 = bf16[256,2048]{1,0:T(8,128)(2,1)S(1)} collective-permute-done((bf16[256,2048]{1,0:T(8,128)(2,1)S(1)}, bf16[256,2048]{1,0:T(8,128)(2,1)S(1)}, u32[]{:S(2)}, u32[]{:S(2)}) %collective-permute-start.2) | collective-permute-done | bytes 1048608 | tf_op jit(solution)/shard_map/while/body/ppermute | solution.py:892
  265.1 1.5 collective-permute-start.3
  268.3 22.2 %collective-permute-done.3 = bf16[128,2048]{1,0:T(8,128)(2,1)S(1)} collective-permute-done((bf16[128,2048]{1,0:T(8,128)(2,1)S(1)}, bf16[128,2048]{1,0:T(8,128)(2,1)S(1)}, u32[]{:S(2)}, u32[]{:S(2)}) %collective-permute-start.3) | collective-permute-done | bytes 524320 | tf_op jit(solution)/shard_map/while/body/ppermute | solution.py:892
  295.6 2.4 copy.55
  300.7 2.5 broadcast_in_dim.8
  303.2 117.1 %while.39 = (s32[]{:T(128)}, bf16[1024,2048]{1,0:T(8,128)(2,1)}, f32[9216]{0:T(1024)}, s32[]{:T(128)}, bf16[128,2048]{1,0:T(8,128)(2,1)S(1)}, /*index=5*/s32[]{:...) while((s32[]{:T(128)}, bf16[1024,2048]{1,0:T(8,128)(2,1)}, ...), condition=%wide.region_9.10_spmd, body=%wide.region_8.9_spmd.sunk | while | flops 27586584 | bytes 52994888 | solution.py:1015
  303.2 2.6 collective-permute-start.5
  305.8 16.3 %collective-permute-done.5 = bf16[64,2048]{1,0:T(8,128)(2,1)S(1)} collective-permute-done((bf16[64,2048]{1,0:T(8,128)(2,1)S(1)}, bf16[64,2048]{1,0:T(8,128)(2,1)S(1)}, u32[]{:S(2)}, u32[]{:S(2)}) %collective-permute-start.5) | collective-permute-done | bytes 262176 | tf_op jit(solution)/shard_map/while/body/ppermute | solution.py:892
  322.3 19.2 %collective-permute-done.6 = bf16[64,2048]{1,0:T(8,128)(2,1)S(1)} collective-permute-done((bf16[64,2048]{1,0:T(8,128)(2,1)S(1)}, bf16[64,2048]{1,0:T(8,128)(2,1)S(1)}, u32[]{:S(2)}, u32[]{:S(2)}) %collective-permute-start.6) | collective-permute-done | bytes 262176 | tf_op jit(solution)/shard_map/while/body/ppermute | solution.py:892
  341.6 22.4 %collective-permute-done.7 = bf16[128,2048]{1,0:T(8,128)(2,1)S(1)} collective-permute-done((bf16[128,2048]{1,0:T(8,128)(2,1)S(1)}, bf16[128,2048]{1,0:T(8,128)(2,1)S(1)}, u32[]{:S(2)}, u32[]{:S(2)}) %collective-permute-start.7) | collective-permute-done | bytes 524320 | tf_op jit(solution)/shard_map/while/body/ppermute | solution.py:892
  364.4 26.9 %collective-permute-done.8 = bf16[256,2048]{1,0:T(8,128)(2,1)} collective-permute-done((bf16[256,2048]{1,0:T(8,128)(2,1)S(1)}, bf16[256,2048]{1,0:T(8,128)(2,1)}, u32[]{:S(2)}, u32[]{:S(2)}) %collective-permute-start.8) | collective-permute-done | bytes 1048608 | tf_op jit(solution)/shard_map/while/body/ppermute | solution.py:892
  391.3 1.7 broadcast_select_fusion.14
  393.0 1.5 pad_maximum_fusion.19
  395.3 1.6 collective-permute-start.10
  397.6 1.5 collective-permute-done.10
  402.0 3.1 collective-permute-done.12
  405.1 3.9 collective-permute-done.13
  409.1 3.1 collective-permute-start.14
  412.1 1.9 collective-permute-done.14
  414.7 3.0 broadcast_select_fusion.15
  417.7 2.6 pad_maximum_fusion.20
  420.3 6.8 %convert_element_type.170 = f32[1024,2048]{1,0:T(8,128)} convert(bf16[1024,2048]{1,0:T(8,128)(2,1)} %get-tuple-element.934) | non-fusion elementwise | flops 2097152 | bytes 12582912 | tf_op jit(solution)/shard_map/convert_element_type | solution.py:1101
  428.4 4.4 convert_element_type.171
  435.5 9.0 %all-reduce.6.cloned.1.call-done = (bf16[1024,512]{1,0:T(8,128)(2,1)}, bf16[1024,512]{1,0:T(8,128)(2,1)}, bf16[1024,512]{1,0:T(8,128)(2,1)}, bf16[512,1024]{1,0:T(8,128)(2,1)}) async-done(((bf16[1024,512]{1,0:T(8,128)(2,1)}, bf16[1024,512]{1,0:T(8,128)(2,1)}, bf16[1024,512]{1,0:T(8,128)(2,1)}, bf16[512,1024]{1,0:T(8,128)(2,1)}), (bf16[1024,512]{1,0:T(8,128)(2,1)}, bf16[1024,512]{1,0:T(8,128)(2,1)}, ...) | async-done | bytes 4194320 | tf_op jit(solution)/shard_map/psum | solution.py:1062
  444.5 2.9 convert_element_type.166
  447.5 1.6 convert_element_type.167
  449.1 1.6 convert_element_type.168
  450.7 1.6 convert_element_type.169
  (207 shorter events, 52.3 us)
Async XLA Ops:
  7.2 101.1 %all-gather.3.cloned.1.call-start = ((), (), s32[]{:S(2)}) async-start(), calls=%async_computation.1 | async-start | bytes 8912896 | tf_op jit(solution)/shard_map/all_gather | solution.py:952
  7.2 17.9 %copy-start.34 = (bf16[2048]{0:T(1024)(128)(2,1)S(1)}, bf16[2048]{0:T(1024)(128)(2,1)}, u32[]{:S(2)}) copy-start(bf16[2048]{0:T(1024)(128)(2,1)} %param.35) | copy-start | bytes 12292
  7.3 19.8 %copy-start.41 = (bf16[512]{0:T(512)(128)(2,1)S(1)}, bf16[512]{0:T(512)(128)(2,1)}, u32[]{:S(2)}) copy-start(bf16[512]{0:T(512)(128)(2,1)} %param.26) | copy-start | bytes 3076
  7.3 19.7 %copy-start.42 = (bf16[512]{0:T(512)(128)(2,1)S(1)}, bf16[512]{0:T(512)(128)(2,1)}, u32[]{:S(2)}) copy-start(bf16[512]{0:T(512)(128)(2,1)} %param.29) | copy-start | bytes 3076
  7.3 19.7 %copy-start.48 = (s32[1,6]{1,0:T(1,128)S(1)}, s32[1,6]{1,0:T(1,128)}, u32[]{:S(2)}) copy-start(s32[1,6]{1,0:T(1,128)} %param.23) | copy-start | bytes 76
  7.3 20.5 %copy-start.2 = (bf16[1024,512]{1,0:T(8,128)(2,1)S(1)}, bf16[1024,512]{1,0:T(8,128)(2,1)}, u32[]{:S(2)}) copy-start(bf16[1024,512]{1,0:T(8,128)(2,1)} %param.27) | copy-start | bytes 3145732
  9.2 20.5 %copy-start.4 = (bf16[1024,512]{1,0:T(8,128)(2,1)S(1)}, bf16[1024,512]{1,0:T(8,128)(2,1)}, u32[]{:S(2)}) copy-start(bf16[1024,512]{1,0:T(8,128)(2,1)} %param.25) | copy-start | bytes 3145732
  9.2 15.1 %collective-permute-start.15 = (bf16[128,2048]{1,0:T(8,128)(2,1)}, bf16[128,2048]{1,0:T(8,128)(2,1)S(1)}, u32[]{:S(2)}, u32[]{:S(2)}) collective-permute-start(bf16[128,2048]{1,0:T(8,128)(2,1)} %pack_weights.1), channel_id=1, source_target_pairs={{0,1},{1,0},{2,3},{3,2},{4,5},{5,4},{6,7},{7,6},{8,9},{9,8},{10,11... | collective-permute-start | bytes 1572872 | tf_op jit(solution)/shard_map/ppermute | solution.py:437
  25.1 270.5 %all-reduce.4.cloned.1.call-start = ((), (), s32[]{:S(2)}) async-start(), calls=%async_computation | async-start | bytes 8388608 | tf_op jit(solution)/shard_map/psum | solution.py:1000
  25.2 14.6 %collective-permute-start.19 = (bf16[2048]{0:T(1024)(128)(2,1)S(1)}, bf16[2048]{0:T(1024)(128)(2,1)S(1)}, u32[]{:S(2)}, u32[]{:S(2)}) collective-permute-start(bf16[2048]{0:T(1024)(128)(2,1)S(1)} %copy-done.34), channel_id=1, source_target_pairs={{0,1},{1,0},{2,3},{3,2},{4,5},{5,4},{6,7},{7,6},{8,9},{9,8},{10,11... | collective-permute-start | bytes 12296 | tf_op jit(solution)/shard_map/ppermute | solution.py:437
  27.4 24.1 %collective-permute-start.16 = (bf16[512,1024]{1,0:T(8,128)(2,1)}, bf16[512,1024]{1,0:T(8,128)(2,1)}, u32[]{:S(2)}, u32[]{:S(2)}) collective-permute-start(bf16[512,1024]{1,0:T(8,128)(2,1)} %tokens_ref.1), channel_id=1, source_target_pairs={{0,1},{1,0},{2,3},{3,2},{4,5},{5,4},{6,7},{7,6},{8,9},{9,8},{10,11... | collective-permute-start | bytes 3145736 | tf_op jit(solution)/shard_map/ppermute | solution.py:437
  31.8 3.6 copy-start.35
  31.8 4.2 copy-start.36
  31.8 4.8 %copy-start.37 = (bf16[1024]{0:T(1024)(128)(2,1)S(1)}, bf16[1024]{0:T(1024)(128)(2,1)}, u32[]{:S(2)}) copy-start(bf16[1024]{0:T(1024)(128)(2,1)} %param.33) | copy-start | bytes 6148
  31.8 5.3 %copy-start.38 = (bf16[1024]{0:T(1024)(128)(2,1)S(1)}, bf16[1024]{0:T(1024)(128)(2,1)}, u32[]{:S(2)}) copy-start(bf16[1024]{0:T(1024)(128)(2,1)} %param.37) | copy-start | bytes 6148
  31.8 6.8 %copy-start.39 = (bf16[1024]{0:T(1024)(128)(2,1)S(1)}, bf16[1024]{0:T(1024)(128)(2,1)}, u32[]{:S(2)}) copy-start(bf16[1024]{0:T(1024)(128)(2,1)} %param.38) | copy-start | bytes 6148
  31.8 7.4 %copy-start.40 = (bf16[1024]{0:T(1024)(128)(2,1)S(1)}, bf16[1024]{0:T(1024)(128)(2,1)}, u32[]{:S(2)}) copy-start(bf16[1024]{0:T(1024)(128)(2,1)} %param.39) | copy-start | bytes 6148
  38.6 15.5 %copy-start.7 = (bf16[1024,512]{1,0:T(8,128)(2,1)S(1)}, bf16[1024,512]{1,0:T(8,128)(2,1)}, u32[]{:S(2)}) copy-start(bf16[1024,512]{1,0:T(8,128)(2,1)} %param.28) | copy-start | bytes 3145732
  51.5 26.3 %collective-permute-start.17 = (bf16[512,1024]{1,0:T(8,128)(2,1)}, bf16[512,1024]{1,0:T(8,128)(2,1)S(1)}, u32[]{:S(2)}, u32[]{:S(2)}) collective-permute-start(bf16[512,1024]{1,0:T(8,128)(2,1)} %w_own_ref.1), channel_id=1, source_target_pairs={{0,1},{1,0},{2,3},{3,2},{4,5},{5,4},{6,7},{7,6},{8,9},{9,8},{10,11... | collective-permute-start | bytes 3145736 | tf_op jit(solution)/shard_map/ppermute | solution.py:437
  56.2 11.4 %copy-start.21 = (bf16[1024,512]{1,0:T(8,128)(2,1)}, bf16[1024,512]{1,0:T(8,128)(2,1)S(1)}, u32[]{:S(2)}) copy-start(bf16[1024,512]{1,0:T(8,128)(2,1)S(1)} %get-tuple-element.744.k_ref) | copy-start | bytes 3145732
  56.3 11.4 %copy-start.22 = (bf16[1024,512]{1,0:T(8,128)(2,1)}, bf16[1024,512]{1,0:T(8,128)(2,1)S(1)}, u32[]{:S(2)}) copy-start(bf16[1024,512]{1,0:T(8,128)(2,1)S(1)} %get-tuple-element.745.v_ref) | copy-start | bytes 3145732
  67.7 21.3 %collective-permute-start.18 = (bf16[512,512]{1,0:T(8,128)(2,1)S(1)}, bf16[512,512]{1,0:T(8,128)(2,1)S(1)}, u32[]{:S(2)}, u32[]{:S(2)}) collective-permute-start(bf16[512,512]{1,0:T(8,128)(2,1)S(1)} %get-tuple-element.244), channel_id=1, source_target_pairs={{0,1},{1,0},{2,3},{3,2},{4,5},{5,4},{6,7},{7,6},{8,9},{9,8},{10,11... | collective-permute-start | bytes 1572872 | tf_op jit(solution)/shard_map/ppermute | solution.py:437
  89.0 6.6 %copy-start.27 = (bf16[512,512]{1,0:T(8,128)(2,1)}, bf16[512,512]{1,0:T(8,128)(2,1)S(1)}, u32[]{:S(2)}) copy-start(bf16[512,512]{1,0:T(8,128)(2,1)S(1)} %get-tuple-element.749.own_ref) | copy-start | bytes 1572868
  89.1 5.8 %copy-start.46 = (bf16[512,512]{1,0:T(8,128)(2,1)}, bf16[512,512]{1,0:T(8,128)(2,1)S(1)}, u32[]{:S(2)}) copy-start(bf16[512,512]{1,0:T(8,128)(2,1)S(1)} %collective-permute-done.18.here_ref) | copy-start | bytes 1572868
  89.1 7.6 %copy-start.14 = (bf16[2048,1024]{1,0:T(8,128)(2,1)S(1)}, bf16[2048,1024]{1,0:T(8,128)(2,1)}, u32[]{:S(2)}) copy-start(bf16[2048,1024]{1,0:T(8,128)(2,1)} %down_ref.3) | copy-start | bytes 12582916
  94.9 56.0 %collective-permute-start.21 = (bf16[512,1024]{1,0:T(8,128)(2,1)}, bf16[512,1024]{1,0:T(8,128)(2,1)}, u32[]{:S(2)}, u32[]{:S(2)}) collective-permute-start(bf16[512,1024]{1,0:T(8,128)(2,1)} %get-tuple-element.738.h_ref), channel_id=1, source_target_pairs={{0,1},{1,0},{2,3},{3,2},{4,5},{5,4},{6,7},{7,6},{8,9},{9,8},{10,11... | collective-permute-start | bytes 3145736 | tf_op jit(solution)/shard_map/ppermute | solution.py:437
  108.3 18.5 %copy-start.15 = (bf16[2048,1024]{1,0:T(8,128)(2,1)S(1)}, bf16[2048,1024]{1,0:T(8,128)(2,1)}, u32[]{:S(2)}) copy-start(bf16[2048,1024]{1,0:T(8,128)(2,1)} %down_ref.3) | copy-start | bytes 12582916
  125.3 26.8 %collective-permute-start.22 = (bf16[512,1024]{1,0:T(8,128)(2,1)}, bf16[512,1024]{1,0:T(8,128)(2,1)S(1)}, u32[]{:S(2)}, u32[]{:S(2)}) collective-permute-start(bf16[512,1024]{1,0:T(8,128)(2,1)} %get-tuple-element.252.f_ref.f_own_ref), channel_id=1, source_target_pairs={{0,1},{1,0},{2,3},{3,2},{4,5},{5,4},{6,7},{7,6},{8,9},{9,8},{10,11... | collective-permute-start | bytes 3145736 | tf_op jit(solution)/shard_map/ppermute | solution.py:437
  126.8 19.0 %copy-start.45 = (bf16[512,1024]{1,0:T(8,128)(2,1)S(1)}, bf16[512,1024]{1,0:T(8,128)(2,1)}, u32[]{:S(2)}) copy-start(bf16[512,1024]{1,0:T(8,128)(2,1)} %copy-done.44) | copy-start | bytes 3145732
  145.8 3.6 copy-start.43
  145.8 3.6 copy-start.49
  148.7 17.7 %collective-permute-start.20 = (bf16[512,512]{1,0:T(8,128)(2,1)}, bf16[512,512]{1,0:T(8,128)(2,1)S(1)}, u32[]{:S(2)}, u32[]{:S(2)}) collective-permute-start(bf16[512,512]{1,0:T(8,128)(2,1)} %convolution_convert_fusion.4), channel_id=1, source_target_pairs={{0,1},{1,0},{2,3},{3,2},{4,5},{5,4},{6,7},{7,6},{8,9},{9,8},{10,11... | collective-permute-start | bytes 1572872 | tf_op jit(solution)/shard_map/ppermute | solution.py:437
  152.1 14.3 %copy-start.23 = (bf16[512,1024]{1,0:T(8,128)(2,1)}, bf16[512,1024]{1,0:T(8,128)(2,1)S(1)}, u32[]{:S(2)}) copy-start(bf16[512,1024]{1,0:T(8,128)(2,1)S(1)} %collective-permute-done.22.f_other_ref) | copy-start | bytes 3145732
  167.2 277.3 %all-reduce.6.cloned.1.call-start = ((), (), s32[]{:S(2)}) async-start(), calls=%async_computation.2 | async-start | bytes 8388608 | tf_op jit(solution)/shard_map/psum | solution.py:1062
  168.8 6.1 %copy-start.3 = (bf16[1024,512]{1,0:T(8,128)(2,1)S(1)}, bf16[1024,512]{1,0:T(8,128)(2,1)}, u32[]{:S(2)}) copy-start(bf16[1024,512]{1,0:T(8,128)(2,1)} %param.27) | copy-start | bytes 3145732
  170.1 4.8 %copy-start.24 = (bf16[512,1024]{1,0:T(8,128)(2,1)S(1)}, bf16[512,1024]{1,0:T(8,128)(2,1)}, u32[]{:S(2)}) copy-start(bf16[512,1024]{1,0:T(8,128)(2,1)} %copy-done.23) | copy-start | bytes 3145732
  186.5 3.4 copy-start.47
  186.5 3.4 copy-start.50
  189.9 4.5 collective-permute-start
  191.7 47.5 %collective-permute-start.1 = (bf16[512,1024]{1,0:T(8,128)(2,1)}, bf16[512,1024]{1,0:T(8,128)(2,1)}, u32[]{:S(2)}, u32[]{:S(2)}) collective-permute-start(bf16[512,1024]{1,0:T(8,128)(2,1)} %convolution_convert_fusion.9), channel_id=1, source_target_pairs={{0,1},{1,0},{2,3},{3,2},{4,5},{5,4},{6,7},{7,6},{8,9},{9,8},{10,11... | collective-permute-start | bytes 3145736 | tf_op jit(solution)/shard_map/while/body/ppermute | solution.py:437
  231.6 33.1 %collective-permute-start.2 = (bf16[256,2048]{1,0:T(8,128)(2,1)S(1)}, bf16[256,2048]{1,0:T(8,128)(2,1)S(1)}, u32[]{:S(2)}, u32[]{:S(2)}) collective-permute-start(bf16[256,2048]{1,0:T(8,128)(2,1)S(1)} %constant_dynamic-slice_fusion.9), channel_id=1, source_target_pairs={{0,4},{2,6},{4,0},{6,2},{8,12},{10,14},{12,8},{14,10},{16,20},{18,... | collective-permute-start | bytes 3145736 | tf_op jit(solution)/shard_map/while/body/ppermute | solution.py:892
  236.9 2.3 copy-start.28
  236.9 2.3 copy-start.51
  242.0 25.0 %collective-permute-start.4 = (bf16[512,1024]{1,0:T(8,128)(2,1)S(1)}, bf16[512,1024]{1,0:T(8,128)(2,1)S(1)}, u32[]{:S(2)}, u32[]{:S(2)}) collective-permute-start(bf16[512,1024]{1,0:T(8,128)(2,1)S(1)} %add_convert_fusion.15), channel_id=1, source_target_pairs={{0,1},{1,0},{2,3},{3,2},{4,5},{5,4},{6,7},{7,6},{8,9},{9,8},{10,11... | collective-permute-start | bytes 3145736 | tf_op jit(solution)/shard_map/while/body/ppermute | solution.py:437
  245.9 21.0 %copy-start.9 = (f32[512,1024]{1,0:T(8,128)S(1)}, f32[512,1024]{1,0:T(8,128)}, u32[]{:S(2)}) copy-start(f32[512,1024]{1,0:T(8,128)} %get-tuple-element.768) | copy-start | bytes 6291460 | tf_op jit(solution)/shard_map/while
  265.1 25.4 %collective-permute-start.3 = (bf16[128,2048]{1,0:T(8,128)(2,1)S(1)}, bf16[128,2048]{1,0:T(8,128)(2,1)S(1)}, u32[]{:S(2)}, u32[]{:S(2)}) collective-permute-start(bf16[128,2048]{1,0:T(8,128)(2,1)S(1)} %constant_dynamic-slice_fusion.10), channel_id=1, source_target_pairs={{0,8},{2,10},{4,12},{6,14},{8,0},{10,2},{12,4},{14,6},{16,24},{18,... | collective-permute-start | bytes 1572872 | tf_op jit(solution)/shard_map/while/body/ppermute | solution.py:892
  268.3 23.2 %copy-start.10 = (f32[512,1024]{1,0:T(8,128)}, f32[512,1024]{1,0:T(8,128)S(1)}, u32[]{:S(2)}) copy-start(f32[512,1024]{1,0:T(8,128)S(1)} %convert_add_fusion.2) | copy-start | bytes 6291460 | tf_op jit(solution)/shard_map/while
  291.7 7.7 %copy-start.25 = (bf16[512,1024]{1,0:T(8,128)(2,1)}, bf16[512,1024]{1,0:T(8,128)(2,1)S(1)}, u32[]{:S(2)}) copy-start(bf16[512,1024]{1,0:T(8,128)(2,1)S(1)} %get-tuple-element.892) | copy-start | bytes 3145732
  291.7 6.3 %copy-start.16 = (bf16[1024,512]{0,1:T(8,128)(2,1)S(1)}, bf16[1024,512]{0,1:T(8,128)(2,1)}, u32[]{:S(2)}) copy-start(bf16[1024,512]{0,1:T(8,128)(2,1)} %get-tuple-element.890) | copy-start | bytes 3145732
  295.6 3.7 copy-start.17
  300.7 2.6 copy-start.11
  303.2 18.9 %collective-permute-start.5 = (bf16[64,2048]{1,0:T(8,128)(2,1)S(1)}, bf16[64,2048]{1,0:T(8,128)(2,1)S(1)}, u32[]{:S(2)}, u32[]{:S(2)}) collective-permute-start(bf16[64,2048]{1,0:T(8,128)(2,1)S(1)} %constant_dynamic-slice_fusion.11), channel_id=1, source_target_pairs={{0,16},{2,18},{4,20},{6,22},{8,24},{10,26},{12,28},{14,30},{16,0},... | collective-permute-start | bytes 786440 | tf_op jit(solution)/shard_map/while/body/ppermute | solution.py:892
  322.2 19.3 %collective-permute-start.6 = (bf16[64,2048]{1,0:T(8,128)(2,1)S(1)}, bf16[64,2048]{1,0:T(8,128)(2,1)S(1)}, u32[]{:S(2)}, u32[]{:S(2)}) collective-permute-start(bf16[64,2048]{1,0:T(8,128)(2,1)S(1)} %add_convert_fusion.17), channel_id=1, source_target_pairs={{0,16},{2,18},{4,20},{6,22},{8,24},{10,26},{12,28},{14,30},{16,0},... | collective-permute-start | bytes 786440 | tf_op jit(solution)/shard_map/while/body/ppermute | solution.py:892
  341.5 22.5 %collective-permute-start.7 = (bf16[128,2048]{1,0:T(8,128)(2,1)S(1)}, bf16[128,2048]{1,0:T(8,128)(2,1)S(1)}, u32[]{:S(2)}, u32[]{:S(2)}) collective-permute-start(bf16[128,2048]{1,0:T(8,128)(2,1)S(1)} %pad_maximum_fusion.17), channel_id=1, source_target_pairs={{0,8},{2,10},{4,12},{6,14},{8,0},{10,2},{12,4},{14,6},{16,24},{18,... | collective-permute-start | bytes 1572872 | tf_op jit(solution)/shard_map/while/body/ppermute | solution.py:892
  364.3 27.0 %collective-permute-start.8 = (bf16[256,2048]{1,0:T(8,128)(2,1)S(1)}, bf16[256,2048]{1,0:T(8,128)(2,1)}, u32[]{:S(2)}, u32[]{:S(2)}) collective-permute-start(bf16[256,2048]{1,0:T(8,128)(2,1)S(1)} %pad_maximum_fusion.18), channel_id=1, source_target_pairs={{0,4},{2,6},{4,0},{6,2},{8,12},{10,14},{12,8},{14,10},{16,20},{18,... | collective-permute-start | bytes 3145736 | tf_op jit(solution)/shard_map/while/body/ppermute | solution.py:892
  394.5 20.2 %collective-permute-start.9 = (bf16[512,2048]{1,0:T(8,128)(2,1)}, bf16[512,2048]{1,0:T(8,128)(2,1)}, u32[]{:S(2)}, u32[]{:S(2)}) collective-permute-start(bf16[512,2048]{1,0:T(8,128)(2,1)} %pad_maximum_fusion.19), channel_id=1, source_target_pairs={{0,2},{2,0},{4,6},{6,4},{8,10},{10,8},{12,14},{14,12},{16,18},{18,... | collective-permute-start | bytes 6291464 | tf_op jit(solution)/shard_map/while/body/ppermute | solution.py:892
  395.3 3.8 collective-permute-start.10
  399.9 1.3 collective-permute-start.11
  401.1 4.0 collective-permute-start.12
  405.1 4.0 collective-permute-start.13
  409.1 5.0 %collective-permute-start.14 = (f32[9216]{0:T(1024)S(1)}, f32[9216]{0:T(1024)S(1)}, u32[]{:S(2)}, u32[]{:S(2)}) collective-permute-start(f32[9216]{0:T(1024)S(1)} %add.205), channel_id=1, source_target_pairs={{0,16},{2,18},{4,20},{6,22},{8,24},{10,26},{12,28},{14,30},{16,0},... | collective-permute-start | bytes 110600 | tf_op jit(solution)/shard_map/while/body/ppermute | solution.py:906
  417.7 2.6 copy-start.12
  420.3 8.1 %copy-start.13 = (bf16[2048,1024]{1,0:T(8,128)(2,1)S(1)}, bf16[2048,1024]{1,0:T(8,128)(2,1)}, u32[]{:S(2)}) copy-start(bf16[2048,1024]{1,0:T(8,128)(2,1)} %all-reduce.4.cloned.1.call-done) | copy-start | bytes 12582916
  444.5 2.9 copy-start.20
  (14 other events, 23.1 us)
Sparse Core Ops, SparseCore 0:
  25.3 76.3 all-gather.2
  166.6 127.0 all-reduce.3
  300.8 143.7 all-reduce.5

commit v3 on v2

--- a/solution.py
+++ b/solution.py
@@ -454,6 +454,15 @@
     return (pre * cumulative).astype(jnp.bfloat16), (cumulative + slope).astype(jnp.bfloat16)
 
 
+def blank(shapes):
+    return pl.pallas_call(
+        lambda *refs: None,
+        out_specs=[pl.BlockSpec(memory_space=pl.ANY)] * len(shapes),
+        out_shape=[jax.ShapeDtypeStruct(*shape) for shape in shapes],
+        name="blank",
+    )()
+
+
 def mean_of(rows):
     return jnp.mean(rows, axis=-1, keepdims=True)
 
@@ -623,8 +632,8 @@
     def _():
         gain = gain_ref[...]
         for_gain = for_shift = for_bias = 0.0
-        for at in range(0, h_ref.shape[0], PIECE):
-            rows = slice(at, at + PIECE)
+        for at in range(0, h_ref.shape[0], 256):
+            rows = slice(at, at + 256)
             final = total[rows, :] + down_bias_ref[...] + hidden_ref[rows, :]
             center = final - mean_of(final)
             inverse = lax.rsqrt(mean_of(center * center) + epsilon)
@@ -644,27 +653,34 @@
         sums_ref[2:3, :] = for_bias
 
 
-def forward_other(hidden_low, packs, bias, base, hidden, down_bias, outer, valid, gain, shift):
-    rows, depth = hidden_low.shape
+def forward_other(hidden_low, packs, bias, base, hidden, down_bias, outer, valid, gain, shift,
+                  at, of, earlier):
+    whole_rows, depth = hidden_low.shape
+    rows = whole_rows // of
     units = packs.shape[3]
     up, down = packed_specs(packs, lambda j: j)
     whole = lambda shape: pl.BlockSpec(shape, lambda j: (0, 0))
+    part = lambda width: pl.BlockSpec((rows, width), lambda j: (at, 0))
+    body = forward_other_kernel
+    if earlier:
+        body = lambda *refs: forward_other_kernel(*refs[:11], *refs[14:])
     return pl.pallas_call(
-        forward_other_kernel,
+        body,
         grid=(units // UNITS,),
         in_specs=[
-            whole((rows, depth)), up, pl.BlockSpec((1, UNITS), lambda j: (0, j)), down,
-            whole((rows, depth)), whole((rows, depth)), whole((1, depth)), whole((rows, depth)),
-            whole((rows, 1)), whole((1, depth)), whole((1, depth)),
-        ],
+            part(depth), up, pl.BlockSpec((1, UNITS), lambda j: (0, j)), down,
+            part(depth), part(depth), whole((1, depth)), part(depth),
+            part(1), whole((1, depth)), whole((1, depth)),
+        ]
+        + [pl.BlockSpec(memory_space=pl.ANY)] * len(earlier),
         out_specs=[
-            pl.BlockSpec((rows, UNITS), lambda j: (0, j)),
-            whole((rows, depth)), whole((rows, depth)), whole((rows, depth)), whole((8, depth)),
+            pl.BlockSpec((rows, UNITS), lambda j: (at, j)),
+            part(depth), part(depth), whole((rows, depth)), whole((8, depth)),
         ],
         out_shape=[
-            jax.ShapeDtypeStruct((rows, units), jnp.bfloat16),
-            jax.ShapeDtypeStruct((rows, depth), jnp.bfloat16),
-            jax.ShapeDtypeStruct((rows, depth), jnp.float32),
+            jax.ShapeDtypeStruct((whole_rows, units), jnp.bfloat16),
+            jax.ShapeDtypeStruct((whole_rows, depth), jnp.bfloat16),
+            jax.ShapeDtypeStruct((whole_rows, depth), jnp.float32),
             jax.ShapeDtypeStruct((rows, depth), jnp.bfloat16),
             jax.ShapeDtypeStruct((8, depth), jnp.float32),
         ],
@@ -672,10 +688,12 @@
             pltpu.VMEM((rows, depth), jnp.float32), pltpu.VMEM((rows, UNITS), jnp.bfloat16),
             pltpu.VMEM((rows, UNITS), jnp.float32),
         ],
+        input_output_aliases={11 + index: index for index in range(len(earlier))},
         compiler_params=pltpu.CompilerParams(vmem_limit_bytes=BIG),
         name="forward_other",
         cost_estimate=work(8 * rows * depth * units),
-    )(hidden_low, packs, bias, packs, base, hidden, down_bias, outer, valid, gain, shift)
+    )(hidden_low, packs, bias, packs, base, hidden, down_bias, outer, valid, gain, shift,
+      *earlier)
 
 
 def backward_rows_kernel(half, f_ref, slope_own_ref, slope_other_ref, up_ref, down_ref,
@@ -765,41 +783,59 @@
       inverse, gain)
 
 
-def down_grad_kernel(h_ref, up_ref, bias_ref, act_ref, f_own_ref, f_other_ref,
-                     slope_ref, grad_ref, act_scr, pre_scr):
-    gelu_block(h_ref, up_ref[...], bias_ref, act_scr, slope_ref, pre_scr)
-    grad_ref[...] = (
-        dot_tn(act_ref[...], f_own_ref[...]) + dot_tn(act_scr[...], f_other_ref[...])
-    ).astype(jnp.bfloat16)
-
-
-def down_grad(hidden_other, up_weight, up_bias, act_own, final_own, final_other):
-    rows, depth = hidden_other.shape
+def gelu_kernel(h_ref, up_ref, bias_ref, act_ref, slope_ref, pre_scr):
+    gelu_block(h_ref, up_ref[...], bias_ref, act_ref, slope_ref, pre_scr)
+
+
+def gelu_rows(hidden, up_weight, up_bias):
+    rows, depth = hidden.shape
     units = up_weight.shape[1]
-    whole = lambda shape: pl.BlockSpec(shape, lambda j: (0, 0))
     return pl.pallas_call(
-        down_grad_kernel,
+        gelu_kernel,
         grid=(units // UNITS,),
         in_specs=[
-            whole((rows, depth)),
+            pl.BlockSpec((rows, depth), lambda j: (0, 0)),
             pl.BlockSpec((depth, UNITS), lambda j: (0, j)),
             pl.BlockSpec((1, UNITS), lambda j: (0, j)),
-            pl.BlockSpec((rows, UNITS), lambda j: (0, j)),
-            whole((rows, depth)), whole((rows, depth)),
-        ],
-        out_specs=[
-            pl.BlockSpec((rows, UNITS), lambda j: (0, j)),
-            pl.BlockSpec((UNITS, depth), lambda j: (j, 0)),
-        ],
-        out_shape=[
-            jax.ShapeDtypeStruct((rows, units), jnp.bfloat16),
-            jax.ShapeDtypeStruct((units, depth), jnp.bfloat16),
-        ],
-        scratch_shapes=[pltpu.VMEM((rows, UNITS), jnp.bfloat16), pltpu.VMEM((rows, UNITS), jnp.float32)],
+        ],
+        out_specs=[pl.BlockSpec((rows, UNITS), lambda j: (0, j))] * 2,
+        out_shape=[jax.ShapeDtypeStruct((rows, units), jnp.bfloat16)] * 2,
+        scratch_shapes=[pltpu.VMEM((rows, UNITS), jnp.float32)],
+        compiler_params=pltpu.CompilerParams(vmem_limit_bytes=BIG),
+        name="gelu_rows",
+        cost_estimate=work(rows * depth),
+    )(hidden, up_weight, up_bias)
+
+
+def down_grad_kernel(count, own_ref, other_ref, *refs):
+    grad_ref = refs[-1]
+    total = None
+    rows = own_ref.shape[0] // count
+    for at in range(count):
+        span = slice(at * rows, (at + 1) * rows)
+        part = dot_tn(own_ref[span, :], refs[at][...]) + dot_tn(
+            other_ref[span, :], refs[count + at][...]
+        )
+        total = part if total is None else total + part
+    grad_ref[...] = total.astype(jnp.bfloat16)
+
+
+def down_grad(act_own, act_other, final_own, final_other):
+    rows, units = act_own.shape
+    count = len(final_own)
+    depth = final_own[0].shape[1]
+    part = pl.BlockSpec((rows, UNITS), lambda j: (0, j))
+    return pl.pallas_call(
+        functools.partial(down_grad_kernel, count),
+        grid=(units // UNITS,),
+        in_specs=[part, part]
+        + [pl.BlockSpec((rows // count, depth), lambda j: (0, 0))] * (2 * count),
+        out_specs=pl.BlockSpec((UNITS, depth), lambda j: (j, 0)),
+        out_shape=jax.ShapeDtypeStruct((units, depth), jnp.bfloat16),
         compiler_params=pltpu.CompilerParams(vmem_limit_bytes=BIG),
         name="down_grad",
-        cost_estimate=work(8 * rows * depth * units),
-    )(hidden_other, up_weight, up_bias, act_own, final_own, final_other)
+        cost_estimate=work(4 * rows * depth * units),
+    )(act_own, act_other, *final_own, *final_other)
 
 
 def up_grad_kernel(f_ref, down_ref, slope_ref, d_pre_ref, h_own_ref, h_other_ref,
@@ -897,14 +933,6 @@
 
     def done(self):
         return not self.steps and self.flying is None
-
-
-def sum_small(values):
-    count = lax.axis_size("dp")
-    for bit in range(count.bit_length() - 1):
-        perm = [(at, at ^ (1 << bit)) for at in range(count)]
-        values = values + lax.ppermute(values, "dp", perm)
-    return values
 
 
 def body_pair(
@@ -960,6 +988,15 @@
         matmul(rows, key_weight).astype(bf16),
         (matmul(rows, value_weight) + value_bias).astype(bf16),
     )
+    fills = blank(
+        [
+            *[((length, query_weight.shape[1]), bf16)] * 3,
+            ((own_rows, tokens.shape[1]), bf16),
+            ((4 * up_weight.shape[0] // count, up_bias.size), bf16),
+            (up_weight.shape, f32),
+            (down_weight.shape, f32),
+        ]
+    )
     query_own, key_own, value_own = project(tokens)
     query_other, key_other, value_other = project(tokens_other)
     key_rows = jnp.concatenate([key_own, key_other])
@@ -979,30 +1016,28 @@
     hidden_other = swap(hidden_own)
 
     act_own, slope_own, base = forward_own(hidden_own, up_weight, row(up_bias), down_weight)
-    slope_local, output, d_final, final_own, second_sums = forward_other(
-        hidden_own, packs, row(bias_other), base, hidden, row(down_bias), cotangent, valid,
-        row(second_gain), row(second_shift),
-    )
-    final_other = swap(final_own)
-    d_pre_own, d_middle, middle_own, first_sums = backward_rows(
-        final_own, slope_own, slope_local, up_weight, down_weight, packs, d_final,
-        normal_first, inverse_first, row(first_gain),
-    )
-    d_context_away = matmul_nt(middle_own, out_other).astype(bf16)
-    d_context_other = swap(d_context_away)
-    d_context_own = matmul_nt(middle_own, out_weight).astype(bf16)
-
-    hidden_other = after(hidden_other, d_context_away, d_context_own)
-    final_other = after(final_other, d_context_away, d_context_own)
-    slope_other, grad_down_weight = down_grad(
-        hidden_other, up_weight, row(up_bias), act_own, final_own, final_other
-    )
+    earlier, final_own, second_sums = (), [], 0.0
+    for at in range(2):
+        *earlier, low_rows, sums = forward_other(
+            hidden_own, packs, row(bias_other), base, hidden, row(down_bias), cotangent, valid,
+            row(second_gain), row(second_shift), at, 2, earlier,
+        )
+        final_own.append(low_rows)
+        second_sums = second_sums + sums
+    slope_local, output, d_final = earlier
+    final_other = [swap(rows) for rows in final_own]
+    act_other, slope_other = gelu_rows(
+        after(hidden_other, *final_own, final_other[0]), up_weight, row(up_bias)
+    )
+    grad_down_weight = down_grad(act_own, act_other, final_own, final_other)
     down_sum = lax.psum(grad_down_weight, "dp")
+
+    *final_own, grad_down_weight = lax.optimization_barrier((*final_own, grad_down_weight))
+    final_rows = jnp.concatenate(final_own)
+    final_away = jnp.concatenate(final_other)
     queries = jnp.concatenate([query_own, query_other])
     context = jnp.concatenate([context_own, context_away])
     mass = jnp.concatenate([mass_own, mass_other], axis=1)
-    d_context_other = after(d_context_other, grad_down_weight)
-    d_context = jnp.concatenate([d_context_own, d_context_other])
     gathered = jnp.concatenate([tokens, tokens_other])
     weights = (query_weight, key_weight, value_weight)
     width = query_weight.shape[1]
@@ -1021,10 +1056,19 @@
     left = []
 
     def backward_part(carry):
-        d_context, final_other, d_middle = carry[0], carry[3], carry[5]
+        final_rows, d_final = carry[0][3], carry[3]
+        d_pre_own, d_middle, middle_own, first_sums = backward_rows(
+            final_rows, slope_own, slope_local, up_weight, down_weight, packs, d_final,
+            normal_first, inverse_first, row(first_gain),
+        )
+        d_context_away = matmul_nt(middle_own, out_other).astype(bf16)
+        d_context_other = swap(d_context_away)
+        d_context_own = matmul_nt(middle_own, out_weight).astype(bf16)
         grad_up_weight, grad_up_bias = up_grad(
-            final_other, down_weight, slope_other, d_pre_own, hidden_own, hidden_other
+            after(final_away, d_context_away, d_context_own), down_weight, slope_other,
+            d_pre_own, hidden_own, hidden_other,
         )
+        d_context = jnp.concatenate([d_context_own, d_context_other])
         up_sum = Chain(grad_up_weight).push()
         partial_away = matmul_tn(after(context_here, grad_up_weight), middle_own).astype(bf16)
         partial_here = swap(partial_away)
@@ -1033,55 +1077,63 @@
         d_rows = attention_backward(
             queries, key_rows, values, rows, context, mass, segment, 0, 1
         )
-        up_sum.push(*d_rows)
+        up_sum.end(*d_rows)
+        left[:] = [up_sum.steps]
+        d_rows, up_sum.held = lax.optimization_barrier((d_rows, up_sum.held))
         grads = [matmul_tn(gathered, d).astype(bf16) for d in d_rows]
         grad_out_weight = matmul_tn(after(context_own, d_rows[0]), middle_own)
         grads.append((grad_out_weight + partial_here.astype(f32)).astype(bf16))
-        away = [parts(d)[1] for d in d_rows]
-        away[0] = after(away[0], *grads)
-        away = entering(away).astype(bf16)
-        back = swap(away)
-        own = [parts(d)[0] for d in d_rows]
-        own[0] = after(own[0], away)
-        own = entering(own) + d_middle
+        away = entering([parts(d)[1] for d in d_rows]).astype(bf16)
+        own = entering([parts(d)[0] for d in d_rows]) + d_middle
         biases = [jnp.sum(d_rows[at], axis=0, dtype=f32) for at in (0, 2)]
-        up_sum.end(own)
-        left[:] = [up_sum.steps]
-        return (*grads, up_sum.held, own + back.astype(f32), *biases, grad_up_bias)
-
-    *grads, held, input_grad, query_bias_sum, value_bias_sum, grad_up_bias = run(
+        return grads, away, up_sum.held, own, biases, grad_up_bias, first_sums
+
+    final_rows = after(final_rows, grad_down_weight)
+    grads, away, held, own, biases, grad_up_bias, first_sums = run(
         backward_part,
         (
-            d_context, jnp.zeros_like(key_rows), jnp.zeros_like(values), final_other,
-            jnp.zeros((2 * up_weight.shape[0] // count, up_bias.size), bf16), d_middle,
-            jnp.zeros((width,), f32), jnp.zeros((width,), f32),
-            jnp.zeros((1, up_bias.size), f32),
+            [*fills[:3], final_rows], fills[3], fills[4], d_final,
+            [jnp.zeros((width,), f32)] * 2, jnp.zeros((1, up_bias.size), f32),
+            jnp.zeros_like(second_sums),
         ),
     )
-    down_sum, *grads = lax.optimization_barrier((down_sum, *grads))
+    down_sum, grads = lax.optimization_barrier((down_sum, grads))
     *qkv, out_sum = lax.psum(tuple(grads), "dp")
 
     short = jnp.concatenate(
         [
             first_sums[:3].reshape(-1), second_sums[:3].reshape(-1), grad_up_bias.reshape(-1),
-            query_bias_sum, value_bias_sum,
+            *biases,
         ]
     )
     sizes = [tokens.shape[1]] * 6 + [up_bias.size, width, width]
 
     def last_part(carry):
-        held, _, short = carry
+        held, _, _, short, own = carry
+        down_total = after(down_sum, short).astype(f32)
         up_sum = Chain(held)
         up_sum.steps = list(left[0])
+        up_sum.push()
+        back = swap(after(away, short))
         both = 6 * tokens.shape[1]
         shared = short[:both] + swap(short[:both])
-        short = sum_small(jnp.concatenate([shared, short[both:]]))
+        short = jnp.concatenate([shared, short[both:]])
+        up_sum.push(short, down_total)
+        for step in range(count.bit_length() - 1):
+            short = short + lax.ppermute(
+                short, "dp", [(at, at ^ (1 << step)) for at in range(count)]
+            )
+            up_sum.push(short)
+        total_grad = own + back.astype(f32)
         while not up_sum.done():
-            up_sum.push()
-        return held, up_sum.held, short
+            up_sum.push(total_grad)
+        return held, up_sum.held.astype(f32), down_total, short, total_grad
 
     held = after(held, grads[0])
-    _, up_total, small = run(last_part, (held, jnp.zeros(up_weight.shape, bf16), short))
+    _, up_total, down_total, small, input_grad = run(
+        last_part, (held, fills[5], fills[6], short, own)
+    )
+    up_total, qkv, out_sum = lax.optimization_barrier((up_total, qkv, out_sum))
     pieces, at = [], 0
     for size in sizes:
         pieces.append(small[at : at + size])
@@ -1098,9 +1150,9 @@
         pieces[2],
         pieces[0],
         pieces[1],
-        up_total.astype(f32),
+        up_total,
         pieces[6],
-        after(down_sum, up_total).astype(f32),
+        down_total,
         pieces[5],
         pieces[3],
         pieces[4],

time: 464 us -> 429 us (0.925)
  waiting for transfers between devices: 176 us -> 130 us
  Pallas kernels: 127 us -> 134 us
  local copies, waits for them, and re-layouts: 35.5 us -> 30.8 us
    ppermute x8, waiting for transfers between devices: 127 us -> 60.5 us  [push(): self.flying = (kind, bit, kept, lax.ppermute(sent, 'dp', perm))]
    ppermute x11 -> x12, waiting for transfers between devices: 29.5 us -> 47.6 us  [swap(): return lax.ppermute(rows, 'mp', [(0, 1), (1, 0)])]
    psum x1, waiting for transfers between devices: 9.02 us -> 0.22 us  [body_pair(): *qkv, out_sum = lax.psum(tuple(grads), 'dp')]
    ppermute x4, waiting for transfers between devices: 10.2 us -> 18.4 us  [last_part(): lax.ppermute(short, 'dp', [(at, at ^ 1 << step) for at in range(count)])]
    pallas_call x2 -> x5, Pallas kernels: 31.3 us -> 37.3 us  [the longest x2 20 us: forward_other(): pl.pallas_call(body, grid=(units // UNITS,), in_specs=[part(depth), up, p...]
    while x1 -> x3, local copies, waits for them, and re-layouts: 1.32 us -> 7.02 us  [run(): lax.while_loop(lambda carry: carry[0] < once, lambda carry: (carry[0] + 1...]
    ppermute x11 -> x12, starting transfers between devices: 14.5 us -> 15.3 us  [swap(): return lax.ppermute(rows, 'mp', [(0, 1), (1, 0)])]
    convert_element_type x2 -> x3, other arithmetic: 11.3 us -> 11.9 us  [the longest x1 7.02 us: last_part(): down_total = after(down_sum, short).astype(f32)]
  transfers between devices with their start and end apart: 26 -> 27, of which waited for: 17 -> 15; matrix products, arithmetic and copies ran while one was open for 22% -> 24% of each run, Pallas kernels for 27% -> 29%
where the time goes in v3:
time: 429 us; the launch traced here: 425 us
  Pallas kernels  134 us (31%)
  waiting for transfers between devices  130 us (30%)
  other arithmetic  51.9 us (12%)
  matrix products  36.5 us (9%)
  local copies, waits for them, and re-layouts  30.8 us (7%)
  starting transfers between devices  27 us (6%)
  between operations  14.4 us (3%)
    ppermute x8, waiting for transfers between devices, push(): self.flying = (kind, bit, kept, lax.ppermute(sent, 'dp', perm))  60.5 us
    ppermute x12, waiting for transfers between devices, swap(): return lax.ppermute(rows, 'mp', [(0, 1), (1, 0)])  47.6 us
    pallas_call x1, Pallas kernels, attention_backward(): pl.pallas_call(functools.partial(backward_kernel, pairs, at * (heads // o...  27.2 us
    pallas_call x2, Pallas kernels, forward_other(): pl.pallas_call(body, grid=(units // UNITS,), in_specs=[part(depth), up, p...  20 us
    pallas_call x1, Pallas kernels, backward_rows(): pl.pallas_call(functools.partial(backward_rows_kernel, half), grid=(2 * h...  19.5 us
    ppermute x4, waiting for transfers between devices, last_part(): lax.ppermute(short, 'dp', [(at, at ^ 1 << step) for at in range(count)])  18.4 us
    pallas_call x2, Pallas kernels, attention_forward(): pl.pallas_call(functools.partial(forward_kernel, pairs), grid=(rows // bl...  18.4 us
    ppermute x12, starting transfers between devices, swap(): return lax.ppermute(rows, 'mp', [(0, 1), (1, 0)])  15.3 us
  transfers between devices with their start and end apart: 27, of which 15 were waited for; matrix products, arithmetic and copies ran while one was open for 24% of the time, Pallas kernels for 29%

profile of v3, /device:TPU:0, one launch (start us, length us, event | category | flops | bytes accessed | tf_op | source)
XLA Modules:
  0.0 425.5 jit_solution(4649664371634451696)
XLA Ops:
  7.3 1.9 pack_weights.1
  9.2 2.9 collective-permute-start.16
  12.2 12.1 %collective-permute-done.16 = bf16[128,2048]{1,0:T(8,128)(2,1)S(1)} collective-permute-done((bf16[128,2048]{1,0:T(8,128)(2,1)}, bf16[128,2048]{1,0:T(8,128)(2,1)S(1)}, u32[]{:S(2)}, u32[]{:S(2)}) %collective-permute-start.16) | collective-permute-done | bytes 524320 | tf_op jit(solution)/shard_map/ppermute | solution.py:437
  25.2 1.8 collective-permute-start.20
  27.8 1.9 convolution_convert_fusion.7
  29.7 3.1 fusion.15
  32.9 2.1 fusion.14.q_ref
  40.2 2.4 copy.60
  42.7 2.3 copy.61
  45.0 2.3 copy.62
  47.9 3.6 collective-permute-done.17
  52.1 2.2 fusion.16
  54.4 2.0 convolution_convert_fusion.6
  56.6 2.7 fusion.17.q_ref
  59.3 8.5 %attention_forward.2 = (bf16[512,512]{1,0:T(8,128)(2,1)S(1)}, f32[8,512]{1,0:T(8,128)S(1)}) custom-call(bf16[512,512]{1,0:T(8,128)(2,1)S(1)} %fusion.17.q_ref, bf16[1024,512]{1,0:T(8,128)(2,1)S(1)} %get-tuple-element.1014.k_ref, bf16[1024,512]{1,0:T(8,128)(2,1)S(1)} %get-tuple-element.1015.v_ref, s32[1,1024]{1,0:T(1,128)S(1)} %bitcast.119, ...), custom_call_target="tpu_custom_call" | custom-call | flops 4294967296 | tf_op jit(solution)/shard_map/attention_forward/pallas_call | solution.py:64
  69.3 3.0 pad_maximum_fusion.5
  72.4 5.4 %collective-permute-done.18.w_other_ref = bf16[512,1024]{1,0:T(8,128)(2,1)S(1)} collective-permute-done((bf16[512,1024]{1,0:T(8,128)(2,1)}, bf16[512,1024]{1,0:T(8,128)(2,1)S(1)}, u32[]{:S(2)}, u32[]{:S(2)}) %collective-permute-start.18) | collective-permute-done | bytes 1048608 | tf_op jit(solution)/shard_map/ppermute | solution.py:437
  78.9 9.8 %attention_forward.3 = (bf16[512,512]{1,0:T(8,128)(2,1)S(1)}, f32[8,512]{1,0:T(8,128)S(1)}) custom-call(bf16[512,512]{1,0:T(8,128)(2,1)S(1)} %fusion.14.q_ref, bf16[1024,512]{1,0:T(8,128)(2,1)S(1)} %copy-done.24, bf16[1024,512]{1,0:T(8,128)(2,1)} %copy-done.25, s32[1,1024]{1,0:T(1,128)S(1)} %bitcast.120, s32[512,1]{1,0:T(8,128)S(1)} %copy.57.col_ref), custom_call_target="tpu_custom_call" | custom-call | flops 4294967296 | tf_op jit(solution)/shard_map/attention_forward/pallas_call | solution.py:64
  88.8 5.6 %middle_norm.1 = (f32[512,1024]{1,0:T(8,128)}, bf16[512,1024]{1,0:T(8,128)(2,1)S(1)}, f32[512,1024]{1,0:T(8,128)}, f32[512,1]{1,0:T(8,128)}) custom-call(bf16[512,512]{1,0:T(8,128)(2,1)S(1)} %get-tuple-element.1019.own_ref, bf16[512,512]{1,0:T(8,128)(2,1)} %collective-permute-done.19.here_ref, bf16[512,1024]{1,0:T(8,128)(2,1)} %w_own_ref.1, ...), custom_call_target="tpu_custom_call" | custom-call | flops 2147483648 | tf_op jit(solution)/shard_map/middle_norm/pallas_call | solution.py:529
  95.1 12.2 %forward_own.1 = (bf16[512,2048]{1,0:T(8,128)(2,1)}, bf16[512,2048]{1,0:T(8,128)(2,1)}, f32[512,1024]{1,0:T(8,128)}) custom-call(bf16[512,1024]{1,0:T(8,128)(2,1)S(1)} %get-tuple-element.1009.h_ref.refs_0_, bf16[1024,2048]{1,0:T(8,128)(2,1)S(1)} %copy-done.12, f32[1,2048]{1,0:T(1,128)} %bitcast.132, bf16[2048,1024]{1,0:T(8,128)(2,1)} %down_ref.1), custom_call_target="tpu_custom_call" | custom-call | flops 6442450944 | tf_op jit(solution)/shard_map/forward_own/pallas_call | solution.py:576
  107.3 10.0 %forward_other.2 = (bf16[512,2048]{1,0:T(8,128)(2,1)S(1)}, bf16[512,1024]{1,0:T(8,128)(2,1)}, f32[512,1024]{1,0:T(8,128)S(1)}, bf16[256,1024]{1,0:T(8,128)(2,1)}, f32[8,1024]{1,0:T(8,128)}) custom-call(bf16[512,1024]{1,0:T(8,128)(2,1)S(1)} %get-tuple-element.1009.h_ref.refs_0_, bf16[16,2,64,2048]{3,2,1,0:T(8,128)(2,1)} %bitcast.113, f32[1,2048]{1,0:T(1,128)} %bitcast.124, ...), custom_call_target="tpu_custom_call" | custom-call | flops 4294967296 | tf_op jit(solution)/shard_map/forward_other/pallas_call | solution.py:667
  118.7 10.0 %forward_other.3 = (bf16[512,2048]{1,0:T(8,128)(2,1)S(1)}, bf16[512,1024]{1,0:T(8,128)(2,1)}, f32[512,1024]{1,0:T(8,128)S(1)}, bf16[256,1024]{1,0:T(8,128)(2,1)}, f32[8,1024]{1,0:T(8,128)}) custom-call(bf16[512,1024]{1,0:T(8,128)(2,1)S(1)} %get-tuple-element.1009.h_ref.refs_0_, ...), custom_call_target="tpu_custom_call", output_to_operand_aliasing={{0}: (11, {}), {1}: (12, {}), {2}: (13, {})} | custom-call | flops 4294967296 | tf_op jit(solution)/shard_map/forward_other/pallas_call | solution.py:667
  132.6 9.0 %gelu_rows.1 = (bf16[512,2048]{1,0:T(8,128)(2,1)}, bf16[512,2048]{1,0:T(8,128)(2,1)}) custom-call(bf16[512,1024]{1,0:T(8,128)(2,1)} %collective-permute-done.21.h_ref, bf16[1024,2048]{1,0:T(8,128)(2,1)} %up_ref.5, f32[1,2048]{1,0:T(1,128)} %bitcast.133), custom_call_target="tpu_custom_call" | custom-call | flops 524288 | tf_op jit(solution)/shard_map/gelu_rows/pallas_call | solution.py:793
  141.6 8.4 %down_grad.1 = bf16[2048,1024]{1,0:T(8,128)(2,1)} custom-call(bf16[512,2048]{1,0:T(8,128)(2,1)} %get-tuple-element.358.own_ref, bf16[512,2048]{1,0:T(8,128)(2,1)} %get-tuple-element.360.other_ref, bf16[256,1024]{1,0:T(8,128)(2,1)} %get-tuple-element.361.refs_0_, bf16[256,1024]{1,0:T(8,128)(2,1)} %get-tuple-element.362.refs_1_, ...), custom_call_target="tpu_custom_call" | custom-call | flops 4294967296 | tf_op jit(solution)/shard_map/down_grad/pallas_call | solution.py:828
  151.5 2.3 pad_maximum_fusion.9
  156.1 102.9 %while.46 = (s32[]{:T(128)}, bf16[1024,512]{0,1:T(8,128)(2,1)}, bf16[1024,512]{0,1:T(8,128)(2,1)}, bf16[1024,512]{0,1:T(8,128)(2,1)}, bf16[512,1024]{1,0:T(8,128...) while((s32[]{:T(128)}, bf16[1024,512]{0,1:T(8,128)(2,1)}, ...), condition=%wide.region_5.6_spmd, body=%wide.region_2.0_spmd.sunk | while | flops 30082596864 | bytes 159403200 | solution.py:1050
  156.8 19.5 %backward_rows.1 = (bf16[512,2048]{1,0:T(8,128)(2,1)}, f32[512,1024]{1,0:T(8,128)}, bf16[512,1024]{1,0:T(8,128)(2,1)}, f32[8,1024]{1,0:T(8,128)}) custom-call(bf16[512,1024]{1,0:T(8,128)(2,1)S(1)} %get-tuple-element.1034.f_ref, bf16[512,2048]{1,0:T(8,128)(2,1)} %get-tuple-element.1090.slope_own_ref, bf16[512,2048]{1,0:T(8,128)(2,1)} %get-tuple-element.1091.slope_other_ref, ...), custom_call_target="tpu_custom_call" | custom-call | flops 10737418240 | tf_op jit(solution)/shard_map/while/body/backward_rows/pallas_call | solution.py:756
  176.4 2.9 convolution_convert_fusion.11
  180.1 12.0 %up_grad.1 = (bf16[1024,2048]{1,0:T(8,128)(2,1)}, f32[1,2048]{1,0:T(1,128)}) custom-call(bf16[512,1024]{1,0:T(8,128)(2,1)} %get-tuple-element.941.f_ref, bf16[2048,1024]{1,0:T(8,128)(2,1)} %get-tuple-element.1093.down_ref, bf16[512,2048]{1,0:T(8,128)(2,1)} %get-tuple-element.1100.slope_ref, bf16[512,2048]{1,0:T(8,128)(2,1)} %get-tuple-element.942.d_pre_ref, ...), custom_call_target="tpu_custom_call" | custom-call | flops 6442450944 | tf_op jit(solution)/shard_map/while/body/up_grad/pallas_call | solution.py:861
  192.1 3.2 constant_dynamic-slice_fusion.8
  196.5 3.2 convolution_convert_fusion.13
  199.7 3.0 add_convert_fusion.12
  205.1 1.5 collective-permute-start.2
  208.1 2.2 collective-permute-done
  211.4 27.2 %attention_backward.1 = (bf16[1024,512]{1,0:T(8,128)(2,1)S(1)}, bf16[1024,512]{1,0:T(8,128)(2,1)S(1)}, bf16[1024,512]{1,0:T(8,128)(2,1)S(1)}) custom-call(bf16[1024,512]{1,0:T(8,128)(2,1)S(1)} %copy-done.21, bf16[1024,512]{1,0:T(8,128)(2,1)} %get-tuple-element.1106.k_ref, bf16[1024,512]{1,0:T(8,128)(2,1)} %get-tuple-element.1107.v_ref, ...), custom_call_target="tpu_custom_call" | custom-call | flops 4294967296 | tf_op jit(solution)/shard_map/while/body/attention_backward/pallas_call | solution.py:152
  238.7 2.7 add_convert_fusion.13
  244.8 2.3 fusion.113
  247.1 2.3 fusion.114
  249.4 2.2 fusion.115
  252.9 1.7 add_convert_fusion.15
  254.6 2.1 add_add_fusion.2
  256.7 2.0 add_convert_fusion.14
  262.0 3.1 all-reduce.4.cloned.1.call-done
  265.1 2.4 copy.63
  271.3 137.7 %while.47 = (s32[]{:T(128)}, f32[1024,2048]{1,0:T(8,128)}, f32[2048,1024]{1,0:T(8,128)}, f32[9216]{0:T(1024)S(1)}, f32[512,1024]{1,0:T(8,128)}, /*index=5*/s32[]...) while((s32[]{:T(128)}, f32[1024,2048]{1,0:T(8,128)}, ...), condition=%wide.region_8.9_spmd, body=%wide.region_7.8_spmd.sunk | while | flops 31780900 | bytes 86025256 | solution.py:1050
  274.0 7.0 %convert_element_type.278 = f32[2048,1024]{1,0:T(8,128)} convert(bf16[2048,1024]{1,0:T(8,128)(2,1)} %get-tuple-element.968) | non-fusion elementwise | flops 2097152 | bytes 12582912 | tf_op jit(solution)/shard_map/while/body/convert_element_type | solution.py:1113
  281.2 13.6 %collective-permute-done.4 = bf16[128,2048]{1,0:T(8,128)(2,1)S(1)} collective-permute-done((bf16[128,2048]{1,0:T(8,128)(2,1)S(1)}, bf16[128,2048]{1,0:T(8,128)(2,1)S(1)}, u32[]{:S(2)}, u32[]{:S(2)}) %collective-permute-start.4) | collective-permute-done | bytes 524320 | tf_op jit(solution)/shard_map/while/body/ppermute | solution.py:928
  295.5 20.1 %collective-permute-done.6 = bf16[64,2048]{1,0:T(8,128)(2,1)S(1)} collective-permute-done((bf16[64,2048]{1,0:T(8,128)(2,1)S(1)}, bf16[64,2048]{1,0:T(8,128)(2,1)S(1)}, u32[]{:S(2)}, u32[]{:S(2)}) %collective-permute-start.6) | collective-permute-done | bytes 262176 | tf_op jit(solution)/shard_map/while/body/ppermute | solution.py:928
  315.8 3.9 collective-permute-done.9
  319.8 11.5 %collective-permute-done.8 = bf16[64,2048]{1,0:T(8,128)(2,1)S(1)} collective-permute-done((bf16[64,2048]{1,0:T(8,128)(2,1)S(1)}, bf16[64,2048]{1,0:T(8,128)(2,1)S(1)}, u32[]{:S(2)}, u32[]{:S(2)}) %collective-permute-start.8) | collective-permute-done | bytes 262176 | tf_op jit(solution)/shard_map/while/body/ppermute | solution.py:928
  331.4 2.0 collective-permute-start.11
  333.4 10.1 %collective-permute-done.11 = f32[9216]{0:T(1024)S(1)} collective-permute-done((f32[9216]{0:T(1024)S(1)}, f32[9216]{0:T(1024)S(1)}, u32[]{:S(2)}, u32[]{:S(2)}) %collective-permute-start.11) | collective-permute-done | bytes 36896 | tf_op jit(solution)/shard_map/while/body/ppermute | solution.py:1123
  343.9 5.2 %collective-permute-start.12 = (bf16[256,2048]{1,0:T(8,128)(2,1)S(1)}, bf16[256,2048]{1,0:T(8,128)(2,1)}, u32[]{:S(2)}, u32[]{:S(2)}) collective-permute-start(bf16[256,2048]{1,0:T(8,128)(2,1)S(1)} %pad_maximum_fusion.21), channel_id=1, source_target_pairs={{0,4},{2,6},{4,0},{6,2},{8,12},{10,14},{12,8},{14,10},{16,20},{18,... | collective-permute-start | bytes 3145736 | tf_op jit(solution)/shard_map/while/body/ppermute | solution.py:928
  349.8 4.4 %collective-permute-done.13 = f32[9216]{0:T(1024)S(1)} collective-permute-done((f32[9216]{0:T(1024)S(1)}, f32[9216]{0:T(1024)S(1)}, u32[]{:S(2)}, u32[]{:S(2)}) %collective-permute-start.13) | collective-permute-done | bytes 36896 | tf_op jit(solution)/shard_map/while/body/ppermute | solution.py:1123
  354.3 15.3 %collective-permute-done.12 = bf16[256,2048]{1,0:T(8,128)(2,1)} collective-permute-done((bf16[256,2048]{1,0:T(8,128)(2,1)S(1)}, bf16[256,2048]{1,0:T(8,128)(2,1)}, u32[]{:S(2)}, u32[]{:S(2)}) %collective-permute-start.12) | collective-permute-done | bytes 1048608 | tf_op jit(solution)/shard_map/while/body/ppermute | solution.py:928
  369.5 1.7 broadcast_select_fusion.14
  374.2 24.3 %collective-permute-done.15 = bf16[512,1024]{1,0:T(8,128)(2,1)S(1)} collective-permute-done((bf16[512,1024]{1,0:T(8,128)(2,1)}, bf16[512,1024]{1,0:T(8,128)(2,1)S(1)}, u32[]{:S(2)}, u32[]{:S(2)}) %collective-permute-start.15) | collective-permute-done | bytes 1048608 | tf_op jit(solution)/shard_map/while/body/ppermute | solution.py:437
  398.5 3.4 convert_add_fusion.2
  401.9 2.8 broadcast_select_fusion.15
  404.7 4.3 %maximum_convert_fusion.2 = f32[1024,2048]{1,0:T(8,128)} fusion(bf16[512,2048]{1,0:T(8,128)(2,1)S(1)} %get-tuple-element.982, bf16[512,2048]{1,0:T(8,128)(2,1)S(1)} %get-tuple-element.983), kind=kLoop, calls=%fused_computation.29.clone.1 | loop fusion | flops 8388608 | bytes 12582912 | tf_op jit(solution)/shard_map/while/body/convert_element_type | solution.py:1130
  411.0 2.9 convert_element_type.180
  413.9 1.6 convert_element_type.181
  415.5 1.6 convert_element_type.182
  417.2 1.6 convert_element_type.183
  (204 shorter events, 49.9 us)
Async XLA Ops:
  7.2 100.1 %all-gather.3.cloned.1.call-start = ((), (), s32[]{:S(2)}) async-start(), calls=%async_computation.1 | async-start | bytes 8912896 | tf_op jit(solution)/shard_map/all_gather | solution.py:980
  7.2 18.0 %copy-start.34 = (bf16[2048]{0:T(1024)(128)(2,1)S(1)}, bf16[2048]{0:T(1024)(128)(2,1)}, u32[]{:S(2)}) copy-start(bf16[2048]{0:T(1024)(128)(2,1)} %param.35) | copy-start | bytes 12292
  7.3 19.8 %copy-start.45 = (s32[1,6]{1,0:T(1,128)S(1)}, s32[1,6]{1,0:T(1,128)}, u32[]{:S(2)}) copy-start(s32[1,6]{1,0:T(1,128)} %param.23) | copy-start | bytes 76
  7.3 19.9 %copy-start.40 = (bf16[512]{0:T(512)(128)(2,1)S(1)}, bf16[512]{0:T(512)(128)(2,1)}, u32[]{:S(2)}) copy-start(bf16[512]{0:T(512)(128)(2,1)} %param.29) | copy-start | bytes 3076
  7.3 19.9 %copy-start.41 = (bf16[512]{0:T(512)(128)(2,1)S(1)}, bf16[512]{0:T(512)(128)(2,1)}, u32[]{:S(2)}) copy-start(bf16[512]{0:T(512)(128)(2,1)} %param.26) | copy-start | bytes 3076
  7.3 20.5 %copy-start.5 = (bf16[1024,512]{1,0:T(8,128)(2,1)S(1)}, bf16[1024,512]{1,0:T(8,128)(2,1)}, u32[]{:S(2)}) copy-start(bf16[1024,512]{1,0:T(8,128)(2,1)} %param.27) | copy-start | bytes 3145732
  9.2 15.1 %collective-permute-start.16 = (bf16[128,2048]{1,0:T(8,128)(2,1)}, bf16[128,2048]{1,0:T(8,128)(2,1)S(1)}, u32[]{:S(2)}, u32[]{:S(2)}) collective-permute-start(bf16[128,2048]{1,0:T(8,128)(2,1)} %pack_weights.1), channel_id=1, source_target_pairs={{0,1},{1,0},{2,3},{3,2},{4,5},{5,4},{6,7},{7,6},{8,9},{9,8},{10,11... | collective-permute-start | bytes 1572872 | tf_op jit(solution)/shard_map/ppermute | solution.py:437
  25.2 239.9 %all-reduce.4.cloned.1.call-start = ((), (), s32[]{:S(2)}) async-start(), calls=%async_computation | async-start | bytes 8388608 | tf_op jit(solution)/shard_map/psum | solution.py:1033
  25.2 22.1 %collective-permute-start.20 = (bf16[2048]{0:T(1024)(128)(2,1)S(1)}, bf16[2048]{0:T(1024)(128)(2,1)S(1)}, u32[]{:S(2)}, u32[]{:S(2)}) collective-permute-start(bf16[2048]{0:T(1024)(128)(2,1)S(1)} %copy-done.34), channel_id=1, source_target_pairs={{0,1},{1,0},{2,3},{3,2},{4,5},{5,4},{6,7},{7,6},{8,9},{9,8},{10,11... | collective-permute-start | bytes 12296 | tf_op jit(solution)/shard_map/ppermute | solution.py:437
  27.4 24.1 %collective-permute-start.17 = (bf16[512,1024]{1,0:T(8,128)(2,1)}, bf16[512,1024]{1,0:T(8,128)(2,1)}, u32[]{:S(2)}, u32[]{:S(2)}) collective-permute-start(bf16[512,1024]{1,0:T(8,128)(2,1)} %tokens_ref.1), channel_id=1, source_target_pairs={{0,1},{1,0},{2,3},{3,2},{4,5},{5,4},{6,7},{7,6},{8,9},{9,8},{10,11... | collective-permute-start | bytes 3145736 | tf_op jit(solution)/shard_map/ppermute | solution.py:437
  29.7 3.2 copy-start.3
  32.9 2.9 copy-start.35
  32.9 3.5 copy-start.30
  32.9 4.1 copy-start.36
  32.9 5.6 %copy-start.37 = (bf16[1024]{0:T(1024)(128)(2,1)S(1)}, bf16[1024]{0:T(1024)(128)(2,1)}, u32[]{:S(2)}) copy-start(bf16[1024]{0:T(1024)(128)(2,1)} %param.37) | copy-start | bytes 6148
  32.9 6.2 %copy-start.38 = (bf16[1024]{0:T(1024)(128)(2,1)S(1)}, bf16[1024]{0:T(1024)(128)(2,1)}, u32[]{:S(2)}) copy-start(bf16[1024]{0:T(1024)(128)(2,1)} %param.38) | copy-start | bytes 6148
  32.9 6.7 %copy-start.39 = (bf16[1024]{0:T(1024)(128)(2,1)S(1)}, bf16[1024]{0:T(1024)(128)(2,1)}, u32[]{:S(2)}) copy-start(bf16[1024]{0:T(1024)(128)(2,1)} %param.39) | copy-start | bytes 6148
  51.5 26.3 %collective-permute-start.18 = (bf16[512,1024]{1,0:T(8,128)(2,1)}, bf16[512,1024]{1,0:T(8,128)(2,1)S(1)}, u32[]{:S(2)}, u32[]{:S(2)}) collective-permute-start(bf16[512,1024]{1,0:T(8,128)(2,1)} %w_own_ref.1), channel_id=1, source_target_pairs={{0,1},{1,0},{2,3},{3,2},{4,5},{5,4},{6,7},{7,6},{8,9},{9,8},{10,11... | collective-permute-start | bytes 3145736 | tf_op jit(solution)/shard_map/ppermute | solution.py:437
  56.6 11.3 %copy-start.23 = (bf16[1024,512]{1,0:T(8,128)(2,1)}, bf16[1024,512]{1,0:T(8,128)(2,1)S(1)}, u32[]{:S(2)}) copy-start(bf16[1024,512]{1,0:T(8,128)(2,1)S(1)} %get-tuple-element.1014.k_ref) | copy-start | bytes 3145732
  56.6 11.3 %copy-start.25 = (bf16[1024,512]{1,0:T(8,128)(2,1)}, bf16[1024,512]{1,0:T(8,128)(2,1)S(1)}, u32[]{:S(2)}) copy-start(bf16[1024,512]{1,0:T(8,128)(2,1)S(1)} %get-tuple-element.1015.v_ref) | copy-start | bytes 3145732
  67.8 11.1 %copy-start.24 = (bf16[1024,512]{1,0:T(8,128)(2,1)S(1)}, bf16[1024,512]{1,0:T(8,128)(2,1)}, u32[]{:S(2)}) copy-start(bf16[1024,512]{1,0:T(8,128)(2,1)} %copy-done.23) | copy-start | bytes 3145732
  67.9 20.9 %collective-permute-start.19 = (bf16[512,512]{1,0:T(8,128)(2,1)S(1)}, bf16[512,512]{1,0:T(8,128)(2,1)}, u32[]{:S(2)}, u32[]{:S(2)}) collective-permute-start(bf16[512,512]{1,0:T(8,128)(2,1)S(1)} %get-tuple-element.340), channel_id=1, source_target_pairs={{0,1},{1,0},{2,3},{3,2},{4,5},{5,4},{6,7},{7,6},{8,9},{9,8},{10,11... | collective-permute-start | bytes 1572872 | tf_op jit(solution)/shard_map/ppermute | solution.py:437
  88.8 42.2 %copy-start.27 = (bf16[512,512]{1,0:T(8,128)(2,1)}, bf16[512,512]{1,0:T(8,128)(2,1)S(1)}, u32[]{:S(2)}) copy-start(bf16[512,512]{1,0:T(8,128)(2,1)S(1)} %get-tuple-element.1019.own_ref) | copy-start | bytes 1572868
  88.8 6.3 %copy-start.12 = (bf16[1024,2048]{1,0:T(8,128)(2,1)S(1)}, bf16[1024,2048]{1,0:T(8,128)(2,1)}, u32[]{:S(2)}) copy-start(bf16[1024,2048]{1,0:T(8,128)(2,1)} %up_ref.5) | copy-start | bytes 12582916
  94.4 24.3 %copy-start.13 = (bf16[512,1024]{1,0:T(8,128)(2,1)}, bf16[512,1024]{1,0:T(8,128)(2,1)S(1)}, u32[]{:S(2)}) copy-start(bf16[512,1024]{1,0:T(8,128)(2,1)S(1)} %get-tuple-element.1009.h_ref.refs_0_) | copy-start | bytes 3145732
  94.4 38.3 %collective-permute-start.21 = (bf16[512,1024]{1,0:T(8,128)(2,1)S(1)}, bf16[512,1024]{1,0:T(8,128)(2,1)}, u32[]{:S(2)}, u32[]{:S(2)}) collective-permute-start(bf16[512,1024]{1,0:T(8,128)(2,1)S(1)} %get-tuple-element.1009.h_ref.refs_0_), channel_id=1, source_target_pairs={{0,1},{1,0},{2,3},{3,2},{4,5},{5,4},{6,7},{7,6},{8,9},{9,8},{10,11... | collective-permute-start | bytes 3145736 | tf_op jit(solution)/shard_map/ppermute | solution.py:437
  117.3 15.3 %collective-permute-start.22 = (bf16[256,1024]{1,0:T(8,128)(2,1)}, bf16[256,1024]{1,0:T(8,128)(2,1)}, u32[]{:S(2)}, u32[]{:S(2)}) collective-permute-start(bf16[256,1024]{1,0:T(8,128)(2,1)} %get-tuple-element.361.refs_0_), channel_id=1, source_target_pairs={{0,1},{1,0},{2,3},{3,2},{4,5},{5,4},{6,7},{7,6},{8,9},{9,8},{10,11... | collective-permute-start | bytes 1572872 | tf_op jit(solution)/shard_map/ppermute | solution.py:437
  128.7 3.3 copy-start.8
  128.7 3.3 copy-start.17
  128.7 3.3 copy-start.32
  128.7 3.3 copy-start.33
  128.7 12.9 %collective-permute-start.23 = (bf16[256,1024]{1,0:T(8,128)(2,1)}, bf16[256,1024]{1,0:T(8,128)(2,1)}, u32[]{:S(2)}, u32[]{:S(2)}) collective-permute-start(bf16[256,1024]{1,0:T(8,128)(2,1)} %get-tuple-element.362.refs_1_), channel_id=1, source_target_pairs={{0,1},{1,0},{2,3},{3,2},{4,5},{5,4},{6,7},{7,6},{8,9},{9,8},{10,11... | collective-permute-start | bytes 1572872 | tf_op jit(solution)/shard_map/ppermute | solution.py:437
  150.0 6.1 %copy-start = (bf16[1024,1024]{1,0:T(8,128)(2,1)S(1)}, bf16[1024,1024]{1,0:T(8,128)(2,1)}, u32[]{:S(2)}) copy-start(bf16[1024,1024]{1,0:T(8,128)(2,1)} %pad_maximum_fusion.5) | copy-start | bytes 6291460
  150.0 261.0 %all-reduce.6.cloned.1.call-start = ((), (), s32[]{:S(2)}) async-start(), calls=%async_computation.2 | async-start | bytes 8388608 | tf_op jit(solution)/shard_map/psum | solution.py:1101
  156.1 103.8 %copy-start.31 = (f32[3072]{0:T(1024)S(1)}, f32[3072]{0:T(1024)}, u32[]{:S(2)}) copy-start(f32[3072]{0:T(1024)} %reshape.217) | copy-start | bytes 36868
  156.8 19.6 %copy-start.44 = (bf16[512,1024]{1,0:T(8,128)(2,1)S(1)}, bf16[512,1024]{1,0:T(8,128)(2,1)}, u32[]{:S(2)}) copy-start(bf16[512,1024]{1,0:T(8,128)(2,1)} %get-tuple-element.1098) | copy-start | bytes 3145732 | tf_op jit(solution)/shard_map/while
  176.4 3.0 copy-start.42
  176.4 3.0 copy-start.46
  195.2 4.5 %collective-permute-start.1 = (bf16[512,2048]{1,0:T(8,128)(2,1)}, bf16[512,2048]{1,0:T(8,128)(2,1)}, u32[]{:S(2)}, u32[]{:S(2)}) collective-permute-start(bf16[512,2048]{1,0:T(8,128)(2,1)} %constant_dynamic-slice_fusion.8), channel_id=1, source_target_pairs={{0,2},{2,0},{4,6},{6,4},{8,10},{10,8},{12,14},{14,12},{16,18},{18,... | collective-permute-start | bytes 6291464 | tf_op jit(solution)/shard_map/while/body/ppermute | solution.py:928
  195.2 15.0 %collective-permute-start = (bf16[512,512]{1,0:T(8,128)(2,1)}, bf16[512,512]{1,0:T(8,128)(2,1)}, u32[]{:S(2)}, u32[]{:S(2)}) collective-permute-start(bf16[512,512]{1,0:T(8,128)(2,1)} %convolution_convert_fusion.11), channel_id=1, source_target_pairs={{0,1},{1,0},{2,3},{3,2},{4,5},{5,4},{6,7},{7,6},{8,9},{9,8},{10,11... | collective-permute-start | bytes 1572872 | tf_op jit(solution)/shard_map/while/body/ppermute | solution.py:437
  205.1 33.5 %collective-permute-start.2 = (bf16[256,2048]{1,0:T(8,128)(2,1)}, bf16[256,2048]{1,0:T(8,128)(2,1)}, u32[]{:S(2)}, u32[]{:S(2)}) collective-permute-start(bf16[256,2048]{1,0:T(8,128)(2,1)} %constant_dynamic-slice_fusion.9), channel_id=1, source_target_pairs={{0,4},{2,6},{4,0},{6,2},{8,12},{10,14},{12,8},{14,10},{16,20},{18,... | collective-permute-start | bytes 3145736 | tf_op jit(solution)/shard_map/while/body/ppermute | solution.py:928
  206.6 50.1 %collective-permute-start.3 = (bf16[512,1024]{1,0:T(8,128)(2,1)}, bf16[512,1024]{1,0:T(8,128)(2,1)}, u32[]{:S(2)}, u32[]{:S(2)}) collective-permute-start(bf16[512,1024]{1,0:T(8,128)(2,1)} %convolution_convert_fusion.13), channel_id=1, source_target_pairs={{0,1},{1,0},{2,3},{3,2},{4,5},{5,4},{6,7},{7,6},{8,9},{9,8},{10,11... | collective-permute-start | bytes 3145736 | tf_op jit(solution)/shard_map/while/body/ppermute | solution.py:437
  208.1 3.3 copy-start.21
  208.1 3.3 copy-start.22
  211.4 27.2 %copy-start.2 = (bf16[512,2048]{1,0:T(8,128)(2,1)S(1)}, bf16[512,2048]{1,0:T(8,128)(2,1)}, u32[]{:S(2)}) copy-start(bf16[512,2048]{1,0:T(8,128)(2,1)} %copy-done.1) | copy-start | bytes 6291460 | tf_op jit(solution)/shard_map/while
  238.6 2.7 copy-start.4
  254.6 2.1 copy-start.47
  258.9 9.8 %copy-start.16 = (bf16[512,1024]{1,0:T(8,128)(2,1)}, bf16[512,1024]{1,0:T(8,128)(2,1)S(1)}, u32[]{:S(2)}) copy-start(bf16[512,1024]{1,0:T(8,128)(2,1)S(1)} %get-tuple-element.393) | copy-start | bytes 3145732
  259.0 8.5 %copy-start.14 = (bf16[1024,512]{0,1:T(8,128)(2,1)S(1)}, bf16[1024,512]{0,1:T(8,128)(2,1)}, u32[]{:S(2)}) copy-start(bf16[1024,512]{0,1:T(8,128)(2,1)} %get-tuple-element.391) | copy-start | bytes 3145732
  265.1 3.7 copy-start.15
  271.3 23.4 %collective-permute-start.4 = (bf16[128,2048]{1,0:T(8,128)(2,1)S(1)}, bf16[128,2048]{1,0:T(8,128)(2,1)S(1)}, u32[]{:S(2)}, u32[]{:S(2)}) collective-permute-start(bf16[128,2048]{1,0:T(8,128)(2,1)S(1)} %constant_dynamic-slice_fusion.10), channel_id=1, source_target_pairs={{0,8},{2,10},{4,12},{6,14},{8,0},{10,2},{12,4},{14,6},{16,24},{18,... | collective-permute-start | bytes 1572872 | tf_op jit(solution)/shard_map/while/body/ppermute | solution.py:928
  272.6 8.5 %collective-permute-start.5 = (f32[6144]{0:T(1024)S(1)}, f32[6144]{0:T(1024)S(1)}, u32[]{:S(2)}, u32[]{:S(2)}) collective-permute-start(f32[6144]{0:T(1024)S(1)} %slice.115), channel_id=1, source_target_pairs={{0,1},{1,0},{2,3},{3,2},{4,5},{5,4},{6,7},{7,6},{8,9},{9,8},{10,11... | collective-permute-start | bytes 73736 | tf_op jit(solution)/shard_map/while/body/ppermute | solution.py:437
  281.1 14.4 %collective-permute-start.7 = (f32[9216]{0:T(1024)S(1)}, f32[9216]{0:T(1024)S(1)}, u32[]{:S(2)}, u32[]{:S(2)}) collective-permute-start(f32[9216]{0:T(1024)S(1)} %pad_maximum_fusion.19), channel_id=1, source_target_pairs={{0,2},{2,0},{4,6},{6,4},{8,10},{10,8},{12,14},{14,12},{16,18},{18,... | collective-permute-start | bytes 110600 | tf_op jit(solution)/shard_map/while/body/ppermute | solution.py:1123
  294.9 20.7 %collective-permute-start.6 = (bf16[64,2048]{1,0:T(8,128)(2,1)S(1)}, bf16[64,2048]{1,0:T(8,128)(2,1)S(1)}, u32[]{:S(2)}, u32[]{:S(2)}) collective-permute-start(bf16[64,2048]{1,0:T(8,128)(2,1)S(1)} %constant_dynamic-slice_fusion.11), channel_id=1, source_target_pairs={{0,16},{2,18},{4,20},{6,22},{8,24},{10,26},{12,28},{14,30},{16,0},... | collective-permute-start | bytes 786440 | tf_op jit(solution)/shard_map/while/body/ppermute | solution.py:928
  315.7 15.6 %collective-permute-start.8 = (bf16[64,2048]{1,0:T(8,128)(2,1)S(1)}, bf16[64,2048]{1,0:T(8,128)(2,1)S(1)}, u32[]{:S(2)}, u32[]{:S(2)}) collective-permute-start(bf16[64,2048]{1,0:T(8,128)(2,1)S(1)} %add_convert_fusion.17), channel_id=1, source_target_pairs={{0,16},{2,18},{4,20},{6,22},{8,24},{10,26},{12,28},{14,30},{16,0},... | collective-permute-start | bytes 786440 | tf_op jit(solution)/shard_map/while/body/ppermute | solution.py:928
  315.7 4.0 collective-permute-start.9
  331.3 12.2 %collective-permute-start.10 = (bf16[128,2048]{1,0:T(8,128)(2,1)S(1)}, bf16[128,2048]{1,0:T(8,128)(2,1)S(1)}, u32[]{:S(2)}, u32[]{:S(2)}) collective-permute-start(bf16[128,2048]{1,0:T(8,128)(2,1)S(1)} %pad_maximum_fusion.20), channel_id=1, source_target_pairs={{0,8},{2,10},{4,12},{6,14},{8,0},{10,2},{12,4},{14,6},{16,24},{18,... | collective-permute-start | bytes 1572872 | tf_op jit(solution)/shard_map/while/body/ppermute | solution.py:928
  331.4 12.1 %collective-permute-start.11 = (f32[9216]{0:T(1024)S(1)}, f32[9216]{0:T(1024)S(1)}, u32[]{:S(2)}, u32[]{:S(2)}) collective-permute-start(f32[9216]{0:T(1024)S(1)} %add.215), channel_id=1, source_target_pairs={{0,8},{2,10},{4,12},{6,14},{8,0},{10,2},{12,4},{14,6},{16,24},{18,... | collective-permute-start | bytes 110600 | tf_op jit(solution)/shard_map/while/body/ppermute | solution.py:1123
  343.9 25.7 %collective-permute-start.12 = (bf16[256,2048]{1,0:T(8,128)(2,1)S(1)}, bf16[256,2048]{1,0:T(8,128)(2,1)}, u32[]{:S(2)}, u32[]{:S(2)}) collective-permute-start(bf16[256,2048]{1,0:T(8,128)(2,1)S(1)} %pad_maximum_fusion.21), channel_id=1, source_target_pairs={{0,4},{2,6},{4,0},{6,2},{8,12},{10,14},{12,8},{14,10},{16,20},{18,... | collective-permute-start | bytes 3145736 | tf_op jit(solution)/shard_map/while/body/ppermute | solution.py:928
  349.0 5.2 %collective-permute-start.13 = (f32[9216]{0:T(1024)S(1)}, f32[9216]{0:T(1024)S(1)}, u32[]{:S(2)}, u32[]{:S(2)}) collective-permute-start(f32[9216]{0:T(1024)S(1)} %add.216), channel_id=1, source_target_pairs={{0,16},{2,18},{4,20},{6,22},{8,24},{10,26},{12,28},{14,30},{16,0},... | collective-permute-start | bytes 110600 | tf_op jit(solution)/shard_map/while/body/ppermute | solution.py:1123
  372.7 29.2 %collective-permute-start.14 = (bf16[512,2048]{1,0:T(8,128)(2,1)}, bf16[512,2048]{1,0:T(8,128)(2,1)}, u32[]{:S(2)}, u32[]{:S(2)}) collective-permute-start(bf16[512,2048]{1,0:T(8,128)(2,1)} %pad_maximum_fusion.22), channel_id=1, source_target_pairs={{0,2},{2,0},{4,6},{6,4},{8,10},{10,8},{12,14},{14,12},{16,18},{18,... | collective-permute-start | bytes 6291464 | tf_op jit(solution)/shard_map/while/body/ppermute | solution.py:928
  372.7 25.8 %collective-permute-start.15 = (bf16[512,1024]{1,0:T(8,128)(2,1)}, bf16[512,1024]{1,0:T(8,128)(2,1)S(1)}, u32[]{:S(2)}, u32[]{:S(2)}) collective-permute-start(bf16[512,1024]{1,0:T(8,128)(2,1)} %get-tuple-element.980), channel_id=1, source_target_pairs={{0,1},{1,0},{2,3},{3,2},{4,5},{5,4},{6,7},{7,6},{8,9},{9,8},{10,11... | collective-permute-start | bytes 3145736 | tf_op jit(solution)/shard_map/while/body/ppermute | solution.py:437
  404.7 4.3 %copy-start.11 = (bf16[256,2048]{1,0:T(8,128)(2,1)S(1)}, bf16[256,2048]{1,0:T(8,128)(2,1)}, u32[]{:S(2)}) copy-start(bf16[256,2048]{1,0:T(8,128)(2,1)} %get-tuple-element.1209) | copy-start | bytes 3145732 | tf_op jit(solution)/shard_map/while
  411.0 2.9 copy-start.20
  (11 other events, 15.9 us)
Sparse Core Ops, SparseCore 0:
  25.3 76.3 all-gather.2
  150.1 114.9 all-reduce.3
  270.3 140.6 all-reduce.5

commit v4 on v3

--- a/solution.py
+++ b/solution.py
@@ -55,7 +55,7 @@
     lse_ref[...] = jnp.transpose(stats)[: lse_ref.shape[0], :]
 
 
-def attention_forward(queries, key_rows, values, row_segment, segment, block=256):
+def attention_forward(queries, key_rows, values, row_segment, segment, block=512):
     rows, width = queries.shape
     length = key_rows.shape[0]
     pairs = width // LANES

time: 429 us -> 428 us (level)
  transfers between devices with their start and end apart: 27 -> 27, of which waited for: 15 -> 15; matrix products, arithmetic and copies ran while one was open for 24% -> 24% of each run, Pallas kernels for 29% -> 28%
where the time goes in v4:
time: 428 us; the launch traced here: 424 us
  waiting for transfers between devices  132 us (31%)
  Pallas kernels  131 us (31%)
  other arithmetic  51.9 us (12%)
  matrix products  36.5 us (9%)
  local copies, waits for them, and re-layouts  30.8 us (7%)
  starting transfers between devices  27 us (6%)
  between operations  14.4 us (3%)
    ppermute x8, waiting for transfers between devices, push(): self.flying = (kind, bit, kept, lax.ppermute(sent, 'dp', perm))  60.5 us
    ppermute x12, waiting for transfers between devices, swap(): return lax.ppermute(rows, 'mp', [(0, 1), (1, 0)])  49.4 us
    pallas_call x1, Pallas kernels, attention_backward(): pl.pallas_call(functools.partial(backward_kernel, pairs, at * (heads // o...  27.2 us
    pallas_call x2, Pallas kernels, forward_other(): pl.pallas_call(body, grid=(units // UNITS,), in_specs=[part(depth), up, p...  20 us
    pallas_call x1, Pallas kernels, backward_rows(): pl.pallas_call(functools.partial(backward_rows_kernel, half), grid=(2 * h...  19.5 us
    ppermute x4, waiting for transfers between devices, last_part(): lax.ppermute(short, 'dp', [(at, at ^ 1 << step) for at in range(count)])  18.4 us
    ppermute x12, starting transfers between devices, swap(): return lax.ppermute(rows, 'mp', [(0, 1), (1, 0)])  15.3 us
    pallas_call x2, Pallas kernels, attention_forward(): pl.pallas_call(functools.partial(forward_kernel, pairs), grid=(rows // bl...  15 us
  transfers between devices with their start and end apart: 27, of which 15 were waited for; matrix products, arithmetic and copies ran while one was open for 24% of the time, Pallas kernels for 28%

profile of v4, /device:TPU:0, one launch (start us, length us, event | category | flops | bytes accessed | tf_op | source)
XLA Modules:
  0.0 423.8 jit_solution(10602846868177843022)
XLA Ops:
  7.3 1.9 pack_weights.1
  9.2 2.9 collective-permute-start.16
  12.2 12.1 %collective-permute-done.16 = bf16[128,2048]{1,0:T(8,128)(2,1)S(1)} collective-permute-done((bf16[128,2048]{1,0:T(8,128)(2,1)}, bf16[128,2048]{1,0:T(8,128)(2,1)S(1)}, u32[]{:S(2)}, u32[]{:S(2)}) %collective-permute-start.16) | collective-permute-done | bytes 524320 | tf_op jit(solution)/shard_map/ppermute | solution.py:437
  25.2 1.8 collective-permute-start.20
  27.8 1.9 convolution_convert_fusion.7
  29.7 3.1 fusion.15
  32.9 2.1 fusion.14.q_ref
  40.2 2.3 copy.60
  42.5 2.3 copy.61
  44.8 2.4 copy.62
  47.9 3.6 collective-permute-done.17
  52.1 2.2 fusion.16
  54.4 2.0 convolution_convert_fusion.6
  56.6 2.7 fusion.17.q_ref
  59.3 6.8 %attention_forward.2 = (bf16[512,512]{1,0:T(8,128)(2,1)S(1)}, f32[8,512]{1,0:T(8,128)S(1)}) custom-call(bf16[512,512]{1,0:T(8,128)(2,1)S(1)} %fusion.17.q_ref, bf16[1024,512]{1,0:T(8,128)(2,1)S(1)} %get-tuple-element.1014.k_ref, bf16[1024,512]{1,0:T(8,128)(2,1)S(1)} %get-tuple-element.1015.v_ref, s32[1,1024]{1,0:T(1,128)S(1)} %bitcast.119, ...), custom_call_target="tpu_custom_call" | custom-call | flops 4294967296 | tf_op jit(solution)/shard_map/attention_forward/pallas_call | solution.py:64
  67.5 3.0 pad_maximum_fusion.5
  70.5 7.2 %collective-permute-done.18.w_other_ref = bf16[512,1024]{1,0:T(8,128)(2,1)S(1)} collective-permute-done((bf16[512,1024]{1,0:T(8,128)(2,1)}, bf16[512,1024]{1,0:T(8,128)(2,1)S(1)}, u32[]{:S(2)}, u32[]{:S(2)}) %collective-permute-start.18) | collective-permute-done | bytes 1048608 | tf_op jit(solution)/shard_map/ppermute | solution.py:437
  78.9 8.2 %attention_forward.3 = (bf16[512,512]{1,0:T(8,128)(2,1)S(1)}, f32[8,512]{1,0:T(8,128)S(1)}) custom-call(bf16[512,512]{1,0:T(8,128)(2,1)S(1)} %fusion.14.q_ref, bf16[1024,512]{1,0:T(8,128)(2,1)S(1)} %copy-done.24, bf16[1024,512]{1,0:T(8,128)(2,1)} %copy-done.25, s32[1,1024]{1,0:T(1,128)S(1)} %bitcast.120, s32[512,1]{1,0:T(8,128)S(1)} %copy.57.col_ref), custom_call_target="tpu_custom_call" | custom-call | flops 4294967296 | tf_op jit(solution)/shard_map/attention_forward/pallas_call | solution.py:64
  87.2 5.6 %middle_norm.1 = (f32[512,1024]{1,0:T(8,128)}, bf16[512,1024]{1,0:T(8,128)(2,1)S(1)}, f32[512,1024]{1,0:T(8,128)}, f32[512,1]{1,0:T(8,128)}) custom-call(bf16[512,512]{1,0:T(8,128)(2,1)S(1)} %get-tuple-element.1019.own_ref, bf16[512,512]{1,0:T(8,128)(2,1)} %collective-permute-done.19.here_ref, bf16[512,1024]{1,0:T(8,128)(2,1)} %w_own_ref.1, ...), custom_call_target="tpu_custom_call" | custom-call | flops 2147483648 | tf_op jit(solution)/shard_map/middle_norm/pallas_call | solution.py:529
  93.5 11.7 %forward_own.1 = (bf16[512,2048]{1,0:T(8,128)(2,1)}, bf16[512,2048]{1,0:T(8,128)(2,1)}, f32[512,1024]{1,0:T(8,128)}) custom-call(bf16[512,1024]{1,0:T(8,128)(2,1)S(1)} %get-tuple-element.1009.h_ref.refs_0_, bf16[1024,2048]{1,0:T(8,128)(2,1)S(1)} %copy-done.12, f32[1,2048]{1,0:T(1,128)} %bitcast.132, bf16[2048,1024]{1,0:T(8,128)(2,1)} %down_ref.1), custom_call_target="tpu_custom_call" | custom-call | flops 6442450944 | tf_op jit(solution)/shard_map/forward_own/pallas_call | solution.py:576
  105.2 10.0 %forward_other.2 = (bf16[512,2048]{1,0:T(8,128)(2,1)S(1)}, bf16[512,1024]{1,0:T(8,128)(2,1)}, f32[512,1024]{1,0:T(8,128)S(1)}, bf16[256,1024]{1,0:T(8,128)(2,1)}, f32[8,1024]{1,0:T(8,128)}) custom-call(bf16[512,1024]{1,0:T(8,128)(2,1)S(1)} %get-tuple-element.1009.h_ref.refs_0_, bf16[16,2,64,2048]{3,2,1,0:T(8,128)(2,1)} %bitcast.113, f32[1,2048]{1,0:T(1,128)} %bitcast.124, ...), custom_call_target="tpu_custom_call" | custom-call | flops 4294967296 | tf_op jit(solution)/shard_map/forward_other/pallas_call | solution.py:667
  116.6 10.0 %forward_other.3 = (bf16[512,2048]{1,0:T(8,128)(2,1)S(1)}, bf16[512,1024]{1,0:T(8,128)(2,1)}, f32[512,1024]{1,0:T(8,128)S(1)}, bf16[256,1024]{1,0:T(8,128)(2,1)}, f32[8,1024]{1,0:T(8,128)}) custom-call(bf16[512,1024]{1,0:T(8,128)(2,1)S(1)} %get-tuple-element.1009.h_ref.refs_0_, ...), custom_call_target="tpu_custom_call", output_to_operand_aliasing={{0}: (11, {}), {1}: (12, {}), {2}: (13, {})} | custom-call | flops 4294967296 | tf_op jit(solution)/shard_map/forward_other/pallas_call | solution.py:667
  130.6 9.4 %gelu_rows.1 = (bf16[512,2048]{1,0:T(8,128)(2,1)}, bf16[512,2048]{1,0:T(8,128)(2,1)}) custom-call(bf16[512,1024]{1,0:T(8,128)(2,1)} %collective-permute-done.21.h_ref, bf16[1024,2048]{1,0:T(8,128)(2,1)} %up_ref.5, f32[1,2048]{1,0:T(1,128)} %bitcast.133), custom_call_target="tpu_custom_call" | custom-call | flops 524288 | tf_op jit(solution)/shard_map/gelu_rows/pallas_call | solution.py:793
  140.0 8.4 %down_grad.1 = bf16[2048,1024]{1,0:T(8,128)(2,1)} custom-call(bf16[512,2048]{1,0:T(8,128)(2,1)} %get-tuple-element.358.own_ref, bf16[512,2048]{1,0:T(8,128)(2,1)} %get-tuple-element.360.other_ref, bf16[256,1024]{1,0:T(8,128)(2,1)} %get-tuple-element.361.refs_0_, bf16[256,1024]{1,0:T(8,128)(2,1)} %get-tuple-element.362.refs_1_, ...), custom_call_target="tpu_custom_call" | custom-call | flops 4294967296 | tf_op jit(solution)/shard_map/down_grad/pallas_call | solution.py:828
  149.8 2.3 pad_maximum_fusion.9
  154.5 102.9 %while.46 = (s32[]{:T(128)}, bf16[1024,512]{0,1:T(8,128)(2,1)}, bf16[1024,512]{0,1:T(8,128)(2,1)}, bf16[1024,512]{0,1:T(8,128)(2,1)}, bf16[512,1024]{1,0:T(8,128...) while((s32[]{:T(128)}, bf16[1024,512]{0,1:T(8,128)(2,1)}, ...), condition=%wide.region_5.6_spmd, body=%wide.region_2.0_spmd.sunk | while | flops 30082596864 | bytes 159403200 | solution.py:1050
  155.2 19.5 %backward_rows.1 = (bf16[512,2048]{1,0:T(8,128)(2,1)}, f32[512,1024]{1,0:T(8,128)}, bf16[512,1024]{1,0:T(8,128)(2,1)}, f32[8,1024]{1,0:T(8,128)}) custom-call(bf16[512,1024]{1,0:T(8,128)(2,1)S(1)} %get-tuple-element.1034.f_ref, bf16[512,2048]{1,0:T(8,128)(2,1)} %get-tuple-element.1090.slope_own_ref, bf16[512,2048]{1,0:T(8,128)(2,1)} %get-tuple-element.1091.slope_other_ref, ...), custom_call_target="tpu_custom_call" | custom-call | flops 10737418240 | tf_op jit(solution)/shard_map/while/body/backward_rows/pallas_call | solution.py:756
  174.8 2.9 convolution_convert_fusion.11
  178.5 12.0 %up_grad.1 = (bf16[1024,2048]{1,0:T(8,128)(2,1)}, f32[1,2048]{1,0:T(1,128)}) custom-call(bf16[512,1024]{1,0:T(8,128)(2,1)} %get-tuple-element.941.f_ref, bf16[2048,1024]{1,0:T(8,128)(2,1)} %get-tuple-element.1093.down_ref, bf16[512,2048]{1,0:T(8,128)(2,1)} %get-tuple-element.1100.slope_ref, bf16[512,2048]{1,0:T(8,128)(2,1)} %get-tuple-element.942.d_pre_ref, ...), custom_call_target="tpu_custom_call" | custom-call | flops 6442450944 | tf_op jit(solution)/shard_map/while/body/up_grad/pallas_call | solution.py:861
  190.5 3.2 constant_dynamic-slice_fusion.8
  194.8 3.2 convolution_convert_fusion.13
  198.1 3.0 add_convert_fusion.12
  203.5 1.5 collective-permute-start.2
  206.5 2.2 collective-permute-done
  209.8 27.2 %attention_backward.1 = (bf16[1024,512]{1,0:T(8,128)(2,1)S(1)}, bf16[1024,512]{1,0:T(8,128)(2,1)S(1)}, bf16[1024,512]{1,0:T(8,128)(2,1)S(1)}) custom-call(bf16[1024,512]{1,0:T(8,128)(2,1)S(1)} %copy-done.21, bf16[1024,512]{1,0:T(8,128)(2,1)} %get-tuple-element.1106.k_ref, bf16[1024,512]{1,0:T(8,128)(2,1)} %get-tuple-element.1107.v_ref, ...), custom_call_target="tpu_custom_call" | custom-call | flops 4294967296 | tf_op jit(solution)/shard_map/while/body/attention_backward/pallas_call | solution.py:152
  237.1 2.7 add_convert_fusion.13
  243.2 2.3 fusion.113
  245.5 2.3 fusion.114
  247.8 2.2 fusion.115
  251.3 1.7 add_convert_fusion.15
  253.0 2.1 add_add_fusion.2
  255.1 2.0 add_convert_fusion.14
  260.4 3.1 all-reduce.4.cloned.1.call-done
  263.4 2.4 copy.63
  269.7 137.7 %while.47 = (s32[]{:T(128)}, f32[1024,2048]{1,0:T(8,128)}, f32[2048,1024]{1,0:T(8,128)}, f32[9216]{0:T(1024)S(1)}, f32[512,1024]{1,0:T(8,128)}, /*index=5*/s32[]...) while((s32[]{:T(128)}, f32[1024,2048]{1,0:T(8,128)}, ...), condition=%wide.region_8.9_spmd, body=%wide.region_7.8_spmd.sunk | while | flops 31780900 | bytes 86025256 | solution.py:1050
  272.4 7.0 %convert_element_type.278 = f32[2048,1024]{1,0:T(8,128)} convert(bf16[2048,1024]{1,0:T(8,128)(2,1)} %get-tuple-element.968) | non-fusion elementwise | flops 2097152 | bytes 12582912 | tf_op jit(solution)/shard_map/while/body/convert_element_type | solution.py:1113
  279.6 13.5 %collective-permute-done.4 = bf16[128,2048]{1,0:T(8,128)(2,1)S(1)} collective-permute-done((bf16[128,2048]{1,0:T(8,128)(2,1)S(1)}, bf16[128,2048]{1,0:T(8,128)(2,1)S(1)}, u32[]{:S(2)}, u32[]{:S(2)}) %collective-permute-start.4) | collective-permute-done | bytes 524320 | tf_op jit(solution)/shard_map/while/body/ppermute | solution.py:928
  293.9 20.1 %collective-permute-done.6 = bf16[64,2048]{1,0:T(8,128)(2,1)S(1)} collective-permute-done((bf16[64,2048]{1,0:T(8,128)(2,1)S(1)}, bf16[64,2048]{1,0:T(8,128)(2,1)S(1)}, u32[]{:S(2)}, u32[]{:S(2)}) %collective-permute-start.6) | collective-permute-done | bytes 262176 | tf_op jit(solution)/shard_map/while/body/ppermute | solution.py:928
  314.2 3.9 collective-permute-done.9
  318.1 11.5 %collective-permute-done.8 = bf16[64,2048]{1,0:T(8,128)(2,1)S(1)} collective-permute-done((bf16[64,2048]{1,0:T(8,128)(2,1)S(1)}, bf16[64,2048]{1,0:T(8,128)(2,1)S(1)}, u32[]{:S(2)}, u32[]{:S(2)}) %collective-permute-start.8) | collective-permute-done | bytes 262176 | tf_op jit(solution)/shard_map/while/body/ppermute | solution.py:928
  329.8 2.0 collective-permute-start.11
  331.8 10.1 %collective-permute-done.11 = f32[9216]{0:T(1024)S(1)} collective-permute-done((f32[9216]{0:T(1024)S(1)}, f32[9216]{0:T(1024)S(1)}, u32[]{:S(2)}, u32[]{:S(2)}) %collective-permute-start.11) | collective-permute-done | bytes 36896 | tf_op jit(solution)/shard_map/while/body/ppermute | solution.py:1123
  342.3 5.1 %collective-permute-start.12 = (bf16[256,2048]{1,0:T(8,128)(2,1)S(1)}, bf16[256,2048]{1,0:T(8,128)(2,1)}, u32[]{:S(2)}, u32[]{:S(2)}) collective-permute-start(bf16[256,2048]{1,0:T(8,128)(2,1)S(1)} %pad_maximum_fusion.21), channel_id=1, source_target_pairs={{0,4},{2,6},{4,0},{6,2},{8,12},{10,14},{12,8},{14,10},{16,20},{18,... | collective-permute-start | bytes 3145736 | tf_op jit(solution)/shard_map/while/body/ppermute | solution.py:928
  348.2 4.4 %collective-permute-done.13 = f32[9216]{0:T(1024)S(1)} collective-permute-done((f32[9216]{0:T(1024)S(1)}, f32[9216]{0:T(1024)S(1)}, u32[]{:S(2)}, u32[]{:S(2)}) %collective-permute-start.13) | collective-permute-done | bytes 36896 | tf_op jit(solution)/shard_map/while/body/ppermute | solution.py:1123
  352.7 15.3 %collective-permute-done.12 = bf16[256,2048]{1,0:T(8,128)(2,1)} collective-permute-done((bf16[256,2048]{1,0:T(8,128)(2,1)S(1)}, bf16[256,2048]{1,0:T(8,128)(2,1)}, u32[]{:S(2)}, u32[]{:S(2)}) %collective-permute-start.12) | collective-permute-done | bytes 1048608 | tf_op jit(solution)/shard_map/while/body/ppermute | solution.py:928
  367.9 1.7 broadcast_select_fusion.14
  372.6 24.3 %collective-permute-done.15 = bf16[512,1024]{1,0:T(8,128)(2,1)S(1)} collective-permute-done((bf16[512,1024]{1,0:T(8,128)(2,1)}, bf16[512,1024]{1,0:T(8,128)(2,1)S(1)}, u32[]{:S(2)}, u32[]{:S(2)}) %collective-permute-start.15) | collective-permute-done | bytes 1048608 | tf_op jit(solution)/shard_map/while/body/ppermute | solution.py:437
  396.9 3.4 convert_add_fusion.2
  400.3 2.8 broadcast_select_fusion.15
  403.1 4.3 %maximum_convert_fusion.2 = f32[1024,2048]{1,0:T(8,128)} fusion(bf16[512,2048]{1,0:T(8,128)(2,1)S(1)} %get-tuple-element.982, bf16[512,2048]{1,0:T(8,128)(2,1)S(1)} %get-tuple-element.983), kind=kLoop, calls=%fused_computation.29.clone.1 | loop fusion | flops 8388608 | bytes 12582912 | tf_op jit(solution)/shard_map/while/body/convert_element_type | solution.py:1130
  409.3 2.9 convert_element_type.180
  412.3 1.6 convert_element_type.181
  413.9 1.6 convert_element_type.182
  415.5 1.6 convert_element_type.183
  (204 shorter events, 49.9 us)
Async XLA Ops:
  7.2 98.0 %all-gather.3.cloned.1.call-start = ((), (), s32[]{:S(2)}) async-start(), calls=%async_computation.1 | async-start | bytes 8912896 | tf_op jit(solution)/shard_map/all_gather | solution.py:980
  7.2 18.0 %copy-start.34 = (bf16[2048]{0:T(1024)(128)(2,1)S(1)}, bf16[2048]{0:T(1024)(128)(2,1)}, u32[]{:S(2)}) copy-start(bf16[2048]{0:T(1024)(128)(2,1)} %param.35) | copy-start | bytes 12292
  7.3 19.8 %copy-start.45 = (s32[1,6]{1,0:T(1,128)S(1)}, s32[1,6]{1,0:T(1,128)}, u32[]{:S(2)}) copy-start(s32[1,6]{1,0:T(1,128)} %param.23) | copy-start | bytes 76
  7.3 19.9 %copy-start.40 = (bf16[512]{0:T(512)(128)(2,1)S(1)}, bf16[512]{0:T(512)(128)(2,1)}, u32[]{:S(2)}) copy-start(bf16[512]{0:T(512)(128)(2,1)} %param.29) | copy-start | bytes 3076
  7.3 19.9 %copy-start.41 = (bf16[512]{0:T(512)(128)(2,1)S(1)}, bf16[512]{0:T(512)(128)(2,1)}, u32[]{:S(2)}) copy-start(bf16[512]{0:T(512)(128)(2,1)} %param.26) | copy-start | bytes 3076
  7.3 20.5 %copy-start.5 = (bf16[1024,512]{1,0:T(8,128)(2,1)S(1)}, bf16[1024,512]{1,0:T(8,128)(2,1)}, u32[]{:S(2)}) copy-start(bf16[1024,512]{1,0:T(8,128)(2,1)} %param.27) | copy-start | bytes 3145732
  9.2 15.1 %collective-permute-start.16 = (bf16[128,2048]{1,0:T(8,128)(2,1)}, bf16[128,2048]{1,0:T(8,128)(2,1)S(1)}, u32[]{:S(2)}, u32[]{:S(2)}) collective-permute-start(bf16[128,2048]{1,0:T(8,128)(2,1)} %pack_weights.1), channel_id=1, source_target_pairs={{0,1},{1,0},{2,3},{3,2},{4,5},{5,4},{6,7},{7,6},{8,9},{9,8},{10,11... | collective-permute-start | bytes 1572872 | tf_op jit(solution)/shard_map/ppermute | solution.py:437
  25.2 238.3 %all-reduce.4.cloned.1.call-start = ((), (), s32[]{:S(2)}) async-start(), calls=%async_computation | async-start | bytes 8388608 | tf_op jit(solution)/shard_map/psum | solution.py:1033
  25.2 22.1 %collective-permute-start.20 = (bf16[2048]{0:T(1024)(128)(2,1)S(1)}, bf16[2048]{0:T(1024)(128)(2,1)S(1)}, u32[]{:S(2)}, u32[]{:S(2)}) collective-permute-start(bf16[2048]{0:T(1024)(128)(2,1)S(1)} %copy-done.34), channel_id=1, source_target_pairs={{0,1},{1,0},{2,3},{3,2},{4,5},{5,4},{6,7},{7,6},{8,9},{9,8},{10,11... | collective-permute-start | bytes 12296 | tf_op jit(solution)/shard_map/ppermute | solution.py:437
  27.4 24.1 %collective-permute-start.17 = (bf16[512,1024]{1,0:T(8,128)(2,1)}, bf16[512,1024]{1,0:T(8,128)(2,1)}, u32[]{:S(2)}, u32[]{:S(2)}) collective-permute-start(bf16[512,1024]{1,0:T(8,128)(2,1)} %tokens_ref.1), channel_id=1, source_target_pairs={{0,1},{1,0},{2,3},{3,2},{4,5},{5,4},{6,7},{7,6},{8,9},{9,8},{10,11... | collective-permute-start | bytes 3145736 | tf_op jit(solution)/shard_map/ppermute | solution.py:437
  29.7 3.2 copy-start.3
  32.9 2.9 copy-start.35
  32.9 3.5 copy-start.30
  32.9 4.1 copy-start.36
  32.9 5.6 %copy-start.37 = (bf16[1024]{0:T(1024)(128)(2,1)S(1)}, bf16[1024]{0:T(1024)(128)(2,1)}, u32[]{:S(2)}) copy-start(bf16[1024]{0:T(1024)(128)(2,1)} %param.37) | copy-start | bytes 6148
  32.9 6.2 %copy-start.38 = (bf16[1024]{0:T(1024)(128)(2,1)S(1)}, bf16[1024]{0:T(1024)(128)(2,1)}, u32[]{:S(2)}) copy-start(bf16[1024]{0:T(1024)(128)(2,1)} %param.38) | copy-start | bytes 6148
  32.9 6.7 %copy-start.39 = (bf16[1024]{0:T(1024)(128)(2,1)S(1)}, bf16[1024]{0:T(1024)(128)(2,1)}, u32[]{:S(2)}) copy-start(bf16[1024]{0:T(1024)(128)(2,1)} %param.39) | copy-start | bytes 6148
  51.5 26.3 %collective-permute-start.18 = (bf16[512,1024]{1,0:T(8,128)(2,1)}, bf16[512,1024]{1,0:T(8,128)(2,1)S(1)}, u32[]{:S(2)}, u32[]{:S(2)}) collective-permute-start(bf16[512,1024]{1,0:T(8,128)(2,1)} %w_own_ref.1), channel_id=1, source_target_pairs={{0,1},{1,0},{2,3},{3,2},{4,5},{5,4},{6,7},{7,6},{8,9},{9,8},{10,11... | collective-permute-start | bytes 3145736 | tf_op jit(solution)/shard_map/ppermute | solution.py:437
  56.6 9.5 %copy-start.23 = (bf16[1024,512]{1,0:T(8,128)(2,1)}, bf16[1024,512]{1,0:T(8,128)(2,1)S(1)}, u32[]{:S(2)}) copy-start(bf16[1024,512]{1,0:T(8,128)(2,1)S(1)} %get-tuple-element.1014.k_ref) | copy-start | bytes 3145732
  56.6 9.5 %copy-start.25 = (bf16[1024,512]{1,0:T(8,128)(2,1)}, bf16[1024,512]{1,0:T(8,128)(2,1)S(1)}, u32[]{:S(2)}) copy-start(bf16[1024,512]{1,0:T(8,128)(2,1)S(1)} %get-tuple-element.1015.v_ref) | copy-start | bytes 3145732
  66.1 12.9 %copy-start.24 = (bf16[1024,512]{1,0:T(8,128)(2,1)S(1)}, bf16[1024,512]{1,0:T(8,128)(2,1)}, u32[]{:S(2)}) copy-start(bf16[1024,512]{1,0:T(8,128)(2,1)} %copy-done.23) | copy-start | bytes 3145732
  66.1 21.1 %collective-permute-start.19 = (bf16[512,512]{1,0:T(8,128)(2,1)S(1)}, bf16[512,512]{1,0:T(8,128)(2,1)}, u32[]{:S(2)}, u32[]{:S(2)}) collective-permute-start(bf16[512,512]{1,0:T(8,128)(2,1)S(1)} %get-tuple-element.340), channel_id=1, source_target_pairs={{0,1},{1,0},{2,3},{3,2},{4,5},{5,4},{6,7},{7,6},{8,9},{9,8},{10,11... | collective-permute-start | bytes 1572872 | tf_op jit(solution)/shard_map/ppermute | solution.py:437
  87.2 41.7 %copy-start.27 = (bf16[512,512]{1,0:T(8,128)(2,1)}, bf16[512,512]{1,0:T(8,128)(2,1)S(1)}, u32[]{:S(2)}) copy-start(bf16[512,512]{1,0:T(8,128)(2,1)S(1)} %get-tuple-element.1019.own_ref) | copy-start | bytes 1572868
  87.2 6.3 %copy-start.12 = (bf16[1024,2048]{1,0:T(8,128)(2,1)S(1)}, bf16[1024,2048]{1,0:T(8,128)(2,1)}, u32[]{:S(2)}) copy-start(bf16[1024,2048]{1,0:T(8,128)(2,1)} %up_ref.5) | copy-start | bytes 12582916
  92.8 23.9 %copy-start.13 = (bf16[512,1024]{1,0:T(8,128)(2,1)}, bf16[512,1024]{1,0:T(8,128)(2,1)S(1)}, u32[]{:S(2)}) copy-start(bf16[512,1024]{1,0:T(8,128)(2,1)S(1)} %get-tuple-element.1009.h_ref.refs_0_) | copy-start | bytes 3145732
  92.8 37.8 %collective-permute-start.21 = (bf16[512,1024]{1,0:T(8,128)(2,1)S(1)}, bf16[512,1024]{1,0:T(8,128)(2,1)}, u32[]{:S(2)}, u32[]{:S(2)}) collective-permute-start(bf16[512,1024]{1,0:T(8,128)(2,1)S(1)} %get-tuple-element.1009.h_ref.refs_0_), channel_id=1, source_target_pairs={{0,1},{1,0},{2,3},{3,2},{4,5},{5,4},{6,7},{7,6},{8,9},{9,8},{10,11... | collective-permute-start | bytes 3145736 | tf_op jit(solution)/shard_map/ppermute | solution.py:437
  115.2 15.3 %collective-permute-start.22 = (bf16[256,1024]{1,0:T(8,128)(2,1)}, bf16[256,1024]{1,0:T(8,128)(2,1)}, u32[]{:S(2)}, u32[]{:S(2)}) collective-permute-start(bf16[256,1024]{1,0:T(8,128)(2,1)} %get-tuple-element.361.refs_0_), channel_id=1, source_target_pairs={{0,1},{1,0},{2,3},{3,2},{4,5},{5,4},{6,7},{7,6},{8,9},{9,8},{10,11... | collective-permute-start | bytes 1572872 | tf_op jit(solution)/shard_map/ppermute | solution.py:437
  126.6 3.3 copy-start.8
  126.6 3.3 copy-start.17
  126.6 3.3 copy-start.32
  126.6 3.3 copy-start.33
  126.6 13.3 %collective-permute-start.23 = (bf16[256,1024]{1,0:T(8,128)(2,1)}, bf16[256,1024]{1,0:T(8,128)(2,1)}, u32[]{:S(2)}, u32[]{:S(2)}) collective-permute-start(bf16[256,1024]{1,0:T(8,128)(2,1)} %get-tuple-element.362.refs_1_), channel_id=1, source_target_pairs={{0,1},{1,0},{2,3},{3,2},{4,5},{5,4},{6,7},{7,6},{8,9},{9,8},{10,11... | collective-permute-start | bytes 1572872 | tf_op jit(solution)/shard_map/ppermute | solution.py:437
  148.4 6.1 %copy-start = (bf16[1024,1024]{1,0:T(8,128)(2,1)S(1)}, bf16[1024,1024]{1,0:T(8,128)(2,1)}, u32[]{:S(2)}) copy-start(bf16[1024,1024]{1,0:T(8,128)(2,1)} %pad_maximum_fusion.5) | copy-start | bytes 6291460
  148.4 260.9 %all-reduce.6.cloned.1.call-start = ((), (), s32[]{:S(2)}) async-start(), calls=%async_computation.2 | async-start | bytes 8388608 | tf_op jit(solution)/shard_map/psum | solution.py:1101
  154.5 103.8 %copy-start.31 = (f32[3072]{0:T(1024)S(1)}, f32[3072]{0:T(1024)}, u32[]{:S(2)}) copy-start(f32[3072]{0:T(1024)} %reshape.217) | copy-start | bytes 36868
  155.2 19.5 %copy-start.44 = (bf16[512,1024]{1,0:T(8,128)(2,1)S(1)}, bf16[512,1024]{1,0:T(8,128)(2,1)}, u32[]{:S(2)}) copy-start(bf16[512,1024]{1,0:T(8,128)(2,1)} %get-tuple-element.1098) | copy-start | bytes 3145732 | tf_op jit(solution)/shard_map/while
  174.7 3.0 copy-start.42
  174.8 3.0 copy-start.46
  193.6 4.5 %collective-permute-start.1 = (bf16[512,2048]{1,0:T(8,128)(2,1)}, bf16[512,2048]{1,0:T(8,128)(2,1)}, u32[]{:S(2)}, u32[]{:S(2)}) collective-permute-start(bf16[512,2048]{1,0:T(8,128)(2,1)} %constant_dynamic-slice_fusion.8), channel_id=1, source_target_pairs={{0,2},{2,0},{4,6},{6,4},{8,10},{10,8},{12,14},{14,12},{16,18},{18,... | collective-permute-start | bytes 6291464 | tf_op jit(solution)/shard_map/while/body/ppermute | solution.py:928
  193.6 15.0 %collective-permute-start = (bf16[512,512]{1,0:T(8,128)(2,1)}, bf16[512,512]{1,0:T(8,128)(2,1)}, u32[]{:S(2)}, u32[]{:S(2)}) collective-permute-start(bf16[512,512]{1,0:T(8,128)(2,1)} %convolution_convert_fusion.11), channel_id=1, source_target_pairs={{0,1},{1,0},{2,3},{3,2},{4,5},{5,4},{6,7},{7,6},{8,9},{9,8},{10,11... | collective-permute-start | bytes 1572872 | tf_op jit(solution)/shard_map/while/body/ppermute | solution.py:437
  203.5 33.5 %collective-permute-start.2 = (bf16[256,2048]{1,0:T(8,128)(2,1)}, bf16[256,2048]{1,0:T(8,128)(2,1)}, u32[]{:S(2)}, u32[]{:S(2)}) collective-permute-start(bf16[256,2048]{1,0:T(8,128)(2,1)} %constant_dynamic-slice_fusion.9), channel_id=1, source_target_pairs={{0,4},{2,6},{4,0},{6,2},{8,12},{10,14},{12,8},{14,10},{16,20},{18,... | collective-permute-start | bytes 3145736 | tf_op jit(solution)/shard_map/while/body/ppermute | solution.py:928
  205.1 50.0 %collective-permute-start.3 = (bf16[512,1024]{1,0:T(8,128)(2,1)}, bf16[512,1024]{1,0:T(8,128)(2,1)}, u32[]{:S(2)}, u32[]{:S(2)}) collective-permute-start(bf16[512,1024]{1,0:T(8,128)(2,1)} %convolution_convert_fusion.13), channel_id=1, source_target_pairs={{0,1},{1,0},{2,3},{3,2},{4,5},{5,4},{6,7},{7,6},{8,9},{9,8},{10,11... | collective-permute-start | bytes 3145736 | tf_op jit(solution)/shard_map/while/body/ppermute | solution.py:437
  206.5 3.3 copy-start.21
  206.5 3.3 copy-start.22
  209.8 27.3 %copy-start.2 = (bf16[512,2048]{1,0:T(8,128)(2,1)S(1)}, bf16[512,2048]{1,0:T(8,128)(2,1)}, u32[]{:S(2)}) copy-start(bf16[512,2048]{1,0:T(8,128)(2,1)} %copy-done.1) | copy-start | bytes 6291460 | tf_op jit(solution)/shard_map/while
  237.1 2.7 copy-start.4
  253.0 2.1 copy-start.47
  257.3 9.8 %copy-start.16 = (bf16[512,1024]{1,0:T(8,128)(2,1)}, bf16[512,1024]{1,0:T(8,128)(2,1)S(1)}, u32[]{:S(2)}) copy-start(bf16[512,1024]{1,0:T(8,128)(2,1)S(1)} %get-tuple-element.393) | copy-start | bytes 3145732
  257.4 8.5 %copy-start.14 = (bf16[1024,512]{0,1:T(8,128)(2,1)S(1)}, bf16[1024,512]{0,1:T(8,128)(2,1)}, u32[]{:S(2)}) copy-start(bf16[1024,512]{0,1:T(8,128)(2,1)} %get-tuple-element.391) | copy-start | bytes 3145732
  263.4 3.7 copy-start.15
  269.7 23.4 %collective-permute-start.4 = (bf16[128,2048]{1,0:T(8,128)(2,1)S(1)}, bf16[128,2048]{1,0:T(8,128)(2,1)S(1)}, u32[]{:S(2)}, u32[]{:S(2)}) collective-permute-start(bf16[128,2048]{1,0:T(8,128)(2,1)S(1)} %constant_dynamic-slice_fusion.10), channel_id=1, source_target_pairs={{0,8},{2,10},{4,12},{6,14},{8,0},{10,2},{12,4},{14,6},{16,24},{18,... | collective-permute-start | bytes 1572872 | tf_op jit(solution)/shard_map/while/body/ppermute | solution.py:928
  271.0 8.5 %collective-permute-start.5 = (f32[6144]{0:T(1024)S(1)}, f32[6144]{0:T(1024)S(1)}, u32[]{:S(2)}, u32[]{:S(2)}) collective-permute-start(f32[6144]{0:T(1024)S(1)} %slice.115), channel_id=1, source_target_pairs={{0,1},{1,0},{2,3},{3,2},{4,5},{5,4},{6,7},{7,6},{8,9},{9,8},{10,11... | collective-permute-start | bytes 73736 | tf_op jit(solution)/shard_map/while/body/ppermute | solution.py:437
  279.5 14.4 %collective-permute-start.7 = (f32[9216]{0:T(1024)S(1)}, f32[9216]{0:T(1024)S(1)}, u32[]{:S(2)}, u32[]{:S(2)}) collective-permute-start(f32[9216]{0:T(1024)S(1)} %pad_maximum_fusion.19), channel_id=1, source_target_pairs={{0,2},{2,0},{4,6},{6,4},{8,10},{10,8},{12,14},{14,12},{16,18},{18,... | collective-permute-start | bytes 110600 | tf_op jit(solution)/shard_map/while/body/ppermute | solution.py:1123
  293.3 20.7 %collective-permute-start.6 = (bf16[64,2048]{1,0:T(8,128)(2,1)S(1)}, bf16[64,2048]{1,0:T(8,128)(2,1)S(1)}, u32[]{:S(2)}, u32[]{:S(2)}) collective-permute-start(bf16[64,2048]{1,0:T(8,128)(2,1)S(1)} %constant_dynamic-slice_fusion.11), channel_id=1, source_target_pairs={{0,16},{2,18},{4,20},{6,22},{8,24},{10,26},{12,28},{14,30},{16,0},... | collective-permute-start | bytes 786440 | tf_op jit(solution)/shard_map/while/body/ppermute | solution.py:928
  314.0 15.6 %collective-permute-start.8 = (bf16[64,2048]{1,0:T(8,128)(2,1)S(1)}, bf16[64,2048]{1,0:T(8,128)(2,1)S(1)}, u32[]{:S(2)}, u32[]{:S(2)}) collective-permute-start(bf16[64,2048]{1,0:T(8,128)(2,1)S(1)} %add_convert_fusion.17), channel_id=1, source_target_pairs={{0,16},{2,18},{4,20},{6,22},{8,24},{10,26},{12,28},{14,30},{16,0},... | collective-permute-start | bytes 786440 | tf_op jit(solution)/shard_map/while/body/ppermute | solution.py:928
  314.1 4.0 collective-permute-start.9
  329.7 12.2 %collective-permute-start.10 = (bf16[128,2048]{1,0:T(8,128)(2,1)S(1)}, bf16[128,2048]{1,0:T(8,128)(2,1)S(1)}, u32[]{:S(2)}, u32[]{:S(2)}) collective-permute-start(bf16[128,2048]{1,0:T(8,128)(2,1)S(1)} %pad_maximum_fusion.20), channel_id=1, source_target_pairs={{0,8},{2,10},{4,12},{6,14},{8,0},{10,2},{12,4},{14,6},{16,24},{18,... | collective-permute-start | bytes 1572872 | tf_op jit(solution)/shard_map/while/body/ppermute | solution.py:928
  329.8 12.1 %collective-permute-start.11 = (f32[9216]{0:T(1024)S(1)}, f32[9216]{0:T(1024)S(1)}, u32[]{:S(2)}, u32[]{:S(2)}) collective-permute-start(f32[9216]{0:T(1024)S(1)} %add.215), channel_id=1, source_target_pairs={{0,8},{2,10},{4,12},{6,14},{8,0},{10,2},{12,4},{14,6},{16,24},{18,... | collective-permute-start | bytes 110600 | tf_op jit(solution)/shard_map/while/body/ppermute | solution.py:1123
  342.3 25.7 %collective-permute-start.12 = (bf16[256,2048]{1,0:T(8,128)(2,1)S(1)}, bf16[256,2048]{1,0:T(8,128)(2,1)}, u32[]{:S(2)}, u32[]{:S(2)}) collective-permute-start(bf16[256,2048]{1,0:T(8,128)(2,1)S(1)} %pad_maximum_fusion.21), channel_id=1, source_target_pairs={{0,4},{2,6},{4,0},{6,2},{8,12},{10,14},{12,8},{14,10},{16,20},{18,... | collective-permute-start | bytes 3145736 | tf_op jit(solution)/shard_map/while/body/ppermute | solution.py:928
  347.4 5.3 %collective-permute-start.13 = (f32[9216]{0:T(1024)S(1)}, f32[9216]{0:T(1024)S(1)}, u32[]{:S(2)}, u32[]{:S(2)}) collective-permute-start(f32[9216]{0:T(1024)S(1)} %add.216), channel_id=1, source_target_pairs={{0,16},{2,18},{4,20},{6,22},{8,24},{10,26},{12,28},{14,30},{16,0},... | collective-permute-start | bytes 110600 | tf_op jit(solution)/shard_map/while/body/ppermute | solution.py:1123
  371.1 29.2 %collective-permute-start.14 = (bf16[512,2048]{1,0:T(8,128)(2,1)}, bf16[512,2048]{1,0:T(8,128)(2,1)}, u32[]{:S(2)}, u32[]{:S(2)}) collective-permute-start(bf16[512,2048]{1,0:T(8,128)(2,1)} %pad_maximum_fusion.22), channel_id=1, source_target_pairs={{0,2},{2,0},{4,6},{6,4},{8,10},{10,8},{12,14},{14,12},{16,18},{18,... | collective-permute-start | bytes 6291464 | tf_op jit(solution)/shard_map/while/body/ppermute | solution.py:928
  371.1 25.8 %collective-permute-start.15 = (bf16[512,1024]{1,0:T(8,128)(2,1)}, bf16[512,1024]{1,0:T(8,128)(2,1)S(1)}, u32[]{:S(2)}, u32[]{:S(2)}) collective-permute-start(bf16[512,1024]{1,0:T(8,128)(2,1)} %get-tuple-element.980), channel_id=1, source_target_pairs={{0,1},{1,0},{2,3},{3,2},{4,5},{5,4},{6,7},{7,6},{8,9},{9,8},{10,11... | collective-permute-start | bytes 3145736 | tf_op jit(solution)/shard_map/while/body/ppermute | solution.py:437
  403.1 4.3 %copy-start.11 = (bf16[256,2048]{1,0:T(8,128)(2,1)S(1)}, bf16[256,2048]{1,0:T(8,128)(2,1)}, u32[]{:S(2)}) copy-start(bf16[256,2048]{1,0:T(8,128)(2,1)} %get-tuple-element.1209) | copy-start | bytes 3145732 | tf_op jit(solution)/shard_map/while
  409.3 2.9 copy-start.20
  (11 other events, 15.9 us)
Sparse Core Ops, SparseCore 0:
  25.3 76.3 all-gather.2
  148.5 114.8 all-reduce.3
  268.6 140.6 all-reduce.5

commit v5 on v4

--- a/solution.py
+++ b/solution.py
@@ -139,7 +139,7 @@
 
 
 def attention_backward(
-    queries, key_rows, values, d_context, context, lse, segment, at, of, block=256
+    queries, key_rows, values, d_context, context, lse, segment, at, of, block=512
 ):
     rows, width = queries.shape
     length = key_rows.shape[0]

time: 428 us -> 428 us (level)
  no operation moved by 1% of the time
where the time goes in v5:
time: 428 us; the launch traced here: 424 us
  waiting for transfers between devices  132 us (31%)
  Pallas kernels  131 us (31%)
  other arithmetic  51.9 us (12%)
  matrix products  36.5 us (9%)
  local copies, waits for them, and re-layouts  30.9 us (7%)
  starting transfers between devices  27.1 us (6%)
  between operations  14.6 us (3%)
    ppermute x8, waiting for transfers between devices, push(): self.flying = (kind, bit, kept, lax.ppermute(sent, 'dp', perm))  60.5 us
    ppermute x12, waiting for transfers between devices, swap(): return lax.ppermute(rows, 'mp', [(0, 1), (1, 0)])  49.4 us
    pallas_call x1, Pallas kernels, attention_backward(): pl.pallas_call(functools.partial(backward_kernel, pairs, at * (heads // o...  26.9 us
    pallas_call x2, Pallas kernels, forward_other(): pl.pallas_call(body, grid=(units // UNITS,), in_specs=[part(depth), up, p...  20 us
    pallas_call x1, Pallas kernels, backward_rows(): pl.pallas_call(functools.partial(backward_rows_kernel, half), grid=(2 * h...  19.5 us
    ppermute x4, waiting for transfers between devices, last_part(): lax.ppermute(short, 'dp', [(at, at ^ 1 << step) for at in range(count)])  18.4 us
    ppermute x12, starting transfers between devices, swap(): return lax.ppermute(rows, 'mp', [(0, 1), (1, 0)])  15.3 us
    pallas_call x2, Pallas kernels, attention_forward(): pl.pallas_call(functools.partial(forward_kernel, pairs), grid=(rows // bl...  15.1 us
  transfers between devices with their start and end apart: 27, of which 15 were waited for; matrix products, arithmetic and copies ran while one was open for 24% of the time, Pallas kernels for 28%

profile of v5, /device:TPU:0, one launch (start us, length us, event | category | flops | bytes accessed | tf_op | source)
XLA Modules:
  0.0 424.1 jit_solution(17820119056906809376)
XLA Ops:
  7.3 1.9 pack_weights.1
  9.2 2.9 collective-permute-start.16
  12.2 12.1 %collective-permute-done.16 = bf16[128,2048]{1,0:T(8,128)(2,1)S(1)} collective-permute-done((bf16[128,2048]{1,0:T(8,128)(2,1)}, bf16[128,2048]{1,0:T(8,128)(2,1)S(1)}, u32[]{:S(2)}, u32[]{:S(2)}) %collective-permute-start.16) | collective-permute-done | bytes 524320 | tf_op jit(solution)/shard_map/ppermute | solution.py:437
  25.2 1.8 collective-permute-start.20
  27.8 1.9 convolution_convert_fusion.7
  29.7 3.1 fusion.15
  32.9 2.1 fusion.14.q_ref
  40.2 2.3 copy.60
  42.5 2.3 copy.61
  44.8 2.5 copy.62
  47.9 3.5 collective-permute-done.17
  52.1 2.2 fusion.16
  54.4 2.0 convolution_convert_fusion.6
  56.6 2.7 fusion.17.q_ref
  59.3 6.8 %attention_forward.2 = (bf16[512,512]{1,0:T(8,128)(2,1)S(1)}, f32[8,512]{1,0:T(8,128)S(1)}) custom-call(bf16[512,512]{1,0:T(8,128)(2,1)S(1)} %fusion.17.q_ref, bf16[1024,512]{1,0:T(8,128)(2,1)S(1)} %get-tuple-element.1014.k_ref, bf16[1024,512]{1,0:T(8,128)(2,1)S(1)} %get-tuple-element.1015.v_ref, s32[1,1024]{1,0:T(1,128)S(1)} %bitcast.119, ...), custom_call_target="tpu_custom_call" | custom-call | flops 4294967296 | tf_op jit(solution)/shard_map/attention_forward/pallas_call | solution.py:64
  67.5 3.0 pad_maximum_fusion.5
  70.5 7.2 %collective-permute-done.18.w_other_ref = bf16[512,1024]{1,0:T(8,128)(2,1)S(1)} collective-permute-done((bf16[512,1024]{1,0:T(8,128)(2,1)}, bf16[512,1024]{1,0:T(8,128)(2,1)S(1)}, u32[]{:S(2)}, u32[]{:S(2)}) %collective-permute-start.18) | collective-permute-done | bytes 1048608 | tf_op jit(solution)/shard_map/ppermute | solution.py:437
  78.9 8.3 %attention_forward.3 = (bf16[512,512]{1,0:T(8,128)(2,1)S(1)}, f32[8,512]{1,0:T(8,128)S(1)}) custom-call(bf16[512,512]{1,0:T(8,128)(2,1)S(1)} %fusion.14.q_ref, bf16[1024,512]{1,0:T(8,128)(2,1)S(1)} %copy-done.24, bf16[1024,512]{1,0:T(8,128)(2,1)} %copy-done.25, s32[1,1024]{1,0:T(1,128)S(1)} %bitcast.120, s32[512,1]{1,0:T(8,128)S(1)} %copy.57.col_ref), custom_call_target="tpu_custom_call" | custom-call | flops 4294967296 | tf_op jit(solution)/shard_map/attention_forward/pallas_call | solution.py:64
  87.2 5.6 %middle_norm.1 = (f32[512,1024]{1,0:T(8,128)}, bf16[512,1024]{1,0:T(8,128)(2,1)S(1)}, f32[512,1024]{1,0:T(8,128)}, f32[512,1]{1,0:T(8,128)}) custom-call(bf16[512,512]{1,0:T(8,128)(2,1)S(1)} %get-tuple-element.1019.own_ref, bf16[512,512]{1,0:T(8,128)(2,1)} %collective-permute-done.19.here_ref, bf16[512,1024]{1,0:T(8,128)(2,1)} %w_own_ref.1, ...), custom_call_target="tpu_custom_call" | custom-call | flops 2147483648 | tf_op jit(solution)/shard_map/middle_norm/pallas_call | solution.py:529
  93.5 11.7 %forward_own.1 = (bf16[512,2048]{1,0:T(8,128)(2,1)}, bf16[512,2048]{1,0:T(8,128)(2,1)}, f32[512,1024]{1,0:T(8,128)}) custom-call(bf16[512,1024]{1,0:T(8,128)(2,1)S(1)} %get-tuple-element.1009.h_ref.refs_0_, bf16[1024,2048]{1,0:T(8,128)(2,1)S(1)} %copy-done.12, f32[1,2048]{1,0:T(1,128)} %bitcast.132, bf16[2048,1024]{1,0:T(8,128)(2,1)} %down_ref.1), custom_call_target="tpu_custom_call" | custom-call | flops 6442450944 | tf_op jit(solution)/shard_map/forward_own/pallas_call | solution.py:576
  105.3 10.0 %forward_other.2 = (bf16[512,2048]{1,0:T(8,128)(2,1)S(1)}, bf16[512,1024]{1,0:T(8,128)(2,1)}, f32[512,1024]{1,0:T(8,128)S(1)}, bf16[256,1024]{1,0:T(8,128)(2,1)}, f32[8,1024]{1,0:T(8,128)}) custom-call(bf16[512,1024]{1,0:T(8,128)(2,1)S(1)} %get-tuple-element.1009.h_ref.refs_0_, bf16[16,2,64,2048]{3,2,1,0:T(8,128)(2,1)} %bitcast.113, f32[1,2048]{1,0:T(1,128)} %bitcast.124, ...), custom_call_target="tpu_custom_call" | custom-call | flops 4294967296 | tf_op jit(solution)/shard_map/forward_other/pallas_call | solution.py:667
  116.6 10.0 %forward_other.3 = (bf16[512,2048]{1,0:T(8,128)(2,1)S(1)}, bf16[512,1024]{1,0:T(8,128)(2,1)}, f32[512,1024]{1,0:T(8,128)S(1)}, bf16[256,1024]{1,0:T(8,128)(2,1)}, f32[8,1024]{1,0:T(8,128)}) custom-call(bf16[512,1024]{1,0:T(8,128)(2,1)S(1)} %get-tuple-element.1009.h_ref.refs_0_, ...), custom_call_target="tpu_custom_call", output_to_operand_aliasing={{0}: (11, {}), {1}: (12, {}), {2}: (13, {})} | custom-call | flops 4294967296 | tf_op jit(solution)/shard_map/forward_other/pallas_call | solution.py:667
  130.6 9.5 %gelu_rows.1 = (bf16[512,2048]{1,0:T(8,128)(2,1)}, bf16[512,2048]{1,0:T(8,128)(2,1)}) custom-call(bf16[512,1024]{1,0:T(8,128)(2,1)} %collective-permute-done.21.h_ref, bf16[1024,2048]{1,0:T(8,128)(2,1)} %up_ref.5, f32[1,2048]{1,0:T(1,128)} %bitcast.133), custom_call_target="tpu_custom_call" | custom-call | flops 524288 | tf_op jit(solution)/shard_map/gelu_rows/pallas_call | solution.py:793
  140.1 8.4 %down_grad.1 = bf16[2048,1024]{1,0:T(8,128)(2,1)} custom-call(bf16[512,2048]{1,0:T(8,128)(2,1)} %get-tuple-element.358.own_ref, bf16[512,2048]{1,0:T(8,128)(2,1)} %get-tuple-element.360.other_ref, bf16[256,1024]{1,0:T(8,128)(2,1)} %get-tuple-element.361.refs_0_, bf16[256,1024]{1,0:T(8,128)(2,1)} %get-tuple-element.362.refs_1_, ...), custom_call_target="tpu_custom_call" | custom-call | flops 4294967296 | tf_op jit(solution)/shard_map/down_grad/pallas_call | solution.py:828
  149.9 2.3 pad_maximum_fusion.9
  154.6 102.6 %while.46 = (s32[]{:T(128)}, bf16[1024,512]{0,1:T(8,128)(2,1)}, bf16[1024,512]{0,1:T(8,128)(2,1)}, bf16[1024,512]{0,1:T(8,128)(2,1)}, bf16[512,1024]{1,0:T(8,128...) while((s32[]{:T(128)}, bf16[1024,512]{0,1:T(8,128)(2,1)}, ...), condition=%wide.region_5.6_spmd, body=%wide.region_2.0_spmd.sunk | while | flops 30082596864 | bytes 159403200 | solution.py:1050
  155.3 19.5 %backward_rows.1 = (bf16[512,2048]{1,0:T(8,128)(2,1)}, f32[512,1024]{1,0:T(8,128)}, bf16[512,1024]{1,0:T(8,128)(2,1)}, f32[8,1024]{1,0:T(8,128)}) custom-call(bf16[512,1024]{1,0:T(8,128)(2,1)S(1)} %get-tuple-element.1034.f_ref, bf16[512,2048]{1,0:T(8,128)(2,1)} %get-tuple-element.1090.slope_own_ref, bf16[512,2048]{1,0:T(8,128)(2,1)} %get-tuple-element.1091.slope_other_ref, ...), custom_call_target="tpu_custom_call" | custom-call | flops 10737418240 | tf_op jit(solution)/shard_map/while/body/backward_rows/pallas_call | solution.py:756
  174.9 2.9 convolution_convert_fusion.11
  178.6 12.0 %up_grad.1 = (bf16[1024,2048]{1,0:T(8,128)(2,1)}, f32[1,2048]{1,0:T(1,128)}) custom-call(bf16[512,1024]{1,0:T(8,128)(2,1)} %get-tuple-element.941.f_ref, bf16[2048,1024]{1,0:T(8,128)(2,1)} %get-tuple-element.1093.down_ref, bf16[512,2048]{1,0:T(8,128)(2,1)} %get-tuple-element.1100.slope_ref, bf16[512,2048]{1,0:T(8,128)(2,1)} %get-tuple-element.942.d_pre_ref, ...), custom_call_target="tpu_custom_call" | custom-call | flops 6442450944 | tf_op jit(solution)/shard_map/while/body/up_grad/pallas_call | solution.py:861
  190.5 3.2 constant_dynamic-slice_fusion.8
  194.9 3.2 convolution_convert_fusion.13
  198.2 3.0 add_convert_fusion.12
  203.6 1.6 collective-permute-start.2
  206.6 2.1 collective-permute-done
  209.9 26.9 %attention_backward.1 = (bf16[1024,512]{1,0:T(8,128)(2,1)S(1)}, bf16[1024,512]{1,0:T(8,128)(2,1)S(1)}, bf16[1024,512]{1,0:T(8,128)(2,1)S(1)}) custom-call(bf16[1024,512]{1,0:T(8,128)(2,1)S(1)} %copy-done.21, bf16[1024,512]{1,0:T(8,128)(2,1)} %get-tuple-element.1106.k_ref, bf16[1024,512]{1,0:T(8,128)(2,1)} %get-tuple-element.1107.v_ref, ...), custom_call_target="tpu_custom_call" | custom-call | flops 4294967296 | tf_op jit(solution)/shard_map/while/body/attention_backward/pallas_call | solution.py:152
  236.9 2.7 add_convert_fusion.13
  243.1 2.3 fusion.113
  245.3 2.3 fusion.114
  247.6 2.2 fusion.115
  251.1 1.7 add_convert_fusion.15
  252.8 2.1 add_add_fusion.2
  255.0 2.0 add_convert_fusion.14
  260.2 3.4 all-reduce.4.cloned.1.call-done
  263.6 2.4 copy.63
  269.8 137.7 %while.47 = (s32[]{:T(128)}, f32[1024,2048]{1,0:T(8,128)}, f32[2048,1024]{1,0:T(8,128)}, f32[9216]{0:T(1024)S(1)}, f32[512,1024]{1,0:T(8,128)}, /*index=5*/s32[]...) while((s32[]{:T(128)}, f32[1024,2048]{1,0:T(8,128)}, ...), condition=%wide.region_8.9_spmd, body=%wide.region_7.8_spmd.sunk | while | flops 31780900 | bytes 86025256 | solution.py:1050
  272.6 7.0 %convert_element_type.278 = f32[2048,1024]{1,0:T(8,128)} convert(bf16[2048,1024]{1,0:T(8,128)(2,1)} %get-tuple-element.968) | non-fusion elementwise | flops 2097152 | bytes 12582912 | tf_op jit(solution)/shard_map/while/body/convert_element_type | solution.py:1113
  279.7 13.6 %collective-permute-done.4 = bf16[128,2048]{1,0:T(8,128)(2,1)S(1)} collective-permute-done((bf16[128,2048]{1,0:T(8,128)(2,1)S(1)}, bf16[128,2048]{1,0:T(8,128)(2,1)S(1)}, u32[]{:S(2)}, u32[]{:S(2)}) %collective-permute-start.4) | collective-permute-done | bytes 524320 | tf_op jit(solution)/shard_map/while/body/ppermute | solution.py:928
  294.1 20.1 %collective-permute-done.6 = bf16[64,2048]{1,0:T(8,128)(2,1)S(1)} collective-permute-done((bf16[64,2048]{1,0:T(8,128)(2,1)S(1)}, bf16[64,2048]{1,0:T(8,128)(2,1)S(1)}, u32[]{:S(2)}, u32[]{:S(2)}) %collective-permute-start.6) | collective-permute-done | bytes 262176 | tf_op jit(solution)/shard_map/while/body/ppermute | solution.py:928
  314.4 3.9 collective-permute-done.9
  318.3 11.5 %collective-permute-done.8 = bf16[64,2048]{1,0:T(8,128)(2,1)S(1)} collective-permute-done((bf16[64,2048]{1,0:T(8,128)(2,1)S(1)}, bf16[64,2048]{1,0:T(8,128)(2,1)S(1)}, u32[]{:S(2)}, u32[]{:S(2)}) %collective-permute-start.8) | collective-permute-done | bytes 262176 | tf_op jit(solution)/shard_map/while/body/ppermute | solution.py:928
  330.0 2.0 collective-permute-start.11
  332.0 10.1 %collective-permute-done.11 = f32[9216]{0:T(1024)S(1)} collective-permute-done((f32[9216]{0:T(1024)S(1)}, f32[9216]{0:T(1024)S(1)}, u32[]{:S(2)}, u32[]{:S(2)}) %collective-permute-start.11) | collective-permute-done | bytes 36896 | tf_op jit(solution)/shard_map/while/body/ppermute | solution.py:1123
  342.4 5.2 %collective-permute-start.12 = (bf16[256,2048]{1,0:T(8,128)(2,1)S(1)}, bf16[256,2048]{1,0:T(8,128)(2,1)}, u32[]{:S(2)}, u32[]{:S(2)}) collective-permute-start(bf16[256,2048]{1,0:T(8,128)(2,1)S(1)} %pad_maximum_fusion.21), channel_id=1, source_target_pairs={{0,4},{2,6},{4,0},{6,2},{8,12},{10,14},{12,8},{14,10},{16,20},{18,... | collective-permute-start | bytes 3145736 | tf_op jit(solution)/shard_map/while/body/ppermute | solution.py:928
  348.4 4.4 %collective-permute-done.13 = f32[9216]{0:T(1024)S(1)} collective-permute-done((f32[9216]{0:T(1024)S(1)}, f32[9216]{0:T(1024)S(1)}, u32[]{:S(2)}, u32[]{:S(2)}) %collective-permute-start.13) | collective-permute-done | bytes 36896 | tf_op jit(solution)/shard_map/while/body/ppermute | solution.py:1123
  352.8 15.2 %collective-permute-done.12 = bf16[256,2048]{1,0:T(8,128)(2,1)} collective-permute-done((bf16[256,2048]{1,0:T(8,128)(2,1)S(1)}, bf16[256,2048]{1,0:T(8,128)(2,1)}, u32[]{:S(2)}, u32[]{:S(2)}) %collective-permute-start.12) | collective-permute-done | bytes 1048608 | tf_op jit(solution)/shard_map/while/body/ppermute | solution.py:928
  368.1 1.7 broadcast_select_fusion.14
  372.7 24.3 %collective-permute-done.15 = bf16[512,1024]{1,0:T(8,128)(2,1)S(1)} collective-permute-done((bf16[512,1024]{1,0:T(8,128)(2,1)}, bf16[512,1024]{1,0:T(8,128)(2,1)S(1)}, u32[]{:S(2)}, u32[]{:S(2)}) %collective-permute-start.15) | collective-permute-done | bytes 1048608 | tf_op jit(solution)/shard_map/while/body/ppermute | solution.py:437
  397.1 3.4 convert_add_fusion.2
  400.4 2.8 broadcast_select_fusion.15
  403.2 4.3 %maximum_convert_fusion.2 = f32[1024,2048]{1,0:T(8,128)} fusion(bf16[512,2048]{1,0:T(8,128)(2,1)S(1)} %get-tuple-element.982, bf16[512,2048]{1,0:T(8,128)(2,1)S(1)} %get-tuple-element.983), kind=kLoop, calls=%fused_computation.29.clone.1 | loop fusion | flops 8388608 | bytes 12582912 | tf_op jit(solution)/shard_map/while/body/convert_element_type | solution.py:1130
  409.5 2.9 convert_element_type.180
  412.4 1.6 convert_element_type.181
  414.0 1.6 convert_element_type.182
  415.6 1.6 convert_element_type.183
  (204 shorter events, 49.9 us)
Async XLA Ops:
  7.2 98.1 %all-gather.3.cloned.1.call-start = ((), (), s32[]{:S(2)}) async-start(), calls=%async_computation.1 | async-start | bytes 8912896 | tf_op jit(solution)/shard_map/all_gather | solution.py:980
  7.2 18.0 %copy-start.34 = (bf16[2048]{0:T(1024)(128)(2,1)S(1)}, bf16[2048]{0:T(1024)(128)(2,1)}, u32[]{:S(2)}) copy-start(bf16[2048]{0:T(1024)(128)(2,1)} %param.35) | copy-start | bytes 12292
  7.3 19.8 %copy-start.45 = (s32[1,6]{1,0:T(1,128)S(1)}, s32[1,6]{1,0:T(1,128)}, u32[]{:S(2)}) copy-start(s32[1,6]{1,0:T(1,128)} %param.23) | copy-start | bytes 76
  7.3 19.9 %copy-start.40 = (bf16[512]{0:T(512)(128)(2,1)S(1)}, bf16[512]{0:T(512)(128)(2,1)}, u32[]{:S(2)}) copy-start(bf16[512]{0:T(512)(128)(2,1)} %param.29) | copy-start | bytes 3076
  7.3 19.9 %copy-start.41 = (bf16[512]{0:T(512)(128)(2,1)S(1)}, bf16[512]{0:T(512)(128)(2,1)}, u32[]{:S(2)}) copy-start(bf16[512]{0:T(512)(128)(2,1)} %param.26) | copy-start | bytes 3076
  7.3 20.5 %copy-start.5 = (bf16[1024,512]{1,0:T(8,128)(2,1)S(1)}, bf16[1024,512]{1,0:T(8,128)(2,1)}, u32[]{:S(2)}) copy-start(bf16[1024,512]{1,0:T(8,128)(2,1)} %param.27) | copy-start | bytes 3145732
  9.2 15.1 %collective-permute-start.16 = (bf16[128,2048]{1,0:T(8,128)(2,1)}, bf16[128,2048]{1,0:T(8,128)(2,1)S(1)}, u32[]{:S(2)}, u32[]{:S(2)}) collective-permute-start(bf16[128,2048]{1,0:T(8,128)(2,1)} %pack_weights.1), channel_id=1, source_target_pairs={{0,1},{1,0},{2,3},{3,2},{4,5},{5,4},{6,7},{7,6},{8,9},{9,8},{10,11... | collective-permute-start | bytes 1572872 | tf_op jit(solution)/shard_map/ppermute | solution.py:437
  25.2 238.5 %all-reduce.4.cloned.1.call-start = ((), (), s32[]{:S(2)}) async-start(), calls=%async_computation | async-start | bytes 8388608 | tf_op jit(solution)/shard_map/psum | solution.py:1033
  25.2 22.1 %collective-permute-start.20 = (bf16[2048]{0:T(1024)(128)(2,1)S(1)}, bf16[2048]{0:T(1024)(128)(2,1)S(1)}, u32[]{:S(2)}, u32[]{:S(2)}) collective-permute-start(bf16[2048]{0:T(1024)(128)(2,1)S(1)} %copy-done.34), channel_id=1, source_target_pairs={{0,1},{1,0},{2,3},{3,2},{4,5},{5,4},{6,7},{7,6},{8,9},{9,8},{10,11... | collective-permute-start | bytes 12296 | tf_op jit(solution)/shard_map/ppermute | solution.py:437
  27.4 24.1 %collective-permute-start.17 = (bf16[512,1024]{1,0:T(8,128)(2,1)}, bf16[512,1024]{1,0:T(8,128)(2,1)}, u32[]{:S(2)}, u32[]{:S(2)}) collective-permute-start(bf16[512,1024]{1,0:T(8,128)(2,1)} %tokens_ref.1), channel_id=1, source_target_pairs={{0,1},{1,0},{2,3},{3,2},{4,5},{5,4},{6,7},{7,6},{8,9},{9,8},{10,11... | collective-permute-start | bytes 3145736 | tf_op jit(solution)/shard_map/ppermute | solution.py:437
  29.7 3.1 copy-start.3
  32.9 2.9 copy-start.35
  32.9 3.5 copy-start.30
  32.9 4.1 copy-start.36
  32.9 5.6 %copy-start.37 = (bf16[1024]{0:T(1024)(128)(2,1)S(1)}, bf16[1024]{0:T(1024)(128)(2,1)}, u32[]{:S(2)}) copy-start(bf16[1024]{0:T(1024)(128)(2,1)} %param.37) | copy-start | bytes 6148
  32.9 6.2 %copy-start.38 = (bf16[1024]{0:T(1024)(128)(2,1)S(1)}, bf16[1024]{0:T(1024)(128)(2,1)}, u32[]{:S(2)}) copy-start(bf16[1024]{0:T(1024)(128)(2,1)} %param.38) | copy-start | bytes 6148
  32.9 6.7 %copy-start.39 = (bf16[1024]{0:T(1024)(128)(2,1)S(1)}, bf16[1024]{0:T(1024)(128)(2,1)}, u32[]{:S(2)}) copy-start(bf16[1024]{0:T(1024)(128)(2,1)} %param.39) | copy-start | bytes 6148
  51.5 26.3 %collective-permute-start.18 = (bf16[512,1024]{1,0:T(8,128)(2,1)}, bf16[512,1024]{1,0:T(8,128)(2,1)S(1)}, u32[]{:S(2)}, u32[]{:S(2)}) collective-permute-start(bf16[512,1024]{1,0:T(8,128)(2,1)} %w_own_ref.1), channel_id=1, source_target_pairs={{0,1},{1,0},{2,3},{3,2},{4,5},{5,4},{6,7},{7,6},{8,9},{9,8},{10,11... | collective-permute-start | bytes 3145736 | tf_op jit(solution)/shard_map/ppermute | solution.py:437
  56.6 9.5 %copy-start.23 = (bf16[1024,512]{1,0:T(8,128)(2,1)}, bf16[1024,512]{1,0:T(8,128)(2,1)S(1)}, u32[]{:S(2)}) copy-start(bf16[1024,512]{1,0:T(8,128)(2,1)S(1)} %get-tuple-element.1014.k_ref) | copy-start | bytes 3145732
  56.6 9.5 %copy-start.25 = (bf16[1024,512]{1,0:T(8,128)(2,1)}, bf16[1024,512]{1,0:T(8,128)(2,1)S(1)}, u32[]{:S(2)}) copy-start(bf16[1024,512]{1,0:T(8,128)(2,1)S(1)} %get-tuple-element.1015.v_ref) | copy-start | bytes 3145732
  66.1 12.9 %copy-start.24 = (bf16[1024,512]{1,0:T(8,128)(2,1)S(1)}, bf16[1024,512]{1,0:T(8,128)(2,1)}, u32[]{:S(2)}) copy-start(bf16[1024,512]{1,0:T(8,128)(2,1)} %copy-done.23) | copy-start | bytes 3145732
  66.1 21.1 %collective-permute-start.19 = (bf16[512,512]{1,0:T(8,128)(2,1)S(1)}, bf16[512,512]{1,0:T(8,128)(2,1)}, u32[]{:S(2)}, u32[]{:S(2)}) collective-permute-start(bf16[512,512]{1,0:T(8,128)(2,1)S(1)} %get-tuple-element.340), channel_id=1, source_target_pairs={{0,1},{1,0},{2,3},{3,2},{4,5},{5,4},{6,7},{7,6},{8,9},{9,8},{10,11... | collective-permute-start | bytes 1572872 | tf_op jit(solution)/shard_map/ppermute | solution.py:437
  87.2 41.7 %copy-start.27 = (bf16[512,512]{1,0:T(8,128)(2,1)}, bf16[512,512]{1,0:T(8,128)(2,1)S(1)}, u32[]{:S(2)}) copy-start(bf16[512,512]{1,0:T(8,128)(2,1)S(1)} %get-tuple-element.1019.own_ref) | copy-start | bytes 1572868
  87.2 6.3 %copy-start.12 = (bf16[1024,2048]{1,0:T(8,128)(2,1)S(1)}, bf16[1024,2048]{1,0:T(8,128)(2,1)}, u32[]{:S(2)}) copy-start(bf16[1024,2048]{1,0:T(8,128)(2,1)} %up_ref.5) | copy-start | bytes 12582916
  92.8 23.9 %copy-start.13 = (bf16[512,1024]{1,0:T(8,128)(2,1)}, bf16[512,1024]{1,0:T(8,128)(2,1)S(1)}, u32[]{:S(2)}) copy-start(bf16[512,1024]{1,0:T(8,128)(2,1)S(1)} %get-tuple-element.1009.h_ref.refs_0_) | copy-start | bytes 3145732
  92.8 37.8 %collective-permute-start.21 = (bf16[512,1024]{1,0:T(8,128)(2,1)S(1)}, bf16[512,1024]{1,0:T(8,128)(2,1)}, u32[]{:S(2)}, u32[]{:S(2)}) collective-permute-start(bf16[512,1024]{1,0:T(8,128)(2,1)S(1)} %get-tuple-element.1009.h_ref.refs_0_), channel_id=1, source_target_pairs={{0,1},{1,0},{2,3},{3,2},{4,5},{5,4},{6,7},{7,6},{8,9},{9,8},{10,11... | collective-permute-start | bytes 3145736 | tf_op jit(solution)/shard_map/ppermute | solution.py:437
  115.3 15.3 %collective-permute-start.22 = (bf16[256,1024]{1,0:T(8,128)(2,1)}, bf16[256,1024]{1,0:T(8,128)(2,1)}, u32[]{:S(2)}, u32[]{:S(2)}) collective-permute-start(bf16[256,1024]{1,0:T(8,128)(2,1)} %get-tuple-element.361.refs_0_), channel_id=1, source_target_pairs={{0,1},{1,0},{2,3},{3,2},{4,5},{5,4},{6,7},{7,6},{8,9},{9,8},{10,11... | collective-permute-start | bytes 1572872 | tf_op jit(solution)/shard_map/ppermute | solution.py:437
  126.6 3.3 copy-start.8
  126.7 3.3 copy-start.17
  126.7 3.3 copy-start.32
  126.7 3.3 copy-start.33
  126.7 13.4 %collective-permute-start.23 = (bf16[256,1024]{1,0:T(8,128)(2,1)}, bf16[256,1024]{1,0:T(8,128)(2,1)}, u32[]{:S(2)}, u32[]{:S(2)}) collective-permute-start(bf16[256,1024]{1,0:T(8,128)(2,1)} %get-tuple-element.362.refs_1_), channel_id=1, source_target_pairs={{0,1},{1,0},{2,3},{3,2},{4,5},{5,4},{6,7},{7,6},{8,9},{9,8},{10,11... | collective-permute-start | bytes 1572872 | tf_op jit(solution)/shard_map/ppermute | solution.py:437
  148.5 6.1 %copy-start = (bf16[1024,1024]{1,0:T(8,128)(2,1)S(1)}, bf16[1024,1024]{1,0:T(8,128)(2,1)}, u32[]{:S(2)}) copy-start(bf16[1024,1024]{1,0:T(8,128)(2,1)} %pad_maximum_fusion.5) | copy-start | bytes 6291460
  148.5 261.0 %all-reduce.6.cloned.1.call-start = ((), (), s32[]{:S(2)}) async-start(), calls=%async_computation.2 | async-start | bytes 8388608 | tf_op jit(solution)/shard_map/psum | solution.py:1101
  154.6 103.5 %copy-start.31 = (f32[3072]{0:T(1024)S(1)}, f32[3072]{0:T(1024)}, u32[]{:S(2)}) copy-start(f32[3072]{0:T(1024)} %reshape.217) | copy-start | bytes 36868
  155.3 19.5 %copy-start.44 = (bf16[512,1024]{1,0:T(8,128)(2,1)S(1)}, bf16[512,1024]{1,0:T(8,128)(2,1)}, u32[]{:S(2)}) copy-start(bf16[512,1024]{1,0:T(8,128)(2,1)} %get-tuple-element.1098) | copy-start | bytes 3145732 | tf_op jit(solution)/shard_map/while
  174.8 3.0 copy-start.42
  174.9 3.0 copy-start.46
  193.7 4.5 %collective-permute-start.1 = (bf16[512,2048]{1,0:T(8,128)(2,1)}, bf16[512,2048]{1,0:T(8,128)(2,1)}, u32[]{:S(2)}, u32[]{:S(2)}) collective-permute-start(bf16[512,2048]{1,0:T(8,128)(2,1)} %constant_dynamic-slice_fusion.8), channel_id=1, source_target_pairs={{0,2},{2,0},{4,6},{6,4},{8,10},{10,8},{12,14},{14,12},{16,18},{18,... | collective-permute-start | bytes 6291464 | tf_op jit(solution)/shard_map/while/body/ppermute | solution.py:928
  193.7 15.0 %collective-permute-start = (bf16[512,512]{1,0:T(8,128)(2,1)}, bf16[512,512]{1,0:T(8,128)(2,1)}, u32[]{:S(2)}, u32[]{:S(2)}) collective-permute-start(bf16[512,512]{1,0:T(8,128)(2,1)} %convolution_convert_fusion.11), channel_id=1, source_target_pairs={{0,1},{1,0},{2,3},{3,2},{4,5},{5,4},{6,7},{7,6},{8,9},{9,8},{10,11... | collective-permute-start | bytes 1572872 | tf_op jit(solution)/shard_map/while/body/ppermute | solution.py:437
  203.6 33.2 %collective-permute-start.2 = (bf16[256,2048]{1,0:T(8,128)(2,1)}, bf16[256,2048]{1,0:T(8,128)(2,1)}, u32[]{:S(2)}, u32[]{:S(2)}) collective-permute-start(bf16[256,2048]{1,0:T(8,128)(2,1)} %constant_dynamic-slice_fusion.9), channel_id=1, source_target_pairs={{0,4},{2,6},{4,0},{6,2},{8,12},{10,14},{12,8},{14,10},{16,20},{18,... | collective-permute-start | bytes 3145736 | tf_op jit(solution)/shard_map/while/body/ppermute | solution.py:928
  205.2 49.8 %collective-permute-start.3 = (bf16[512,1024]{1,0:T(8,128)(2,1)}, bf16[512,1024]{1,0:T(8,128)(2,1)}, u32[]{:S(2)}, u32[]{:S(2)}) collective-permute-start(bf16[512,1024]{1,0:T(8,128)(2,1)} %convolution_convert_fusion.13), channel_id=1, source_target_pairs={{0,1},{1,0},{2,3},{3,2},{4,5},{5,4},{6,7},{7,6},{8,9},{9,8},{10,11... | collective-permute-start | bytes 3145736 | tf_op jit(solution)/shard_map/while/body/ppermute | solution.py:437
  206.6 3.3 copy-start.21
  206.6 3.3 copy-start.22
  209.9 27.0 %copy-start.2 = (bf16[512,2048]{1,0:T(8,128)(2,1)S(1)}, bf16[512,2048]{1,0:T(8,128)(2,1)}, u32[]{:S(2)}) copy-start(bf16[512,2048]{1,0:T(8,128)(2,1)} %copy-done.1) | copy-start | bytes 6291460 | tf_op jit(solution)/shard_map/while
  236.8 2.8 copy-start.4
  252.8 2.1 copy-start.47
  257.2 10.1 %copy-start.16 = (bf16[512,1024]{1,0:T(8,128)(2,1)}, bf16[512,1024]{1,0:T(8,128)(2,1)S(1)}, u32[]{:S(2)}) copy-start(bf16[512,1024]{1,0:T(8,128)(2,1)S(1)} %get-tuple-element.393) | copy-start | bytes 3145732
  257.2 8.8 %copy-start.14 = (bf16[1024,512]{0,1:T(8,128)(2,1)S(1)}, bf16[1024,512]{0,1:T(8,128)(2,1)}, u32[]{:S(2)}) copy-start(bf16[1024,512]{0,1:T(8,128)(2,1)} %get-tuple-element.391) | copy-start | bytes 3145732
  263.6 3.7 copy-start.15
  269.9 23.4 %collective-permute-start.4 = (bf16[128,2048]{1,0:T(8,128)(2,1)S(1)}, bf16[128,2048]{1,0:T(8,128)(2,1)S(1)}, u32[]{:S(2)}, u32[]{:S(2)}) collective-permute-start(bf16[128,2048]{1,0:T(8,128)(2,1)S(1)} %constant_dynamic-slice_fusion.10), channel_id=1, source_target_pairs={{0,8},{2,10},{4,12},{6,14},{8,0},{10,2},{12,4},{14,6},{16,24},{18,... | collective-permute-start | bytes 1572872 | tf_op jit(solution)/shard_map/while/body/ppermute | solution.py:928
  271.1 8.5 %collective-permute-start.5 = (f32[6144]{0:T(1024)S(1)}, f32[6144]{0:T(1024)S(1)}, u32[]{:S(2)}, u32[]{:S(2)}) collective-permute-start(f32[6144]{0:T(1024)S(1)} %slice.115), channel_id=1, source_target_pairs={{0,1},{1,0},{2,3},{3,2},{4,5},{5,4},{6,7},{7,6},{8,9},{9,8},{10,11... | collective-permute-start | bytes 73736 | tf_op jit(solution)/shard_map/while/body/ppermute | solution.py:437
  279.6 14.4 %collective-permute-start.7 = (f32[9216]{0:T(1024)S(1)}, f32[9216]{0:T(1024)S(1)}, u32[]{:S(2)}, u32[]{:S(2)}) collective-permute-start(f32[9216]{0:T(1024)S(1)} %pad_maximum_fusion.19), channel_id=1, source_target_pairs={{0,2},{2,0},{4,6},{6,4},{8,10},{10,8},{12,14},{14,12},{16,18},{18,... | collective-permute-start | bytes 110600 | tf_op jit(solution)/shard_map/while/body/ppermute | solution.py:1123
  293.5 20.7 %collective-permute-start.6 = (bf16[64,2048]{1,0:T(8,128)(2,1)S(1)}, bf16[64,2048]{1,0:T(8,128)(2,1)S(1)}, u32[]{:S(2)}, u32[]{:S(2)}) collective-permute-start(bf16[64,2048]{1,0:T(8,128)(2,1)S(1)} %constant_dynamic-slice_fusion.11), channel_id=1, source_target_pairs={{0,16},{2,18},{4,20},{6,22},{8,24},{10,26},{12,28},{14,30},{16,0},... | collective-permute-start | bytes 786440 | tf_op jit(solution)/shard_map/while/body/ppermute | solution.py:928
  314.2 15.6 %collective-permute-start.8 = (bf16[64,2048]{1,0:T(8,128)(2,1)S(1)}, bf16[64,2048]{1,0:T(8,128)(2,1)S(1)}, u32[]{:S(2)}, u32[]{:S(2)}) collective-permute-start(bf16[64,2048]{1,0:T(8,128)(2,1)S(1)} %add_convert_fusion.17), channel_id=1, source_target_pairs={{0,16},{2,18},{4,20},{6,22},{8,24},{10,26},{12,28},{14,30},{16,0},... | collective-permute-start | bytes 786440 | tf_op jit(solution)/shard_map/while/body/ppermute | solution.py:928
  314.3 4.0 collective-permute-start.9
  329.9 12.2 %collective-permute-start.10 = (bf16[128,2048]{1,0:T(8,128)(2,1)S(1)}, bf16[128,2048]{1,0:T(8,128)(2,1)S(1)}, u32[]{:S(2)}, u32[]{:S(2)}) collective-permute-start(bf16[128,2048]{1,0:T(8,128)(2,1)S(1)} %pad_maximum_fusion.20), channel_id=1, source_target_pairs={{0,8},{2,10},{4,12},{6,14},{8,0},{10,2},{12,4},{14,6},{16,24},{18,... | collective-permute-start | bytes 1572872 | tf_op jit(solution)/shard_map/while/body/ppermute | solution.py:928
  330.0 12.1 %collective-permute-start.11 = (f32[9216]{0:T(1024)S(1)}, f32[9216]{0:T(1024)S(1)}, u32[]{:S(2)}, u32[]{:S(2)}) collective-permute-start(f32[9216]{0:T(1024)S(1)} %add.215), channel_id=1, source_target_pairs={{0,8},{2,10},{4,12},{6,14},{8,0},{10,2},{12,4},{14,6},{16,24},{18,... | collective-permute-start | bytes 110600 | tf_op jit(solution)/shard_map/while/body/ppermute | solution.py:1123
  342.4 25.6 %collective-permute-start.12 = (bf16[256,2048]{1,0:T(8,128)(2,1)S(1)}, bf16[256,2048]{1,0:T(8,128)(2,1)}, u32[]{:S(2)}, u32[]{:S(2)}) collective-permute-start(bf16[256,2048]{1,0:T(8,128)(2,1)S(1)} %pad_maximum_fusion.21), channel_id=1, source_target_pairs={{0,4},{2,6},{4,0},{6,2},{8,12},{10,14},{12,8},{14,10},{16,20},{18,... | collective-permute-start | bytes 3145736 | tf_op jit(solution)/shard_map/while/body/ppermute | solution.py:928
  347.6 5.2 %collective-permute-start.13 = (f32[9216]{0:T(1024)S(1)}, f32[9216]{0:T(1024)S(1)}, u32[]{:S(2)}, u32[]{:S(2)}) collective-permute-start(f32[9216]{0:T(1024)S(1)} %add.216), channel_id=1, source_target_pairs={{0,16},{2,18},{4,20},{6,22},{8,24},{10,26},{12,28},{14,30},{16,0},... | collective-permute-start | bytes 110600 | tf_op jit(solution)/shard_map/while/body/ppermute | solution.py:1123
  371.3 29.2 %collective-permute-start.14 = (bf16[512,2048]{1,0:T(8,128)(2,1)}, bf16[512,2048]{1,0:T(8,128)(2,1)}, u32[]{:S(2)}, u32[]{:S(2)}) collective-permute-start(bf16[512,2048]{1,0:T(8,128)(2,1)} %pad_maximum_fusion.22), channel_id=1, source_target_pairs={{0,2},{2,0},{4,6},{6,4},{8,10},{10,8},{12,14},{14,12},{16,18},{18,... | collective-permute-start | bytes 6291464 | tf_op jit(solution)/shard_map/while/body/ppermute | solution.py:928
  371.3 25.8 %collective-permute-start.15 = (bf16[512,1024]{1,0:T(8,128)(2,1)}, bf16[512,1024]{1,0:T(8,128)(2,1)S(1)}, u32[]{:S(2)}, u32[]{:S(2)}) collective-permute-start(bf16[512,1024]{1,0:T(8,128)(2,1)} %get-tuple-element.980), channel_id=1, source_target_pairs={{0,1},{1,0},{2,3},{3,2},{4,5},{5,4},{6,7},{7,6},{8,9},{9,8},{10,11... | collective-permute-start | bytes 3145736 | tf_op jit(solution)/shard_map/while/body/ppermute | solution.py:437
  403.2 4.3 %copy-start.11 = (bf16[256,2048]{1,0:T(8,128)(2,1)S(1)}, bf16[256,2048]{1,0:T(8,128)(2,1)}, u32[]{:S(2)}) copy-start(bf16[256,2048]{1,0:T(8,128)(2,1)} %get-tuple-element.1209) | copy-start | bytes 3145732 | tf_op jit(solution)/shard_map/while
  409.5 2.9 copy-start.20
  (11 other events, 15.9 us)
Sparse Core Ops, SparseCore 0:
  25.3 76.3 all-gather.2
  148.6 114.9 all-reduce.3
  268.8 140.6 all-reduce.5
